TPU v7x, 32 devices: a whole 2x2x4 slice. The times are simulated.
32 devices in a mesh: elem: 8 (over y, x, core), band: 4 (over z).
Axes of the slice: x: 2, y: 2, z: 4, core: 2. Of those that a mesh axis runs over, the one named last changes fastest.
Arguments:
- state: bfloat16 [16384, 256], P(('elem', 'band')), may hold values from -6 to 6
- dest_map: int32 [16384, 1], P(('elem', 'band')), may hold values from 0 to 7; in each aligned block of 512 rows (0 to 511, 512 to 1023, ...) at most 128 rows name the same one
- day_mask: int32 [16384, 1], P(('elem', 'band')), may hold values 0 or 1
- cloud: bfloat16 [32768, 512], P(('elem', 'band')), may hold values from -6 to 6
- conv_in: bfloat16 [768, 256], replicated, may hold values from -0.21875 to 0.21875
- conv_mid: bfloat16 [256, 256], replicated, may hold values from -0.375 to 0.375
- conv_out: bfloat16 [256, 768], replicated, may hold values from -0.375 to 0.375
- rad_in: bfloat16 [768, 256], replicated, may hold values from -0.21875 to 0.21875
- rad_mid: bfloat16 [256, 256], replicated, may hold values from -0.375 to 0.375
- rad_out: bfloat16 [256, 128], replicated, may hold values from -0.375 to 0.375
Outputs:
- tendency: bfloat16 [16384, 256], P(('elem', 'band'))
- new_cloud: bfloat16 [32768, 512], P(('elem', 'band'))
Inputs may be any that keep to these rules, and one draw needn't show every extreme that they name: `dest_map`: among the columns of one device (aligned blocks of 512 rows) no value is named by more than 128 rows, a bound that some block reaches.
All inputs are finite; a program needn't handle non-finite values. No bound on the sum of `day_mask` on one device may be relied on, other than what follows from the above.
Results may differ from a plain program's by a relative error of at most 0.0058.
Values may be sent and summed in bfloat16 or wider, within the bound.
No kernel may reach another device: no remote copies, remote signals or barrier semaphores. Data moves between devices by JAX's collectives and lax.ppermute only.
A program may use at most 64 MiB of HBM per device.

v0:
```python
import jax
import jax.numpy as jnp
from jax import lax
from jax.sharding import PartitionSpec as P


def passed_along(block, axis, distance):
    devices = range(lax.axis_size(axis))
    route = [((i - distance) % len(devices), i) for i in devices]
    return lax.ppermute(block, axis, route)


def column_physics(inputs, daylight, cloud, conv_in, conv_mid, conv_out, rad_in, rad_mid, rad_out):
    levels = rad_out.shape[1]
    joined = jnp.concatenate([inputs, cloud], axis=1)
    conv_one = jax.nn.silu(jnp.dot(joined, conv_in, preferred_element_type=jnp.float32)).astype(
        jnp.bfloat16
    )
    conv_two = jax.nn.silu(jnp.dot(conv_one, conv_mid, preferred_element_type=jnp.float32)).astype(
        jnp.bfloat16
    )
    conv_result = jnp.dot(conv_two, conv_out, preferred_element_type=jnp.float32)
    rad_one = jax.nn.silu(jnp.dot(joined, rad_in, preferred_element_type=jnp.float32)).astype(
        jnp.bfloat16
    )
    rad_two = jax.nn.silu(jnp.dot(rad_one, rad_mid, preferred_element_type=jnp.float32)).astype(
        jnp.bfloat16
    )
    rad_result = jnp.dot(rad_two, rad_out, preferred_element_type=jnp.float32)
    heating = daylight.astype(jnp.float32)[:, None] * rad_result
    padded = jnp.concatenate([heating, jnp.zeros_like(heating)], axis=1)
    tendency_rows = (conv_result[:, : 2 * levels] + padded).astype(jnp.bfloat16)
    updated = (cloud.astype(jnp.float32) + conv_result[:, 2 * levels :]).astype(jnp.bfloat16)
    return (tendency_rows, updated)


def slot_places(target, groups, capacity):
    onehot = (target[:, None] == jnp.arange(groups, dtype=jnp.int32)[None, :]).astype(jnp.int32)
    order_in = jnp.sum((jnp.cumsum(onehot, axis=0) - onehot) * onehot, axis=1)
    return target * capacity + order_in


def per_device(
    state, dest_map, day_mask, cloud, conv_in, conv_mid, conv_out, rad_in, rad_mid, rad_out
):
    groups = lax.axis_size("elem")
    band_count = lax.axis_size("band")
    capacity = cloud.shape[0] // groups
    features = state.shape[1]
    weights = (conv_in, conv_mid, conv_out, rad_in, rad_mid, rad_out)
    half_rows = groups // 2 * capacity
    partner = band_count // 2
    target = dest_map[:, 0]
    sun_flag = day_mask[:, 0]
    position = slot_places(target, groups, capacity)
    outgoing = jnp.zeros((groups * capacity, features), jnp.bfloat16).at[position].set(state)
    sunlit = (
        jnp.zeros((groups * capacity,), jnp.bfloat16)
        .at[position]
        .set(sun_flag.astype(jnp.bfloat16))
    )
    arrived, arrived_sun = (
        lax.all_to_all(
            outgoing.reshape(groups, capacity, features),
            "elem",
            split_axis=0,
            concat_axis=0,
            tiled=True,
        ),
        lax.all_to_all(
            sunlit.reshape(groups, capacity), "elem", split_axis=0, concat_axis=0, tiled=True
        ),
    )
    arrived = arrived.reshape(groups * capacity, features)
    arrived_sun = arrived_sun.reshape(groups * capacity)
    borrowed = passed_along(cloud[half_rows:], "band", partner)
    serving_cloud = jnp.concatenate([cloud[:half_rows], borrowed], axis=0)
    tendency_rows, updated = column_physics(arrived, arrived_sun, serving_cloud, *weights)
    handed_back = passed_along(updated[half_rows:], "band", partner)
    new_cloud = jnp.concatenate([updated[:half_rows], handed_back], axis=0)
    returned = lax.all_to_all(
        tendency_rows.reshape(groups, capacity, features),
        "elem",
        split_axis=0,
        concat_axis=0,
        tiled=True,
    )
    tendency = returned.reshape(groups * capacity, features)[position]
    return (tendency, new_cloud)


def solution(mesh):
    placed = (
        P(("elem", "band"), None),
        P(("elem", "band"), None),
        P(("elem", "band"), None),
        P(("elem", "band"), None),
        P(),
        P(),
        P(),
        P(),
        P(),
        P(),
    )
    return jax.shard_map(
        per_device,
        mesh=mesh,
        in_specs=placed,
        out_specs=(P(("elem", "band"), None), P(("elem", "band"), None)),
        check_vma=False,
    )
```

profile of v0, /device:TPU:2, one launch (start us, length us, event | category | flops | bytes accessed | tf_op | source)
XLA Modules:
  0.0 66.9 jit_solution(15080386732252344029)
XLA Ops:
  0.6 0.0 copy-start
  0.6 0.0 copy-start.6
  0.7 0.0 copy-start.7
  0.7 0.0 copy-start.9
  0.7 0.0 copy-start.8
  0.7 1.3 %fusion.22 = (bf16[512,512]{1,0:T(8,128)(2,1)S(1)}, bf16[512,512]{1,0:T(8,128)(2,1)S(1)}) fusion(bf16[1024,512]{1,0:T(8,128)(2,1)} %param.13), kind=kLoop, calls=%fused_computation.39 | loop fusion | bytes 2097152 | tf_op jit(solution)/shard_map/slice | solution.py:77
  2.0 0.0 copy-start.2
  2.0 2.7 %collective-permute-start = (bf16[512,512]{1,0:T(8,128)(2,1)S(1)}, bf16[512,512]{1,0:T(8,128)(2,1)S(1)}, u32[]{:S(2)}, u32[]{:S(2)}) collective-permute-start(bf16[512,512]{1,0:T(8,128)(2,1)S(1)} %get-tuple-element.5), channel_id=1, source_target_pairs={{2,0},{3,1},{0,2},{1,3},{6,4},{7,5},{4,6},{5,7},{10,8},{11,9},{8,1... | collective-permute-start | bytes 1572872 | tf_op jit(solution)/shard_map/ppermute | solution.py:10
  4.7 0.0 copy-done.6
  4.7 1.1 %reduce-window.6 = s32[8,4,128]{2,0,1:T(8,128)S(1)} reduce-window(s32[8,4,128]{2,0,1:T(8,128)S(1)} %fusion.12, s32[]{:T(128)} %constant.18.clone.1), window={size=1x1x128 pad=0_0x0_0x127_0}, to_apply=%region_0.0 | reduce-window | flops 520192 | bytes 32772 | tf_op jit(solution)/shard_map/reduce-window
  5.8 0.2 slice_reduce_fusion
  6.1 0.1 fusion.11
  6.2 0.0 copy-done.7
  6.2 3.8 %scatter_custom_fusion.1 = bf16[1024]{0:T(1024)(128)(2,1)S(1)} fusion(s32[512]{0:T(512)S(1)} %bitcast.31, bf16[512]{0:T(512)(128)(2,1)S(1)} %convert_reduce_fusion, bf16[]{:T(256)} %constant.7.clone.1), kind=kCustom, calls=%fused_computation.32 | custom fusion | bytes 2050 | tf_op jit(solution)/shard_map/scatter | solution.py:60
  10.0 0.6 copy.12
  10.6 4.3 %all-to-all-start.1 = ((bf16[8,1,128]{2,1,0:T(2,128)(2,1)}), bf16[8,1,128]{2,1,0:T(2,128)(2,1)S(1)}, u32[]{:S(2)}, u32[]{:S(2)}) async-start(bf16[8,1,128]{2,1,0:T(2,128)(2,1)} %copy.12), calls=%async_computation.1 | async-start | bytes 8192 | tf_op jit(solution)/shard_map/all_to_all | solution.py:70
  14.9 3.5 %scatter_custom_fusion = bf16[1024,256]{1,0:T(8,128)(2,1)} fusion(s32[512]{0:T(512)S(1)} %bitcast.32, bf16[512,256]{1,0:T(8,128)(2,1)} %param.10, bf16[]{:T(256)} %constant.7.clone.1), kind=kCustom, calls=%fused_computation.20 | custom fusion | bytes 524800 | tf_op jit(solution)/shard_map/scatter | solution.py:56
  18.4 0.0 all-to-all-done.1
  18.4 5.1 %all-to-all-start = ((bf16[8,128,256]{2,1,0:T(8,128)(2,1)}), bf16[8,128,256]{2,1,0:T(8,128)(2,1)}, u32[]{:S(2)}, u32[]{:S(2)}) async-start(bf16[8,128,256]{2,1,0:T(8,128)(2,1)} %bitcast.6), calls=%async_computation | async-start | bytes 1048576 | tf_op jit(solution)/shard_map/all_to_all | solution.py:63
  23.5 8.4 %all-to-all-done = bf16[8,128,256]{2,1,0:T(8,128)(2,1)} async-done(((bf16[8,128,256]{2,1,0:T(8,128)(2,1)}), bf16[8,128,256]{2,1,0:T(8,128)(2,1)}, u32[]{:S(2)}, u32[]{:S(2)}) %all-to-all-start) | async-done | bytes 524320 | tf_op jit(solution)/shard_map/all_to_all | solution.py:63
  31.9 0.0 collective-permute-done
  31.9 0.0 copy-start.4
  31.9 0.0 copy-done.2
  31.9 0.8 %copy-done.4 = bf16[512,512]{1,0:T(8,128)(2,1)} copy-done((bf16[512,512]{1,0:T(8,128)(2,1)}, bf16[512,512]{1,0:T(8,128)(2,1)S(1)}, u32[]{:S(2)}) %copy-start.4) | copy-done | bytes 524312
  32.7 0.0 copy-done.9
  32.7 0.0 copy-done.8
  32.7 2.8 %multiply_convert_fusion.2 = bf16[1024,256]{1,0:T(8,128)(2,1)} fusion(bf16[256,256]{1,0:T(8,128)(2,1)S(1)} %copy-done.9, bf16[768,256]{1,0:T(8,128)(2,1)S(1)} %copy-done.8, bf16[512,512]{1,0:T(8,128)(2,1)S(1)} %collective-permute-done, bf16[512,512]{1,0:T(8,128)(2,1)S(1)} %get-tuple-element.4, bf16[1024,256]{1,0:T(8,128)(2,1)} %bitcast.7), kind=kOutput, calls=%fused_computation.12 | convolution fusion | flops 544210944 | bytes 2621440 | tf_op jit(solution)/shard_map/dot_general | solution.py:19
  35.5 0.0 copy-done
  35.5 0.0 copy-start.3
  35.5 0.0 copy-start.5
  35.5 1.7 %fusion.23 = f32[1024,768]{1,0:T(8,128)S(1)} fusion(bf16[1024,256]{1,0:T(8,128)(2,1)} %multiply_convert_fusion.2, bf16[256,768]{1,0:T(8,128)(2,1)S(1)} %copy-done), kind=kOutput, calls=%fused_computation.40 | convolution fusion | flops 402653184 | bytes 4063232 | tf_op jit(solution)/shard_map/dot_general | solution.py:22
  37.2 0.0 copy-done.3
  37.2 0.0 copy-done.5
  37.2 0.2 fusion
  37.5 1.0 %fusion.21 = (bf16[512,512]{1,0:T(8,128)(2,1)}, bf16[512,512]{1,0:T(8,128)(2,1)}) fusion(bf16[1024,512]{1,0:T(8,128)(2,1)S(1)} %fusion), kind=kLoop, calls=%fused_computation.38 | loop fusion | bytes 2097152 | tf_op jit(solution)/shard_map/slice | solution.py:80
  38.5 0.3 collective-permute-start.1
  38.9 3.3 %multiply_convert_fusion = bf16[1024,256]{1,0:T(8,128)(2,1)} fusion(bf16[256,256]{1,0:T(8,128)(2,1)} %param.18, bf16[768,256]{1,0:T(8,128)(2,1)} %param.17, bf16[512,512]{1,0:T(8,128)(2,1)} %copy-done.4, bf16[512,512]{1,0:T(8,128)(2,1)} %copy-done.2, bf16[1024,256]{1,0:T(8,128)(2,1)} %bitcast.7), kind=kOutput, calls=%fused_computation.10 | convolution fusion | flops 544210944 | bytes 2621440 | tf_op jit(solution)/shard_map/dot_general | solution.py:26
  42.1 1.3 %convolution_multiply_fusion = f32[1024,128]{1,0:T(8,128)S(1)} fusion(bf16[1024,256]{1,0:T(8,128)(2,1)} %multiply_convert_fusion, bf16[256,128]{1,0:T(8,128)(2,1)} %param.19, f32[1024]{0:T(1024)S(1)} %bitcast.30), kind=kOutput, calls=%fused_computation.6 | convolution fusion | flops 67239936 | bytes 1118208 | tf_op jit(solution)/shard_map/dot_general | solution.py:29
  43.5 0.9 %fusion.1 = bf16[1024,256]{1,0:T(8,128)(2,1)} fusion(f32[1024,768]{1,0:T(8,128)S(1)} %fusion.23, f32[1024,128]{1,0:T(8,128)S(1)} %convolution_multiply_fusion), kind=kLoop, calls=%fused_computation.8 | loop fusion | flops 524288 | bytes 2097152 | tf_op jit(solution)/shard_map/convert_element_type | solution.py:32
  44.4 0.0 copy-start.1
  44.4 5.0 %all-to-all-start.2 = ((bf16[8,128,256]{2,1,0:T(8,128)(2,1)}), bf16[8,128,256]{2,1,0:T(8,128)(2,1)S(1)}, u32[]{:S(2)}, u32[]{:S(2)}) async-start(bf16[8,128,256]{2,1,0:T(8,128)(2,1)} %bitcast.27), calls=%async_computation.2 | async-start | bytes 1048576 | tf_op jit(solution)/shard_map/all_to_all | solution.py:81
  49.4 8.3 %all-to-all-done.2 = bf16[8,128,256]{2,1,0:T(8,128)(2,1)S(1)} async-done(((bf16[8,128,256]{2,1,0:T(8,128)(2,1)}), bf16[8,128,256]{2,1,0:T(8,128)(2,1)S(1)}, u32[]{:S(2)}, u32[]{:S(2)}) %all-to-all-start.2) | async-done | bytes 524320 | tf_op jit(solution)/shard_map/all_to_all | solution.py:81
  57.7 2.6 %gather_fusion = bf16[512,256]{1,0:T(8,128)(2,1)} fusion(bf16[1024,256]{1,0:T(8,128)(2,1)S(1)} %bitcast.26, s32[1024]{0:T(1024)S(1)} %pad_clamp_fusion), kind=kCustom, calls=%fused_computation | custom fusion | bytes 526336 | tf_op jit(solution)/shard_map/gather | solution.py:88
  60.3 4.6 %collective-permute-done.1 = bf16[512,512]{1,0:T(8,128)(2,1)} collective-permute-done((bf16[512,512]{1,0:T(8,128)(2,1)}, bf16[512,512]{1,0:T(8,128)(2,1)}, u32[]{:S(2)}, u32[]{:S(2)}) %collective-permute-start.1) | collective-permute-done | bytes 524320 | tf_op jit(solution)/shard_map/ppermute | solution.py:10
  64.9 0.0 copy-done.1
  64.9 2.1 %pad_maximum_fusion = bf16[1024,512]{1,0:T(8,128)(2,1)} fusion(bf16[512,512]{1,0:T(8,128)(2,1)} %collective-permute-done.1, bf16[512,512]{1,0:T(8,128)(2,1)S(1)} %copy-done.1), kind=kLoop, calls=%fused_computation.9 | loop fusion | flops 2097152 | bytes 2097152 | tf_op jit(solution)/shard_map/concatenate | solution.py:80
  (7 shorter events, 0.1 us)
Async XLA Ops:
  0.6 34.9 %copy-start = (bf16[256,768]{1,0:T(8,128)(2,1)S(1)}, bf16[256,768]{1,0:T(8,128)(2,1)}, u32[]{:S(2)}) copy-start(bf16[256,768]{1,0:T(8,128)(2,1)} %param.16) | copy-start | bytes 1179652
  0.6 4.1 %copy-start.6 = (s32[512,1]{0,1:T(1,128)S(1)}, s32[512,1]{0,1:T(1,128)}, u32[]{:S(2)}) copy-start(s32[512,1]{0,1:T(1,128)} %param.11) | copy-start | bytes 6148
  0.7 5.6 %copy-start.7 = (s32[512,1]{0,1:T(1,128)S(1)}, s32[512,1]{0,1:T(1,128)}, u32[]{:S(2)}) copy-start(s32[512,1]{0,1:T(1,128)} %param.12) | copy-start | bytes 6148
  0.7 32.0 %copy-start.9 = (bf16[256,256]{1,0:T(8,128)(2,1)S(1)}, bf16[256,256]{1,0:T(8,128)(2,1)}, u32[]{:S(2)}) copy-start(bf16[256,256]{1,0:T(8,128)(2,1)} %param.15) | copy-start | bytes 393220
  0.7 32.0 %copy-start.8 = (bf16[768,256]{1,0:T(8,128)(2,1)S(1)}, bf16[768,256]{1,0:T(8,128)(2,1)}, u32[]{:S(2)}) copy-start(bf16[768,256]{1,0:T(8,128)(2,1)} %param.14) | copy-start | bytes 1179652
  2.0 29.9 %copy-start.2 = (bf16[512,512]{1,0:T(8,128)(2,1)}, bf16[512,512]{1,0:T(8,128)(2,1)S(1)}, u32[]{:S(2)}) copy-start(bf16[512,512]{1,0:T(8,128)(2,1)S(1)} %get-tuple-element.4) | copy-start | bytes 1572868
  2.0 29.8 %collective-permute-start = (bf16[512,512]{1,0:T(8,128)(2,1)S(1)}, bf16[512,512]{1,0:T(8,128)(2,1)S(1)}, u32[]{:S(2)}, u32[]{:S(2)}) collective-permute-start(bf16[512,512]{1,0:T(8,128)(2,1)S(1)} %get-tuple-element.5), channel_id=1, source_target_pairs={{2,0},{3,1},{0,2},{1,3},{6,4},{7,5},{4,6},{5,7},{10,8},{11,9},{8,1... | collective-permute-start | bytes 1572872 | tf_op jit(solution)/shard_map/ppermute | solution.py:10
  10.6 7.8 %all-to-all-start.1 = ((bf16[8,1,128]{2,1,0:T(2,128)(2,1)}), bf16[8,1,128]{2,1,0:T(2,128)(2,1)S(1)}, u32[]{:S(2)}, u32[]{:S(2)}) async-start(bf16[8,1,128]{2,1,0:T(2,128)(2,1)} %copy.12), calls=%async_computation.1 | async-start | bytes 8192 | tf_op jit(solution)/shard_map/all_to_all | solution.py:70
  18.4 13.5 %all-to-all-start = ((bf16[8,128,256]{2,1,0:T(8,128)(2,1)}), bf16[8,128,256]{2,1,0:T(8,128)(2,1)}, u32[]{:S(2)}, u32[]{:S(2)}) async-start(bf16[8,128,256]{2,1,0:T(8,128)(2,1)} %bitcast.6), calls=%async_computation | async-start | bytes 1048576 | tf_op jit(solution)/shard_map/all_to_all | solution.py:63
  31.9 0.8 %copy-start.4 = (bf16[512,512]{1,0:T(8,128)(2,1)}, bf16[512,512]{1,0:T(8,128)(2,1)S(1)}, u32[]{:S(2)}) copy-start(bf16[512,512]{1,0:T(8,128)(2,1)S(1)} %collective-permute-done) | copy-start | bytes 1572868
  35.5 1.7 %copy-start.3 = (bf16[512,512]{1,0:T(8,128)(2,1)S(1)}, bf16[512,512]{1,0:T(8,128)(2,1)}, u32[]{:S(2)}) copy-start(bf16[512,512]{1,0:T(8,128)(2,1)} %copy-done.2) | copy-start | bytes 1572868
  35.5 1.7 %copy-start.5 = (bf16[512,512]{1,0:T(8,128)(2,1)S(1)}, bf16[512,512]{1,0:T(8,128)(2,1)}, u32[]{:S(2)}) copy-start(bf16[512,512]{1,0:T(8,128)(2,1)} %copy-done.4) | copy-start | bytes 1572868
  38.5 26.3 %collective-permute-start.1 = (bf16[512,512]{1,0:T(8,128)(2,1)}, bf16[512,512]{1,0:T(8,128)(2,1)}, u32[]{:S(2)}, u32[]{:S(2)}) collective-permute-start(bf16[512,512]{1,0:T(8,128)(2,1)} %get-tuple-element.3), channel_id=1, source_target_pairs={{2,0},{3,1},{0,2},{1,3},{6,4},{7,5},{4,6},{5,7},{10,8},{11,9},{8,1... | collective-permute-start | bytes 1572872 | tf_op jit(solution)/shard_map/ppermute | solution.py:10
  44.4 20.5 %copy-start.1 = (bf16[512,512]{1,0:T(8,128)(2,1)S(1)}, bf16[512,512]{1,0:T(8,128)(2,1)}, u32[]{:S(2)}) copy-start(bf16[512,512]{1,0:T(8,128)(2,1)} %get-tuple-element.2) | copy-start | bytes 1572868
  44.4 13.3 %all-to-all-start.2 = ((bf16[8,128,256]{2,1,0:T(8,128)(2,1)}), bf16[8,128,256]{2,1,0:T(8,128)(2,1)S(1)}, u32[]{:S(2)}, u32[]{:S(2)}) async-start(bf16[8,128,256]{2,1,0:T(8,128)(2,1)} %bitcast.27), calls=%async_computation.2 | async-start | bytes 1048576 | tf_op jit(solution)/shard_map/all_to_all | solution.py:81
where the time goes:
time: 67.5 us; the launch traced here: 66.9 us
  waiting for transfers between devices  21.3 us (32%)
  starting transfers between devices  17.3 us (26%)
  local copies, waits for them, and re-layouts  13.9 us (21%)
  matrix products  9.14 us (14%)
  other arithmetic  4.51 us (7%)
  between operations  0.77 us (1%)
    all_to_all x1, waiting for transfers between devices, per_device(): lax.all_to_all(outgoing.reshape(groups, capacity, features), 'elem', spli...  8.4 us
    all_to_all x1, waiting for transfers between devices, per_device(): lax.all_to_all(tendency_rows.reshape(groups, capacity, features), 'elem',...  8.29 us
    all_to_all x1, starting transfers between devices, per_device(): lax.all_to_all(outgoing.reshape(groups, capacity, features), 'elem', spli...  5.07 us
    all_to_all x1, starting transfers between devices, per_device(): lax.all_to_all(tendency_rows.reshape(groups, capacity, features), 'elem',...  5.01 us
    ppermute x2, waiting for transfers between devices, passed_along(): return lax.ppermute(block, axis, route)  4.61 us
    all_to_all x1, starting transfers between devices, per_device(): lax.all_to_all(sunlit.reshape(groups, capacity), 'elem', split_axis=0, co...  4.25 us
    scatter x1, local copies, waits for them, and re-layouts, per_device(): sunlit = jnp.zeros((groups * capacity,), jnp.bfloat16).at[position].set(s...  3.77 us
    scatter x1, local copies, waits for them, and re-layouts, per_device(): jnp.zeros((groups * capacity, features), jnp.bfloat16).at[position]  3.53 us
  transfers between devices with their start and end apart: 5, of which 3 were waited for; matrix products, arithmetic and copies ran while one was open for 26% of the time, Pallas kernels for 0%

commit v1 on v0

v1 whole, which is shorter than its diff:
```python
import functools

import jax
import jax.numpy as jnp
from jax import lax
from jax.experimental import pallas as pl
from jax.experimental.pallas import tpu as pltpu
from jax.sharding import PartitionSpec as P

VMEM_BYTES = 20 * 1024 * 1024
FLAG_ROWS = 16


def moved(block, target):
    groups, bands = lax.axis_size("elem"), lax.axis_size("band")
    route = []
    for e in range(groups):
        for b in range(bands):
            to_elem, to_band = target(e, b)
            route.append((e * bands + b, to_elem * bands + to_band))
    return lax.ppermute(block, ("elem", "band"), route)


def orders(dest, groups):
    count = dest.shape[1]
    lanes = 128
    hot = (lax.broadcasted_iota(jnp.int32, (groups, count), 0) == dest).astype(jnp.float32)
    before = (
        lax.broadcasted_iota(jnp.int32, (lanes, lanes), 0)
        < lax.broadcasted_iota(jnp.int32, (lanes, lanes), 1)
    ).astype(jnp.bfloat16)
    parts, seen = [], jnp.zeros((groups, 1), jnp.float32)
    for start in range(0, count, lanes):
        piece = hot[:, start : start + lanes]
        inside = jnp.dot(piece.astype(jnp.bfloat16), before, preferred_element_type=jnp.float32)
        parts.append(jnp.sum(piece * (inside + seen), axis=0, keepdims=True))
        seen = seen + jnp.sum(piece, axis=1, keepdims=True)
    return jnp.concatenate(parts, axis=1).astype(jnp.int32)


def place_kernel(groups, cap, ids_ref, maps_ref, far_maps_ref, state_ref, far_state_ref, order_ref, *out_refs):
    core, unit = ids_ref[0], ids_ref[1]
    units = groups // 2
    columns, features = state_ref.shape
    flags = []
    for far, (maps, rows) in enumerate(((maps_ref, state_ref), (far_maps_ref, far_state_ref))):
        source_core = core if far == 0 else 1 - core
        dest, day = maps[0:1, :], maps[1:2, :]
        order = orders(dest, groups)
        if far == 0:
            order_ref[...] = jnp.concatenate([dest, order] + [jnp.zeros_like(dest)] * 6, axis=0)
        step = lax.bitwise_xor(lax.shift_right_logical(dest, 1), jnp.full_like(dest, unit))
        row = jnp.where(lax.bitwise_and(dest, 1) == core, step * cap + order, -1)
        hot = (lax.broadcasted_iota(jnp.int32, (units * cap, columns), 0) == row).astype(jnp.bfloat16)
        placed = jnp.dot(hot, rows[...], preferred_element_type=jnp.float32).astype(jnp.bfloat16)
        sun = jnp.broadcast_to(day.astype(jnp.float32), (FLAG_ROWS, columns)).astype(jnp.bfloat16)
        flags.append(
            lax.dot_general(sun, hot, (((1,), (1,)), ((), ())), preferred_element_type=jnp.float32)
        )
        for du in range(units):
            out_refs[du][pl.ds(pl.multiple_of(source_core * cap, cap), cap), :] = placed[du * cap : (du + 1) * cap, :]
    first = jnp.where(core == 0, flags[0], flags[1]).astype(jnp.bfloat16)
    second = jnp.where(core == 0, flags[1], flags[0]).astype(jnp.bfloat16)
    middle = features // 2
    for du in range(units):
        if cap < middle:
            out_refs[du][2 * cap :, :] = jnp.zeros((FLAG_ROWS, features), jnp.bfloat16)
        out_refs[du][2 * cap :, 0:cap] = first[:, du * cap : (du + 1) * cap]
        out_refs[du][2 * cap :, middle : middle + cap] = second[:, du * cap : (du + 1) * cap]


def silu(v):
    return (0.5 * v) * (1.0 + jnp.tanh(0.5 * v))


def dot(a, b):
    return jnp.dot(a, b, preferred_element_type=jnp.float32)


def as_column(row, cap):
    same = lax.broadcasted_iota(jnp.int32, (cap, cap), 0) == lax.broadcasted_iota(jnp.int32, (cap, cap), 1)
    return jnp.sum(jnp.where(same, jnp.broadcast_to(row, (cap, cap)), 0.0), axis=1, keepdims=True)


def physics_kernel(cap, has_base, ids_ref, near_ref, cross_ref, lent_ref, cloud_ref, conv_in, conv_mid, conv_out, rad_in, rad_mid, rad_out, *rest):
    straight_ref, crossed_ref, new_ref = rest[1:] if has_base else rest
    step = pl.program_id(0)
    upper = ids_ref[2]
    features = near_ref.shape[1]
    levels = rad_out.shape[1]

    def serve(packet, out_ref):
        state = packet[0 : 2 * cap, :]
        cloud = cloud_ref[...]
        conv = silu(dot(state, conv_in[:features, :]) + dot(cloud, conv_in[features:, :])).astype(jnp.bfloat16)
        rad = silu(dot(state, rad_in[:features, :]) + dot(cloud, rad_in[features:, :])).astype(jnp.bfloat16)
        conv = silu(dot(conv, conv_mid[...])).astype(jnp.bfloat16)
        rad = silu(dot(rad, rad_mid[...])).astype(jnp.bfloat16)
        conv = dot(conv, conv_out[...])
        rad = dot(rad, rad_out[...])
        flags = packet[2 * cap : 2 * cap + FLAG_ROWS, :].astype(jnp.float32)[0:1, :]
        middle = features // 2
        day = jnp.concatenate(
            [as_column(flags[:, 0:cap], cap), as_column(flags[:, middle : middle + cap], cap)], axis=0
        )
        out_ref[:, :levels] = (conv[:, :levels] + day * rad).astype(jnp.bfloat16)
        out_ref[:, levels:] = conv[:, levels : 2 * levels].astype(jnp.bfloat16)
        new_ref[...] = (cloud.astype(jnp.float32) + conv[:, 2 * levels :]).astype(jnp.bfloat16)

    @pl.when(jnp.logical_and(step == 0, upper == 0))
    def _():
        serve(near_ref, straight_ref)

    @pl.when(jnp.logical_and(step == 0, upper == 1))
    def _():
        serve(cross_ref, crossed_ref)

    @pl.when(jnp.logical_and(step == 1, upper == 0))
    def _():
        serve(lent_ref, crossed_ref)

    @pl.when(jnp.logical_and(step == 1, upper == 1))
    def _():
        serve(lent_ref, straight_ref)


def collect_kernel(groups, cap, ids_ref, order_ref, *refs):
    units = groups // 2
    core, unit = ids_ref[0], ids_ref[1]
    own, far, out_ref = refs[:units], refs[units : 2 * units], refs[2 * units]
    table = jnp.transpose(order_ref[...].astype(jnp.float32)).astype(jnp.int32)
    dest, order = table[:, 0:1], table[:, 1:2]
    step = lax.bitwise_xor(lax.shift_right_logical(dest, 1), jnp.full_like(dest, unit))
    side = jnp.where(lax.bitwise_and(dest, 1) == core, 0, 1)
    row = (step * 2 + side) * cap + order
    columns = dest.shape[0]
    total = jnp.zeros((columns, out_ref.shape[1]), jnp.float32)
    offset = pl.multiple_of(core * cap, cap)
    for du in range(units):
        hot = (lax.broadcasted_iota(jnp.int32, (columns, 2 * cap), 1) + 2 * du * cap == row).astype(jnp.bfloat16)
        block = jnp.concatenate([own[du][pl.ds(offset, cap), :], far[du][pl.ds(offset, cap), :]], axis=0)
        total = total + dot(hot, block)
    out_ref[...] = total.astype(jnp.bfloat16)


def per_device(state, dest_map, day_mask, cloud, conv_in, conv_mid, conv_out, rad_in, rad_mid, rad_out):
    groups, bands = lax.axis_size("elem"), lax.axis_size("band")
    units, half, away = groups // 2, groups // 4, bands // 2
    cap = cloud.shape[0] // groups
    columns, features = state.shape
    elem = lax.axis_index("elem")
    core, unit = elem % 2, elem // 2
    upper = (unit >= half).astype(jnp.int32)
    ids = jnp.stack([core, unit, upper]).astype(jnp.int32)
    smem = pl.BlockSpec(memory_space=pltpu.SMEM)
    vmem = pl.BlockSpec(memory_space=pltpu.VMEM)
    params = pltpu.CompilerParams(vmem_limit_bytes=VMEM_BYTES)

    def swapped(block):
        return moved(block, lambda e, b: (e ^ 1, b))

    maps = jnp.concatenate([dest_map.reshape(1, columns), day_mask.reshape(1, columns)], axis=0)
    far_maps = swapped(maps)
    far_state = swapped(state)

    packet = jax.ShapeDtypeStruct((2 * cap + FLAG_ROWS, features), jnp.bfloat16)
    order, *packets = pl.pallas_call(
        functools.partial(place_kernel, groups, cap),
        out_shape=[jax.ShapeDtypeStruct((8, columns), jnp.int32)] + [packet] * units,
        in_specs=[smem] + [vmem] * 4,
        out_specs=[vmem] * (units + 1),
        compiler_params=params,
        name="place_columns",
    )(ids, maps, far_maps, state, far_state)

    came = [packets[0]] + [None] * (units - 1)
    for low in range(half):
        for du in (half + low, low):
            if du:
                came[du] = moved(packets[du], lambda e, b: (e ^ (2 * du), b))

    lent = []
    for low in range(half):
        leaving = jnp.where(upper == 0, came[half + low], came[low])
        lent.append(moved(leaving, lambda e, b: (e, (b + away) % bands)))

    answers = [None] * units
    new_cloud = None
    tile = jax.ShapeDtypeStruct((2 * cap, features), jnp.bfloat16)
    weights = (conv_in, conv_mid, conv_out, rad_in, rad_mid, rad_out)
    whole = lambda a: pl.BlockSpec(a.shape, lambda i, ids: (0, 0))
    for low in range(half):
        lower_unit = (unit % half) ^ low
        call_ids = jnp.stack([lower_unit, half + lower_unit, upper]).astype(jnp.int32)
        cloud_spec = pl.BlockSpec((2 * cap, cloud.shape[1]), lambda i, ids: (ids[i], 0))
        base = () if new_cloud is None else (new_cloud,)
        args = (came[low], came[half + low], lent[low], cloud) + weights + base
        answers[low], answers[half + low], new_cloud = pl.pallas_call(
            functools.partial(physics_kernel, cap, bool(base)),
            grid_spec=pltpu.PrefetchScalarGridSpec(
                num_scalar_prefetch=1,
                grid=(2,),
                in_specs=[whole(came[low])] * 3 + [cloud_spec] + [whole(w) for w in weights]
                + [pl.BlockSpec(memory_space=pl.ANY)] * len(base),
                out_specs=[pl.BlockSpec(tile.shape, lambda i, ids: (0, 0))] * 2 + [cloud_spec],
            ),
            out_shape=[tile, tile, jax.ShapeDtypeStruct(cloud.shape, jnp.bfloat16)],
            input_output_aliases={len(args): 2} if base else {},
            compiler_params=params,
            name="column_physics",
        )(call_ids, *args)

    def home(du):
        def target(e, b):
            to_elem = e ^ (2 * du)
            return to_elem, (b + away) % bands if to_elem >= groups // 2 else b

        return target

    back, far_back = [None] * units, [None] * units
    for low in range(half):
        for du in (low, half + low):
            back[du] = moved(answers[du], home(du))
            far_back[du] = swapped(back[du])

    tendency = pl.pallas_call(
        functools.partial(collect_kernel, groups, cap),
        out_shape=jax.ShapeDtypeStruct(state.shape, jnp.bfloat16),
        in_specs=[smem] + [vmem] * (2 * units + 1),
        out_specs=vmem,
        compiler_params=params,
        name="collect_columns",
    )(ids, order, *back, *far_back)
    return (tendency, new_cloud)


def solution(mesh):
    rows = P(("elem", "band"), None)
    return jax.shard_map(
        per_device,
        mesh=mesh,
        in_specs=(rows,) * 4 + (P(),) * 6,
        out_specs=(rows, rows),
        check_vma=False,
    )
```

time: 67.5 us -> 56.8 us (0.84)
  the two profiles are of different devices: /device:TPU:2 before, /device:TPU:5 now
where the time goes in v1:
time: 56.8 us; the launch traced here: 56.5 us
  starting transfers between devices  31.6 us (56%)
  Pallas kernels  9.48 us (17%)
  waiting for transfers between devices  8.01 us (14%)
  local copies, waits for them, and re-layouts  5.61 us (10%)
  other arithmetic  0.97 us (2%)
  between operations  0.76 us (1%)
    ppermute x15, starting transfers between devices, moved(): return lax.ppermute(block, ('elem', 'band'), route)  31.6 us
    ppermute x15, waiting for transfers between devices, moved(): return lax.ppermute(block, ('elem', 'band'), route)  8.01 us
    pallas_call x2, Pallas kernels, per_device(): pl.pallas_call(functools.partial(physics_kernel, cap, bool(base)), grid_s...  5.86 us
    unnamed x24, local copies, waits for them, and re-layouts  5.61 us
    pallas_call x1, Pallas kernels, per_device(): pl.pallas_call(functools.partial(collect_kernel, groups, cap), out_shape=...  2.08 us
    pallas_call x1, Pallas kernels, per_device(): pl.pallas_call(functools.partial(place_kernel, groups, cap), out_shape=[j...  1.54 us
  transfers between devices with their start and end apart: 15, of which 5 were waited for; matrix products, arithmetic and copies ran while one was open for 2% of the time, Pallas kernels for 10%

profile of v1, /device:TPU:5, one launch (start us, length us, event | category | flops | bytes accessed | tf_op | source)
XLA Modules:
  0.0 56.5 jit_solution(18436488019165110439)
XLA Ops:
  0.6 0.0 copy-start
  0.6 0.7 %collective-permute-start.1 = (bf16[512,256]{1,0:T(8,128)(2,1)}, bf16[512,256]{1,0:T(8,128)(2,1)S(1)}, u32[]{:S(2)}, u32[]{:S(2)}) collective-permute-start(bf16[512,256]{1,0:T(8,128)(2,1)} %state_ref.1), channel_id=1, source_target_pairs={{0,4},{1,5},{2,6},{3,7},{4,0},{5,1},{6,2},{7,3},{8,12},{9,13},{10,... | collective-permute-start | bytes 786440 | tf_op jit(solution)/shard_map/ppermute | solution.py:21
  1.4 0.7 %pad_add_fusion.maps_ref = s32[2,512]{1,0:T(2,128)S(1)} fusion(s32[1,512]{1,0:T(1,128)} %bitcast.9, s32[1,512]{1,0:T(1,128)} %bitcast.10), kind=kLoop, calls=%fused_computation.2 | loop fusion | flops 1024 | bytes 8192 | tf_op jit(solution)/shard_map/concatenate | solution.py:162
  2.1 0.1 collective-permute-start
  2.2 0.1 add_add_fusion.ids_ref
  2.3 1.0 %collective-permute-done.far_maps_ref = s32[2,512]{1,0:T(2,128)S(1)} collective-permute-done((s32[2,512]{1,0:T(2,128)S(1)}, s32[2,512]{1,0:T(2,128)S(1)}, u32[]{:S(2)}, u32[]{:S(2)}) %collective-permute-start) | collective-permute-done | bytes 4128 | tf_op jit(solution)/shard_map/ppermute | solution.py:21
  3.3 0.0 collective-permute-done.1.far_state_ref
  3.3 0.0 copy-start.11
  3.3 0.9 %copy-done.11 = bf16[512,256]{1,0:T(8,128)(2,1)S(1)} copy-done((bf16[512,256]{1,0:T(8,128)(2,1)S(1)}, bf16[512,256]{1,0:T(8,128)(2,1)}, u32[]{:S(2)}) %copy-start.11) | copy-done | bytes 262168
  4.2 1.5 %place_columns.1 = (s32[8,512]{1,0:T(8,128)S(1)}, bf16[272,256]{1,0:T(8,128)(2,1)S(1)}, bf16[272,256]{1,0:T(8,128)(2,1)S(1)}, bf16[272,256]{1,0:T(8,128)(2,1)S(1)}, bf16[272,256]{1,0:T(8,128)(2,1)S(1)}) custom-call(s32[3]{0:T(128)S(1)} %add_add_fusion.ids_ref, s32[2,512]{1,0:T(2,128)S(1)} %pad_add_fusion.maps_ref, ...), custom_call_target="tpu_custom_call" | custom-call | tf_op jit(solution)/shard_map/place_columns/pallas_call | solution.py:167
  5.8 0.1 collective-permute-start.2
  5.9 1.4 %collective-permute-start.5 = (bf16[272,256]{1,0:T(8,128)(2,1)S(1)}, bf16[272,256]{1,0:T(8,128)(2,1)S(1)}, u32[]{:S(2)}, u32[]{:S(2)}) collective-permute-start(bf16[272,256]{1,0:T(8,128)(2,1)S(1)} %get-tuple-element.17), channel_id=1, source_target_pairs={{0,8},{1,9},{2,10},{3,11},{4,12},{5,13},{6,14},{7,15},{8,0},{9,1},... | collective-permute-start | bytes 417800 | tf_op jit(solution)/shard_map/ppermute | solution.py:21
  7.3 1.2 %collective-permute-start.6 = (bf16[272,256]{1,0:T(8,128)(2,1)S(1)}, bf16[272,256]{1,0:T(8,128)(2,1)S(1)}, u32[]{:S(2)}, u32[]{:S(2)}) collective-permute-start(bf16[272,256]{1,0:T(8,128)(2,1)S(1)} %get-tuple-element.18), channel_id=1, source_target_pairs={{0,24},{1,25},{2,26},{3,27},{4,28},{5,29},{6,30},{7,31},{8,16},{9,... | collective-permute-start | bytes 417800 | tf_op jit(solution)/shard_map/ppermute | solution.py:21
  8.5 2.5 %collective-permute-done.2.cross_ref = bf16[272,256]{1,0:T(8,128)(2,1)S(1)} collective-permute-done((bf16[272,256]{1,0:T(8,128)(2,1)S(1)}, bf16[272,256]{1,0:T(8,128)(2,1)S(1)}, u32[]{:S(2)}, u32[]{:S(2)}) %collective-permute-start.2) | collective-permute-done | bytes 139296 | tf_op jit(solution)/shard_map/ppermute | solution.py:21
  10.9 0.0 copy-start.1
  11.0 2.4 %collective-permute-start.3 = (bf16[272,256]{1,0:T(8,128)(2,1)S(1)}, bf16[272,256]{1,0:T(8,128)(2,1)S(1)}, u32[]{:S(2)}, u32[]{:S(2)}) collective-permute-start(bf16[272,256]{1,0:T(8,128)(2,1)S(1)} %broadcast_select_fusion.1), channel_id=1, source_target_pairs={{0,2},{1,3},{2,0},{3,1},{4,6},{5,7},{6,4},{7,5},{8,10},{9,11},{10,... | collective-permute-start | bytes 417800 | tf_op jit(solution)/shard_map/ppermute | solution.py:21
  13.3 0.0 collective-permute-done.5.near_ref
  13.3 1.4 %collective-permute-done.6.cross_ref = bf16[272,256]{1,0:T(8,128)(2,1)S(1)} collective-permute-done((bf16[272,256]{1,0:T(8,128)(2,1)S(1)}, bf16[272,256]{1,0:T(8,128)(2,1)S(1)}, u32[]{:S(2)}, u32[]{:S(2)}) %collective-permute-start.6) | collective-permute-done | bytes 139296 | tf_op jit(solution)/shard_map/ppermute | solution.py:21
  14.8 2.4 %collective-permute-start.7 = (bf16[272,256]{1,0:T(8,128)(2,1)S(1)}, bf16[272,256]{1,0:T(8,128)(2,1)S(1)}, u32[]{:S(2)}, u32[]{:S(2)}) collective-permute-start(bf16[272,256]{1,0:T(8,128)(2,1)S(1)} %broadcast_select_fusion), channel_id=1, source_target_pairs={{0,2},{1,3},{2,0},{3,1},{4,6},{5,7},{6,4},{7,5},{8,10},{9,11},{10,... | collective-permute-start | bytes 417800 | tf_op jit(solution)/shard_map/ppermute | solution.py:21
  17.2 0.1 add_add_fusion.1.ids_ref
  17.3 0.1 add_add_fusion.2.ids_ref
  17.3 2.1 %collective-permute-done.3.lent_ref = bf16[272,256]{1,0:T(8,128)(2,1)S(1)} collective-permute-done((bf16[272,256]{1,0:T(8,128)(2,1)S(1)}, bf16[272,256]{1,0:T(8,128)(2,1)S(1)}, u32[]{:S(2)}, u32[]{:S(2)}) %collective-permute-start.3) | collective-permute-done | bytes 139296 | tf_op jit(solution)/shard_map/ppermute | solution.py:21
  19.4 0.0 copy-done
  19.4 0.0 copy-done.1
  19.4 0.0 copy-start.2
  19.4 1.0 %copy-done.2 = bf16[256,768]{1,0:T(8,128)(2,1)S(1)} copy-done((bf16[256,768]{1,0:T(8,128)(2,1)S(1)}, bf16[256,768]{1,0:T(8,128)(2,1)}, u32[]{:S(2)}) %copy-start.2) | copy-done | bytes 393240
  20.4 0.0 copy-start.4
  20.4 1.0 %copy-done.4 = bf16[768,256]{1,0:T(8,128)(2,1)S(1)} copy-done((bf16[768,256]{1,0:T(8,128)(2,1)S(1)}, bf16[768,256]{1,0:T(8,128)(2,1)}, u32[]{:S(2)}) %copy-start.4) | copy-done | bytes 393240
  21.4 0.0 copy-start.6
  21.4 0.9 %copy-done.6 = bf16[256,256]{1,0:T(8,128)(2,1)S(1)} copy-done((bf16[256,256]{1,0:T(8,128)(2,1)S(1)}, bf16[256,256]{1,0:T(8,128)(2,1)}, u32[]{:S(2)}) %copy-start.6) | copy-done | bytes 131096
  22.3 0.0 copy-start.7
  22.3 0.9 %copy-done.7 = bf16[256,256]{1,0:T(8,128)(2,1)S(1)} copy-done((bf16[256,256]{1,0:T(8,128)(2,1)S(1)}, bf16[256,256]{1,0:T(8,128)(2,1)}, u32[]{:S(2)}) %copy-start.7) | copy-done | bytes 131096
  23.2 0.0 copy-start.9
  23.2 0.8 %copy-done.9 = bf16[256,128]{1,0:T(8,128)(2,1)S(1)} copy-done((bf16[256,128]{1,0:T(8,128)(2,1)S(1)}, bf16[256,128]{1,0:T(8,128)(2,1)}, u32[]{:S(2)}) %copy-start.9) | copy-done | bytes 65560
  24.1 0.0 copy-start.3
  24.1 0.0 copy-start.5
  24.1 0.0 copy-start.8
  24.1 0.0 copy-start.10
  24.1 2.9 %column_physics.2 = (bf16[256,256]{1,0:T(8,128)(2,1)S(1)}, bf16[256,256]{1,0:T(8,128)(2,1)S(1)}, bf16[1024,512]{1,0:T(8,128)(2,1)}) custom-call(s32[3]{0:T(128)S(1)} %add_add_fusion.1.ids_ref, bf16[272,256]{1,0:T(8,128)(2,1)S(1)} %get-tuple-element.14.near_ref, bf16[272,256]{1,0:T(8,128)(2,1)S(1)} %collective-permute-done.2.cross_ref, ...), custom_call_target="tpu_custom_call" | custom-call | tf_op jit(solution)/shard_map/column_physics/pallas_call | solution.py:198
  27.0 1.9 %collective-permute-start.4 = (bf16[256,256]{1,0:T(8,128)(2,1)S(1)}, bf16[256,256]{1,0:T(8,128)(2,1)S(1)}, u32[]{:S(2)}, u32[]{:S(2)}) collective-permute-start(bf16[256,256]{1,0:T(8,128)(2,1)S(1)} %get-tuple-element.16), channel_id=1, source_target_pairs={{0,0},{1,1},{2,2},{3,3},{4,4},{5,5},{6,6},{7,7},{8,8},{9,9},{10,10... | collective-permute-start | bytes 393224 | tf_op jit(solution)/shard_map/ppermute | solution.py:21
  28.9 0.0 collective-permute-done.7.lent_ref
  29.0 0.0 copy-done.3
  29.0 0.0 copy-done.5
  29.0 0.0 copy-done.8
  29.0 0.0 copy-done.10
  29.0 2.9 %column_physics.3 = (bf16[256,256]{1,0:T(8,128)(2,1)S(1)}, bf16[256,256]{1,0:T(8,128)(2,1)S(1)}, bf16[1024,512]{1,0:T(8,128)(2,1)}) custom-call(s32[3]{0:T(128)S(1)} %add_add_fusion.2.ids_ref, bf16[272,256]{1,0:T(8,128)(2,1)S(1)} %collective-permute-done.5.near_ref, ...), custom_call_target="tpu_custom_call", output_to_operand_aliasing={{2}: (11, {})} | custom-call | tf_op jit(solution)/shard_map/column_physics/pallas_call | solution.py:198
  31.9 3.3 %collective-permute-start.8 = (bf16[256,256]{1,0:T(8,128)(2,1)S(1)}, bf16[256,256]{1,0:T(8,128)(2,1)S(1)}, u32[]{:S(2)}, u32[]{:S(2)}) collective-permute-start(bf16[256,256]{1,0:T(8,128)(2,1)S(1)} %get-tuple-element.20), channel_id=1, source_target_pairs={{0,8},{1,9},{2,10},{3,11},{4,12},{5,13},{6,14},{7,15},{8,0},{9,1},... | collective-permute-start | bytes 393224 | tf_op jit(solution)/shard_map/ppermute | solution.py:21
  35.2 0.0 collective-permute-start.9
  35.2 1.2 %collective-permute-start.10 = (bf16[256,256]{1,0:T(8,128)(2,1)S(1)}, bf16[256,256]{1,0:T(8,128)(2,1)S(1)}, u32[]{:S(2)}, u32[]{:S(2)}) collective-permute-start(bf16[256,256]{1,0:T(8,128)(2,1)S(1)} %get-tuple-element.22), channel_id=1, source_target_pairs={{0,26},{1,27},{2,24},{3,25},{4,30},{5,31},{6,28},{7,29},{8,18},{9,... | collective-permute-start | bytes 393224 | tf_op jit(solution)/shard_map/ppermute | solution.py:21
  36.4 0.0 collective-permute-done.4.refs_0_
  36.4 6.6 %collective-permute-start.11 = (bf16[256,256]{1,0:T(8,128)(2,1)S(1)}, bf16[256,256]{1,0:T(8,128)(2,1)S(1)}, u32[]{:S(2)}, u32[]{:S(2)}) collective-permute-start(bf16[256,256]{1,0:T(8,128)(2,1)S(1)} %collective-permute-done.4.refs_0_), channel_id=1, source_target_pairs={{0,4},{1,5},{2,6},{3,7},{4,0},{5,1},{6,2},{7,3},{8,12},{9,13},{10,... | collective-permute-start | bytes 393224 | tf_op jit(solution)/shard_map/ppermute | solution.py:21
  43.0 0.0 collective-permute-done.8.refs_1_
  43.0 4.4 %collective-permute-start.12 = (bf16[256,256]{1,0:T(8,128)(2,1)S(1)}, bf16[256,256]{1,0:T(8,128)(2,1)S(1)}, u32[]{:S(2)}, u32[]{:S(2)}) collective-permute-start(bf16[256,256]{1,0:T(8,128)(2,1)S(1)} %collective-permute-done.8.refs_1_), channel_id=1, source_target_pairs={{0,4},{1,5},{2,6},{3,7},{4,0},{5,1},{6,2},{7,3},{8,12},{9,13},{10,... | collective-permute-start | bytes 393224 | tf_op jit(solution)/shard_map/ppermute | solution.py:21
  47.3 0.0 collective-permute-done.9.refs_2_
  47.3 4.7 %collective-permute-start.13 = (bf16[256,256]{1,0:T(8,128)(2,1)S(1)}, bf16[256,256]{1,0:T(8,128)(2,1)S(1)}, u32[]{:S(2)}, u32[]{:S(2)}) collective-permute-start(bf16[256,256]{1,0:T(8,128)(2,1)S(1)} %collective-permute-done.9.refs_2_), channel_id=1, source_target_pairs={{0,4},{1,5},{2,6},{3,7},{4,0},{5,1},{6,2},{7,3},{8,12},{9,13},{10,... | collective-permute-start | bytes 393224 | tf_op jit(solution)/shard_map/ppermute | solution.py:21
  52.0 0.0 collective-permute-done.10.refs_3_
  52.0 1.4 %collective-permute-start.14 = (bf16[256,256]{1,0:T(8,128)(2,1)S(1)}, bf16[256,256]{1,0:T(8,128)(2,1)S(1)}, u32[]{:S(2)}, u32[]{:S(2)}) collective-permute-start(bf16[256,256]{1,0:T(8,128)(2,1)S(1)} %collective-permute-done.10.refs_3_), channel_id=1, source_target_pairs={{0,4},{1,5},{2,6},{3,7},{4,0},{5,1},{6,2},{7,3},{8,12},{9,13},{10,... | collective-permute-start | bytes 393224 | tf_op jit(solution)/shard_map/ppermute | solution.py:21
  53.4 0.0 collective-permute-done.11.refs_4_
  53.4 0.0 collective-permute-done.12.refs_5_
  53.4 0.0 collective-permute-done.13.refs_6_
  53.4 1.0 %collective-permute-done.14.refs_7_ = bf16[256,256]{1,0:T(8,128)(2,1)S(1)} collective-permute-done((bf16[256,256]{1,0:T(8,128)(2,1)S(1)}, bf16[256,256]{1,0:T(8,128)(2,1)S(1)}, u32[]{:S(2)}, u32[]{:S(2)}) %collective-permute-start.14) | collective-permute-done | bytes 131104 | tf_op jit(solution)/shard_map/ppermute | solution.py:21
  54.4 2.1 %collect_columns.1 = bf16[512,256]{1,0:T(8,128)(2,1)} custom-call(s32[3]{0:T(128)S(1)} %add_add_fusion.ids_ref, s32[8,512]{1,0:T(8,128)S(1)} %get-tuple-element.13.order_ref, bf16[256,256]{1,0:T(8,128)(2,1)S(1)} %collective-permute-done.4.refs_0_, bf16[256,256]{1,0:T(8,128)(2,1)S(1)} %collective-permute-done.8.refs_1_, ...), custom_call_target="tpu_custom_call" | custom-call | tf_op jit(solution)/shard_map/collect_columns/pallas_call | solution.py:226
  (2 shorter events, 0.0 us)
Async XLA Ops:
  0.6 18.8 %copy-start = (bf16[1024,512]{1,0:T(8,128)(2,1)S(1)}, bf16[1024,512]{1,0:T(8,128)(2,1)}, u32[]{:S(2)}) copy-start(bf16[1024,512]{1,0:T(8,128)(2,1)} %cloud_ref.3) | copy-start | bytes 3145732
  0.6 2.6 %collective-permute-start.1 = (bf16[512,256]{1,0:T(8,128)(2,1)}, bf16[512,256]{1,0:T(8,128)(2,1)S(1)}, u32[]{:S(2)}, u32[]{:S(2)}) collective-permute-start(bf16[512,256]{1,0:T(8,128)(2,1)} %state_ref.1), channel_id=1, source_target_pairs={{0,4},{1,5},{2,6},{3,7},{4,0},{5,1},{6,2},{7,3},{8,12},{9,13},{10,... | collective-permute-start | bytes 786440 | tf_op jit(solution)/shard_map/ppermute | solution.py:21
  2.1 1.2 %collective-permute-start = (s32[2,512]{1,0:T(2,128)S(1)}, s32[2,512]{1,0:T(2,128)S(1)}, u32[]{:S(2)}, u32[]{:S(2)}) collective-permute-start(s32[2,512]{1,0:T(2,128)S(1)} %pad_add_fusion.maps_ref), channel_id=1, source_target_pairs={{0,4},{1,5},{2,6},{3,7},{4,0},{5,1},{6,2},{7,3},{8,12},{9,13},{10,... | collective-permute-start | bytes 12296 | tf_op jit(solution)/shard_map/ppermute | solution.py:21
  3.3 1.0 %copy-start.11 = (bf16[512,256]{1,0:T(8,128)(2,1)S(1)}, bf16[512,256]{1,0:T(8,128)(2,1)}, u32[]{:S(2)}) copy-start(bf16[512,256]{1,0:T(8,128)(2,1)} %state_ref.1) | copy-start | bytes 786436
  5.8 5.2 %collective-permute-start.2 = (bf16[272,256]{1,0:T(8,128)(2,1)S(1)}, bf16[272,256]{1,0:T(8,128)(2,1)S(1)}, u32[]{:S(2)}, u32[]{:S(2)}) collective-permute-start(bf16[272,256]{1,0:T(8,128)(2,1)S(1)} %get-tuple-element.15), channel_id=1, source_target_pairs={{0,16},{1,17},{2,18},{3,19},{4,20},{5,21},{6,22},{7,23},{8,24},{9,... | collective-permute-start | bytes 417800 | tf_op jit(solution)/shard_map/ppermute | solution.py:21
  5.9 7.5 %collective-permute-start.5 = (bf16[272,256]{1,0:T(8,128)(2,1)S(1)}, bf16[272,256]{1,0:T(8,128)(2,1)S(1)}, u32[]{:S(2)}, u32[]{:S(2)}) collective-permute-start(bf16[272,256]{1,0:T(8,128)(2,1)S(1)} %get-tuple-element.17), channel_id=1, source_target_pairs={{0,8},{1,9},{2,10},{3,11},{4,12},{5,13},{6,14},{7,15},{8,0},{9,1},... | collective-permute-start | bytes 417800 | tf_op jit(solution)/shard_map/ppermute | solution.py:21
  7.3 7.5 %collective-permute-start.6 = (bf16[272,256]{1,0:T(8,128)(2,1)S(1)}, bf16[272,256]{1,0:T(8,128)(2,1)S(1)}, u32[]{:S(2)}, u32[]{:S(2)}) collective-permute-start(bf16[272,256]{1,0:T(8,128)(2,1)S(1)} %get-tuple-element.18), channel_id=1, source_target_pairs={{0,24},{1,25},{2,26},{3,27},{4,28},{5,29},{6,30},{7,31},{8,16},{9,... | collective-permute-start | bytes 417800 | tf_op jit(solution)/shard_map/ppermute | solution.py:21
  10.9 8.5 %copy-start.1 = (bf16[768,256]{1,0:T(8,128)(2,1)S(1)}, bf16[768,256]{1,0:T(8,128)(2,1)}, u32[]{:S(2)}) copy-start(bf16[768,256]{1,0:T(8,128)(2,1)} %conv_in.3) | copy-start | bytes 1179652
  11.0 8.5 %collective-permute-start.3 = (bf16[272,256]{1,0:T(8,128)(2,1)S(1)}, bf16[272,256]{1,0:T(8,128)(2,1)S(1)}, u32[]{:S(2)}, u32[]{:S(2)}) collective-permute-start(bf16[272,256]{1,0:T(8,128)(2,1)S(1)} %broadcast_select_fusion.1), channel_id=1, source_target_pairs={{0,2},{1,3},{2,0},{3,1},{4,6},{5,7},{6,4},{7,5},{8,10},{9,11},{10,... | collective-permute-start | bytes 417800 | tf_op jit(solution)/shard_map/ppermute | solution.py:21
  14.8 14.1 %collective-permute-start.7 = (bf16[272,256]{1,0:T(8,128)(2,1)S(1)}, bf16[272,256]{1,0:T(8,128)(2,1)S(1)}, u32[]{:S(2)}, u32[]{:S(2)}) collective-permute-start(bf16[272,256]{1,0:T(8,128)(2,1)S(1)} %broadcast_select_fusion), channel_id=1, source_target_pairs={{0,2},{1,3},{2,0},{3,1},{4,6},{5,7},{6,4},{7,5},{8,10},{9,11},{10,... | collective-permute-start | bytes 417800 | tf_op jit(solution)/shard_map/ppermute | solution.py:21
  19.4 1.0 %copy-start.2 = (bf16[256,768]{1,0:T(8,128)(2,1)S(1)}, bf16[256,768]{1,0:T(8,128)(2,1)}, u32[]{:S(2)}) copy-start(bf16[256,768]{1,0:T(8,128)(2,1)} %conv_out.3) | copy-start | bytes 1179652
  20.4 1.0 %copy-start.4 = (bf16[768,256]{1,0:T(8,128)(2,1)S(1)}, bf16[768,256]{1,0:T(8,128)(2,1)}, u32[]{:S(2)}) copy-start(bf16[768,256]{1,0:T(8,128)(2,1)} %rad_in.3) | copy-start | bytes 1179652
  21.4 0.9 %copy-start.6 = (bf16[256,256]{1,0:T(8,128)(2,1)S(1)}, bf16[256,256]{1,0:T(8,128)(2,1)}, u32[]{:S(2)}) copy-start(bf16[256,256]{1,0:T(8,128)(2,1)} %conv_mid.3) | copy-start | bytes 393220
  22.3 0.9 %copy-start.7 = (bf16[256,256]{1,0:T(8,128)(2,1)S(1)}, bf16[256,256]{1,0:T(8,128)(2,1)}, u32[]{:S(2)}) copy-start(bf16[256,256]{1,0:T(8,128)(2,1)} %rad_mid.3) | copy-start | bytes 393220
  23.2 0.8 %copy-start.9 = (bf16[256,128]{1,0:T(8,128)(2,1)S(1)}, bf16[256,128]{1,0:T(8,128)(2,1)}, u32[]{:S(2)}) copy-start(bf16[256,128]{1,0:T(8,128)(2,1)} %rad_out.3) | copy-start | bytes 196612
  24.1 4.9 %copy-start.3 = (bf16[256,768]{1,0:T(8,128)(2,1)S(1)}, bf16[256,768]{1,0:T(8,128)(2,1)}, u32[]{:S(2)}) copy-start(bf16[256,768]{1,0:T(8,128)(2,1)} %conv_out.3) | copy-start | bytes 1179652
  24.1 4.9 %copy-start.5 = (bf16[768,256]{1,0:T(8,128)(2,1)S(1)}, bf16[768,256]{1,0:T(8,128)(2,1)}, u32[]{:S(2)}) copy-start(bf16[768,256]{1,0:T(8,128)(2,1)} %rad_in.3) | copy-start | bytes 1179652
  24.1 4.9 %copy-start.8 = (bf16[256,256]{1,0:T(8,128)(2,1)S(1)}, bf16[256,256]{1,0:T(8,128)(2,1)}, u32[]{:S(2)}) copy-start(bf16[256,256]{1,0:T(8,128)(2,1)} %rad_mid.3) | copy-start | bytes 393220
  24.1 4.9 %copy-start.10 = (bf16[256,128]{1,0:T(8,128)(2,1)S(1)}, bf16[256,128]{1,0:T(8,128)(2,1)}, u32[]{:S(2)}) copy-start(bf16[256,128]{1,0:T(8,128)(2,1)} %rad_out.3) | copy-start | bytes 196612
  27.0 9.3 %collective-permute-start.4 = (bf16[256,256]{1,0:T(8,128)(2,1)S(1)}, bf16[256,256]{1,0:T(8,128)(2,1)S(1)}, u32[]{:S(2)}, u32[]{:S(2)}) collective-permute-start(bf16[256,256]{1,0:T(8,128)(2,1)S(1)} %get-tuple-element.16), channel_id=1, source_target_pairs={{0,0},{1,1},{2,2},{3,3},{4,4},{5,5},{6,6},{7,7},{8,8},{9,9},{10,10... | collective-permute-start | bytes 393224 | tf_op jit(solution)/shard_map/ppermute | solution.py:21
  31.9 11.0 %collective-permute-start.8 = (bf16[256,256]{1,0:T(8,128)(2,1)S(1)}, bf16[256,256]{1,0:T(8,128)(2,1)S(1)}, u32[]{:S(2)}, u32[]{:S(2)}) collective-permute-start(bf16[256,256]{1,0:T(8,128)(2,1)S(1)} %get-tuple-element.20), channel_id=1, source_target_pairs={{0,8},{1,9},{2,10},{3,11},{4,12},{5,13},{6,14},{7,15},{8,0},{9,1},... | collective-permute-start | bytes 393224 | tf_op jit(solution)/shard_map/ppermute | solution.py:21
  35.2 12.2 %collective-permute-start.9 = (bf16[256,256]{1,0:T(8,128)(2,1)S(1)}, bf16[256,256]{1,0:T(8,128)(2,1)S(1)}, u32[]{:S(2)}, u32[]{:S(2)}) collective-permute-start(bf16[256,256]{1,0:T(8,128)(2,1)S(1)} %get-tuple-element.21), channel_id=1, source_target_pairs={{0,18},{1,19},{2,16},{3,17},{4,22},{5,23},{6,20},{7,21},{8,26},{9,... | collective-permute-start | bytes 393224 | tf_op jit(solution)/shard_map/ppermute | solution.py:21
  35.2 16.8 %collective-permute-start.10 = (bf16[256,256]{1,0:T(8,128)(2,1)S(1)}, bf16[256,256]{1,0:T(8,128)(2,1)S(1)}, u32[]{:S(2)}, u32[]{:S(2)}) collective-permute-start(bf16[256,256]{1,0:T(8,128)(2,1)S(1)} %get-tuple-element.22), channel_id=1, source_target_pairs={{0,26},{1,27},{2,24},{3,25},{4,30},{5,31},{6,28},{7,29},{8,18},{9,... | collective-permute-start | bytes 393224 | tf_op jit(solution)/shard_map/ppermute | solution.py:21
  36.4 17.0 %collective-permute-start.11 = (bf16[256,256]{1,0:T(8,128)(2,1)S(1)}, bf16[256,256]{1,0:T(8,128)(2,1)S(1)}, u32[]{:S(2)}, u32[]{:S(2)}) collective-permute-start(bf16[256,256]{1,0:T(8,128)(2,1)S(1)} %collective-permute-done.4.refs_0_), channel_id=1, source_target_pairs={{0,4},{1,5},{2,6},{3,7},{4,0},{5,1},{6,2},{7,3},{8,12},{9,13},{10,... | collective-permute-start | bytes 393224 | tf_op jit(solution)/shard_map/ppermute | solution.py:21
  43.0 10.5 %collective-permute-start.12 = (bf16[256,256]{1,0:T(8,128)(2,1)S(1)}, bf16[256,256]{1,0:T(8,128)(2,1)S(1)}, u32[]{:S(2)}, u32[]{:S(2)}) collective-permute-start(bf16[256,256]{1,0:T(8,128)(2,1)S(1)} %collective-permute-done.8.refs_1_), channel_id=1, source_target_pairs={{0,4},{1,5},{2,6},{3,7},{4,0},{5,1},{6,2},{7,3},{8,12},{9,13},{10,... | collective-permute-start | bytes 393224 | tf_op jit(solution)/shard_map/ppermute | solution.py:21
  47.3 6.1 %collective-permute-start.13 = (bf16[256,256]{1,0:T(8,128)(2,1)S(1)}, bf16[256,256]{1,0:T(8,128)(2,1)S(1)}, u32[]{:S(2)}, u32[]{:S(2)}) collective-permute-start(bf16[256,256]{1,0:T(8,128)(2,1)S(1)} %collective-permute-done.9.refs_2_), channel_id=1, source_target_pairs={{0,4},{1,5},{2,6},{3,7},{4,0},{5,1},{6,2},{7,3},{8,12},{9,13},{10,... | collective-permute-start | bytes 393224 | tf_op jit(solution)/shard_map/ppermute | solution.py:21
  52.0 2.4 %collective-permute-start.14 = (bf16[256,256]{1,0:T(8,128)(2,1)S(1)}, bf16[256,256]{1,0:T(8,128)(2,1)S(1)}, u32[]{:S(2)}, u32[]{:S(2)}) collective-permute-start(bf16[256,256]{1,0:T(8,128)(2,1)S(1)} %collective-permute-done.10.refs_3_), channel_id=1, source_target_pairs={{0,4},{1,5},{2,6},{3,7},{4,0},{5,1},{6,2},{7,3},{8,12},{9,13},{10,... | collective-permute-start | bytes 393224 | tf_op jit(solution)/shard_map/ppermute | solution.py:21

commit v2 on v1

v2 whole, which is shorter than its diff:
```python
import functools

import jax
import jax.numpy as jnp
from jax import lax
from jax.experimental import pallas as pl
from jax.experimental.pallas import tpu as pltpu
from jax.sharding import PartitionSpec as P

VMEM_BYTES = 24 * 1024 * 1024
FLAG_ROWS = 16


def moved(block, target):
    groups, bands = lax.axis_size("elem"), lax.axis_size("band")
    route = []
    for e in range(groups):
        for b in range(bands):
            to = target(e, b)
            if to is not None:
                route.append((e * bands + b, to[0] * bands + to[1]))
    return lax.ppermute(block, ("elem", "band"), route)


def work(microseconds):
    return pl.CostEstimate(flops=int(microseconds * 1.15e9), bytes_accessed=0, transcendentals=0)


def dot(a, b):
    return jnp.dot(a, b, preferred_element_type=jnp.float32)


def as_row(table):
    return jnp.concatenate([table[r : r + 1, :] for r in range(table.shape[0])], axis=1)


def orders(dest, groups):
    count = dest.shape[1]
    lanes = 128
    hot = (lax.broadcasted_iota(jnp.int32, (groups, count), 0) == dest).astype(jnp.float32)
    before = (
        lax.broadcasted_iota(jnp.int32, (lanes, lanes), 0)
        < lax.broadcasted_iota(jnp.int32, (lanes, lanes), 1)
    ).astype(jnp.bfloat16)
    parts, seen = [], jnp.zeros((groups, 1), jnp.float32)
    for start in range(0, count, lanes):
        piece = hot[:, start : start + lanes]
        inside = dot(piece.astype(jnp.bfloat16), before)
        parts.append(jnp.sum(piece * (inside + seen), axis=0, keepdims=True))
        seen = seen + jnp.sum(piece, axis=1, keepdims=True)
    return jnp.concatenate(parts, axis=1).astype(jnp.int32)


def place_kernel(groups, cap, ids_ref, far_dest_ref, far_day_ref, far_state_ref, *refs):
    units = groups // 2
    dest_ref, day_ref, state_ref, order_ref, *out_refs = refs
    core, unit = ids_ref[0], ids_ref[1]
    columns, features = state_ref.shape
    flags = []
    for far, (dest_table, day_table, rows) in enumerate(
        ((dest_ref, day_ref, state_ref), (far_dest_ref, far_day_ref, far_state_ref))
    ):
        source_core = core if far == 0 else 1 - core
        dest, day = as_row(dest_table[...]), as_row(day_table[...])
        order = orders(dest, groups)
        if far == 0:
            order_ref[...] = jnp.concatenate([dest, order] + [jnp.zeros_like(dest)] * 6, axis=0)
        step = lax.bitwise_xor(lax.shift_right_logical(dest, 1), jnp.full_like(dest, unit))
        row = jnp.where(lax.bitwise_and(dest, 1) == core, step * cap + order, -1)
        hot = (lax.broadcasted_iota(jnp.int32, (units * cap, columns), 0) == row).astype(jnp.bfloat16)
        sun = jnp.broadcast_to(day.astype(jnp.float32), (FLAG_ROWS, columns)).astype(jnp.bfloat16)
        flags.append(
            lax.dot_general(sun, hot, (((1,), (1,)), ((), ())), preferred_element_type=jnp.float32)
        )
        placed = dot(hot, rows[...]).astype(jnp.bfloat16)
        for du in range(units):
            out_refs[du][pl.ds(pl.multiple_of(source_core * cap, cap), cap), :] = placed[du * cap : (du + 1) * cap, :]
    first = jnp.where(core == 0, flags[0], flags[1]).astype(jnp.bfloat16)
    second = jnp.where(core == 0, flags[1], flags[0]).astype(jnp.bfloat16)
    middle = features // 2
    for du in range(units):
        if cap < middle:
            out_refs[du][2 * cap :, :] = jnp.zeros((FLAG_ROWS, features), jnp.bfloat16)
        out_refs[du][2 * cap :, 0:cap] = first[:, du * cap : (du + 1) * cap]
        out_refs[du][2 * cap :, middle : middle + cap] = second[:, du * cap : (du + 1) * cap]


def silu(v):
    return (0.5 * v) * (1.0 + jnp.tanh(0.5 * v))


def as_column(row, cap):
    same = lax.broadcasted_iota(jnp.int32, (cap, cap), 0) == lax.broadcasted_iota(jnp.int32, (cap, cap), 1)
    return jnp.sum(jnp.where(same, jnp.broadcast_to(row, (cap, cap)), 0.0), axis=1, keepdims=True)


def serve(cap, packet, cloud, weights):
    conv_in, conv_mid, conv_out, rad_in, rad_mid, rad_out = weights
    features, levels = packet.shape[1], rad_out.shape[1]
    state = packet[0 : 2 * cap, :]
    conv = silu(dot(state, conv_in[:features, :]) + dot(cloud, conv_in[features:, :])).astype(jnp.bfloat16)
    rad = silu(dot(state, rad_in[:features, :]) + dot(cloud, rad_in[features:, :])).astype(jnp.bfloat16)
    conv = silu(dot(conv, conv_mid[...])).astype(jnp.bfloat16)
    rad = silu(dot(rad, rad_mid[...])).astype(jnp.bfloat16)
    conv = dot(conv, conv_out[...])
    rad = dot(rad, rad_out[...])
    updated = (cloud.astype(jnp.float32) + conv[:, 2 * levels :]).astype(jnp.bfloat16)
    flags = packet[2 * cap : 2 * cap + FLAG_ROWS, :].astype(jnp.float32)[0:1, :]
    middle = features // 2
    day = jnp.concatenate(
        [as_column(flags[:, 0:cap], cap), as_column(flags[:, middle : middle + cap], cap)], axis=0
    )
    heated = conv[:, :levels] + day * rad
    return jnp.concatenate([heated, conv[:, levels : 2 * levels]], axis=1).astype(jnp.bfloat16), updated


def rows_of(unit, cap):
    return pl.ds(pl.multiple_of(unit * 2 * cap, 2 * cap), 2 * cap)


def lower_kernel(groups, cap, base, pick, ids_ref, order_ref, *refs):
    near, cross, cloud_ref, weights, refs = refs[0:2], refs[2:4], refs[4], refs[5:11], refs[11 + base :]
    answers, new_ref, refs = refs[0:2], refs[2], refs[3:]
    core, unit, upper, lower_unit = ids_ref[0], ids_ref[1], ids_ref[2], ids_ref[3]
    packet_ref, updated_ref, sems = refs[-3:]
    copies = []
    for i in range(2):

        @pl.when(upper == 0)
        def _():
            packet_ref[...] = near[i][...]

        @pl.when(upper == 1)
        def _():
            packet_ref[...] = cross[i][...]

        served = rows_of(lax.bitwise_xor(lower_unit, i), cap)
        answers[i][...], updated_ref[i] = serve(cap, packet_ref, cloud_ref[served, :], weights)
        copies.append(pltpu.make_async_copy(updated_ref.at[i], new_ref.at[served, :], sems.at[i]))
        copies[-1].start()
    if pick:
        hot_ref = refs[0]
        table = jnp.transpose(order_ref[...].astype(jnp.float32)).astype(jnp.int32)
        dest, order = table[:, 0:1], table[:, 1:2]
        step = lax.bitwise_xor(lax.shift_right_logical(dest, 1), jnp.full_like(dest, unit))
        side = jnp.where(lax.bitwise_and(dest, 1) == core, 0, 1)
        row = (step * 2 + side) * cap + order
        hot_ref[...] = (lax.broadcasted_iota(jnp.int32, hot_ref.shape, 1) == row).astype(jnp.bfloat16)
    for copy in copies:
        copy.wait()


def upper_kernel(cap, ids_ref, lent_ref, lower_answer_ref, cloud_ref, *refs):
    weights, (straight_ref, crossed_ref, new_ref) = refs[:6], refs[6:]
    upper, upper_unit = ids_ref[2], ids_ref[4]
    answer, new_ref[...] = serve(cap, lent_ref, cloud_ref[rows_of(upper_unit, cap), :], weights)

    @pl.when(upper == 0)
    def _():
        crossed_ref[...] = answer
        straight_ref[...] = lower_answer_ref[...]

    @pl.when(upper == 1)
    def _():
        straight_ref[...] = answer
        crossed_ref[...] = lower_answer_ref[...]


def collect_kernel(groups, cap, ids_ref, hot_ref, *refs):
    units = groups // 2
    half = units // 2
    own, far, news, refs = refs[:units], refs[units : 2 * units], refs[2 * units : 2 * units + half], refs[2 * units + half + 1 :]
    out_ref, new_ref, sems = refs
    core, upper_unit = ids_ref[0], ids_ref[4]
    copies = []
    for low, piece in enumerate(news):
        served = lax.bitwise_xor(upper_unit, low)
        copies.append(pltpu.make_async_copy(piece, new_ref.at[rows_of(served, cap), :], sems.at[low]))
        copies[-1].start()
    offset = pl.multiple_of(core * cap, cap)
    total = None
    for du in range(units):
        block = jnp.concatenate([own[du][pl.ds(offset, cap), :], far[du][pl.ds(offset, cap), :]], axis=0)
        part = dot(hot_ref[:, 2 * du * cap : 2 * (du + 1) * cap], block)
        total = part if total is None else total + part
    out_ref[...] = total.astype(jnp.bfloat16)
    for copy in copies:
        copy.wait()


def per_device(state, dest_map, day_mask, cloud, conv_in, conv_mid, conv_out, rad_in, rad_mid, rad_out):
    groups, bands = lax.axis_size("elem"), lax.axis_size("band")
    units, half, away = groups // 2, groups // 4, bands // 2
    cap = cloud.shape[0] // groups
    columns, features = state.shape
    elem = lax.axis_index("elem")
    core, unit = elem % 2, elem // 2
    upper = unit // half
    smem = pl.BlockSpec(memory_space=pltpu.SMEM)
    vmem = pl.BlockSpec(memory_space=pltpu.VMEM)
    hbm = pl.BlockSpec(memory_space=pltpu.HBM)
    params = pltpu.CompilerParams(vmem_limit_bytes=VMEM_BYTES)
    weights = (conv_in, conv_mid, conv_out, rad_in, rad_mid, rad_out)

    def ids_for(low):
        lower_unit = (unit % half) ^ low
        return jnp.stack([core, unit, upper, lower_unit, half + lower_unit]).astype(jnp.int32)

    def like(a):
        return jax.ShapeDtypeStruct(a.shape, a.dtype)

    def swapped(block):
        return moved(block, lambda e, b: (e ^ 1, b))

    ids = ids_for(0)
    dest_table, day_table = dest_map.reshape(columns // 128, 128), day_mask.reshape(columns // 128, 128)
    far_state = swapped(state)
    far_dest, far_day = swapped(dest_table), swapped(day_table)

    packet = jax.ShapeDtypeStruct((2 * cap + FLAG_ROWS, features), jnp.bfloat16)
    order, *packets = pl.pallas_call(
        functools.partial(place_kernel, groups, cap),
        out_shape=[jax.ShapeDtypeStruct((8, columns), jnp.int32)] + [packet] * units,
        in_specs=[smem] + [vmem] * 6,
        out_specs=[vmem] * (units + 1),
        compiler_params=params,
        cost_estimate=work(4),
        name="place_columns",
    )(ids, far_dest, far_day, far_state, dest_table, day_table, state)

    came = [packets[0]] + [None] * (units - 1)
    for low in range(half):
        for du in (half + low, low):
            if du:
                came[du] = moved(packets[du], lambda e, b: (e ^ (2 * du), b))
    lent = []
    for low in range(half):
        leaving = jnp.where(upper == 0, came[half + low], came[low])
        lent.append(moved(leaving, lambda e, b: (e, (b + away) % bands)))

    tile = jax.ShapeDtypeStruct((2 * cap, features), jnp.bfloat16)
    new_tile = jax.ShapeDtypeStruct((2 * cap, cloud.shape[1]), jnp.bfloat16)
    hot_shape = jax.ShapeDtypeStruct((columns, groups * cap), jnp.bfloat16)
    packet_buffer = pltpu.VMEM(packet.shape, jnp.bfloat16)
    answers, lower_answers, news, new_cloud = [None] * units, [], [], None
    for low in range(0, half, 2):
        pick, base = low == 0, () if low == 0 else (new_cloud,)
        outs = pl.pallas_call(
            functools.partial(lower_kernel, groups, cap, len(base), pick),
            out_shape=[tile, tile, like(cloud)] + [hot_shape] * pick,
            in_specs=[smem] + [vmem] * 12 + [hbm] * len(base),
            out_specs=[vmem, vmem, hbm] + [vmem] * pick,
            scratch_shapes=[packet_buffer, pltpu.VMEM((2,) + new_tile.shape, jnp.bfloat16), pltpu.SemaphoreType.DMA((2,))],
            input_output_aliases={13: 2} if base else {},
            compiler_params=params,
            cost_estimate=work(4),
            name="lower_physics",
        )(ids_for(low), order, came[low], came[low + 1], came[half + low], came[half + low + 1], cloud, *weights, *base)
        lower_answers += outs[0:2]
        new_cloud = outs[2]
        if pick:
            hot = outs[3]
    for low in range(half):
        answers[low], answers[half + low], new = pl.pallas_call(
            functools.partial(upper_kernel, cap),
            out_shape=[tile, tile, new_tile],
            in_specs=[smem] + [vmem] * 9,
            out_specs=[vmem] * 3,
            compiler_params=params,
            cost_estimate=work(3),
            name="upper_physics",
        )(ids_for(low), lent[low], lower_answers[low], cloud, *weights)
        news.append(new)

    def home(du):
        def target(e, b):
            to_elem = e ^ (2 * du)
            return to_elem, (b + away) % bands if to_elem >= groups // 2 else b

        return target

    back, far_back = [None] * units, [None] * units
    for low in range(half):
        for du in (half + low, low):
            back[du] = moved(answers[du], home(du))
    for du in range(units):
        far_back[du] = swapped(back[du])

    tendency, new_cloud = pl.pallas_call(
        functools.partial(collect_kernel, groups, cap),
        out_shape=[like(state), like(cloud)],
        in_specs=[smem] + [vmem] * (2 * units + half + 1) + [hbm],
        out_specs=[vmem, hbm],
        scratch_shapes=[pltpu.SemaphoreType.DMA((half,))],
        input_output_aliases={2 + 2 * units + half: 1},
        compiler_params=params,
        cost_estimate=work(3),
        name="collect_columns",
    )(ids, hot, *back, *far_back, *news, new_cloud)
    return (tendency, new_cloud)


def solution(mesh):
    rows = P(("elem", "band"), None)
    return jax.shard_map(
        per_device,
        mesh=mesh,
        in_specs=(rows,) * 4 + (P(),) * 6,
        out_specs=(rows, rows),
        check_vma=False,
    )
```

time: 56.8 us -> 48.2 us (0.85)
  starting transfers between devices: 31.6 us -> 25.2 us
  local copies, waits for them, and re-layouts: 5.61 us -> 1.15 us
  waiting for transfers between devices: 8.01 us -> 11.1 us
  other arithmetic: 0.97 us -> 0.04 us
    ppermute x15 -> x16, starting transfers between devices: 31.6 us -> 25.2 us  [moved(): return lax.ppermute(block, ('elem', 'band'), route)]
    unnamed x24 -> x20, local copies, waits for them, and re-layouts: 5.61 us -> 0.98 us
    ppermute x15 -> x16, waiting for transfers between devices: 8.01 us -> 11.1 us  [moved(): return lax.ppermute(block, ('elem', 'band'), route)]
    concatenate x1 -> x0, other arithmetic: 0.71 us -> none  [per_device(): jnp.concatenate([dest_map.reshape(1, columns), day_mask.reshape(1, column...]
    pallas_call x2 -> x3, Pallas kernels: 5.86 us -> 5.82 us  [the longest x1 3.13 us: per_device(): pl.pallas_call(functools.partial(lower_kernel, groups, cap, len(base), pi...]
  transfers between devices with their start and end apart: 15 -> 16, of which waited for: 5 -> 7; matrix products, arithmetic and copies ran while one was open for 2% -> 0% of each run, Pallas kernels for 10% -> 12%
where the time goes in v2:
time: 48.2 us; the launch traced here: 48 us
  starting transfers between devices  25.2 us (52%)
  waiting for transfers between devices  11.1 us (23%)
  Pallas kernels  9.71 us (20%)
  local copies, waits for them, and re-layouts  1.15 us (2%)
  between operations  0.77 us (2%)
    ppermute x16, starting transfers between devices, moved(): return lax.ppermute(block, ('elem', 'band'), route)  25.2 us
    ppermute x16, waiting for transfers between devices, moved(): return lax.ppermute(block, ('elem', 'band'), route)  11.1 us
    pallas_call x1, Pallas kernels, per_device(): pl.pallas_call(functools.partial(lower_kernel, groups, cap, len(base), pi...  3.13 us
    pallas_call x2, Pallas kernels, per_device(): pl.pallas_call(functools.partial(upper_kernel, cap), out_shape=[tile, til...  2.69 us
    pallas_call x1, Pallas kernels, per_device(): pl.pallas_call(functools.partial(collect_kernel, groups, cap), out_shape=...  2.36 us
    pallas_call x1, Pallas kernels, per_device(): pl.pallas_call(functools.partial(place_kernel, groups, cap), out_shape=[j...  1.53 us
    unnamed x20, local copies, waits for them, and re-layouts  0.98 us
  transfers between devices with their start and end apart: 16, of which 7 were waited for; matrix products, arithmetic and copies ran while one was open for 0% of the time, Pallas kernels for 12%

profile of v2, /device:TPU:5, one launch (start us, length us, event | category | flops | bytes accessed | tf_op | source)
XLA Modules:
  0.0 48.0 jit_solution(11302014469521953068)
XLA Ops:
  0.6 0.0 copy-start.9
  0.6 0.7 %collective-permute-start.2 = (bf16[512,256]{1,0:T(8,128)(2,1)}, bf16[512,256]{1,0:T(8,128)(2,1)S(1)}, u32[]{:S(2)}, u32[]{:S(2)}) collective-permute-start(bf16[512,256]{1,0:T(8,128)(2,1)} %refs_2_.3), channel_id=1, source_target_pairs={{0,4},{1,5},{2,6},{3,7},{4,0},{5,1},{6,2},{7,3},{8,12},{9,13},{10,... | collective-permute-start | bytes 786440 | tf_op jit(solution)/shard_map/ppermute | solution.py:22
  1.4 0.1 collective-permute-start
  1.5 0.0 copy-done.9
  1.5 0.5 %collective-permute-start.1 = (s32[4,128]{1,0:T(4,128)S(1)}, s32[4,128]{1,0:T(4,128)S(1)}, u32[]{:S(2)}, u32[]{:S(2)}) collective-permute-start(s32[4,128]{1,0:T(4,128)S(1)} %bitcast.11), channel_id=1, source_target_pairs={{0,4},{1,5},{2,6},{3,7},{4,0},{5,1},{6,2},{7,3},{8,12},{9,13},{10,... | collective-permute-start | bytes 6152 | tf_op jit(solution)/shard_map/ppermute | solution.py:22
  2.0 0.0 copy-start.8
  2.0 0.1 stack.23.ids_ref
  2.1 0.0 copy-start
  2.1 0.7 %collective-permute-done.far_dest_ref = s32[4,128]{1,0:T(4,128)S(1)} collective-permute-done((s32[4,128]{1,0:T(4,128)}, s32[4,128]{1,0:T(4,128)S(1)}, u32[]{:S(2)}, u32[]{:S(2)}) %collective-permute-start) | collective-permute-done | bytes 2080 | tf_op jit(solution)/shard_map/ppermute | solution.py:22
  2.8 0.1 collective-permute-done.1.far_day_ref
  2.8 0.0 collective-permute-done.2.far_state_ref
  2.8 0.0 copy-done.8
  2.8 0.0 copy-start.4
  2.8 0.9 %copy-done.4 = bf16[512,256]{1,0:T(8,128)(2,1)S(1)} copy-done((bf16[512,256]{1,0:T(8,128)(2,1)S(1)}, bf16[512,256]{1,0:T(8,128)(2,1)}, u32[]{:S(2)}) %copy-start.4) | copy-done | bytes 262168
  3.8 0.0 copy-start.3
  3.8 0.0 copy-start.5
  3.8 0.0 copy-start.6
  3.8 0.0 copy-start.7
  3.8 1.5 %place_columns.1 = (s32[8,512]{1,0:T(8,128)S(1)}, bf16[272,256]{1,0:T(8,128)(2,1)S(1)}, bf16[272,256]{1,0:T(8,128)(2,1)S(1)}, bf16[272,256]{1,0:T(8,128)(2,1)S(1)}, bf16[272,256]{1,0:T(8,128)(2,1)S(1)}) custom-call(s32[5]{0:T(128)S(1)} %stack.23.ids_ref, s32[4,128]{1,0:T(4,128)S(1)} %collective-permute-done.far_dest_ref, ...), custom_call_target="tpu_custom_call" | custom-call | flops 4600000000 | tf_op jit(solution)/shard_map/place_columns/pallas_call | solution.py:221
  5.3 0.1 collective-permute-start.4
  5.4 0.1 stack.50.ids_ref
  5.5 1.4 %collective-permute-start.3 = (bf16[272,256]{1,0:T(8,128)(2,1)S(1)}, bf16[272,256]{1,0:T(8,128)(2,1)S(1)}, u32[]{:S(2)}, u32[]{:S(2)}) collective-permute-start(bf16[272,256]{1,0:T(8,128)(2,1)S(1)} %get-tuple-element.19), channel_id=1, source_target_pairs={{0,8},{1,9},{2,10},{3,11},{4,12},{5,13},{6,14},{7,15},{8,0},{9,1},... | collective-permute-start | bytes 417800 | tf_op jit(solution)/shard_map/ppermute | solution.py:22
  6.9 1.2 %collective-permute-start.5 = (bf16[272,256]{1,0:T(8,128)(2,1)S(1)}, bf16[272,256]{1,0:T(8,128)(2,1)S(1)}, u32[]{:S(2)}, u32[]{:S(2)}) collective-permute-start(bf16[272,256]{1,0:T(8,128)(2,1)S(1)} %get-tuple-element.21), channel_id=1, source_target_pairs={{0,24},{1,25},{2,26},{3,27},{4,28},{5,29},{6,30},{7,31},{8,16},{9,... | collective-permute-start | bytes 417800 | tf_op jit(solution)/shard_map/ppermute | solution.py:22
  8.1 2.2 %collective-permute-done.4.refs_2_ = bf16[272,256]{1,0:T(8,128)(2,1)S(1)} collective-permute-done((bf16[272,256]{1,0:T(8,128)(2,1)S(1)}, bf16[272,256]{1,0:T(8,128)(2,1)S(1)}, u32[]{:S(2)}, u32[]{:S(2)}) %collective-permute-start.4) | collective-permute-done | bytes 139296 | tf_op jit(solution)/shard_map/ppermute | solution.py:22
  10.3 0.0 copy-start.1
  10.3 0.0 copy-start.2
  10.3 2.4 %collective-permute-start.6 = (bf16[272,256]{1,0:T(8,128)(2,1)S(1)}, bf16[272,256]{1,0:T(8,128)(2,1)S(1)}, u32[]{:S(2)}, u32[]{:S(2)}) collective-permute-start(bf16[272,256]{1,0:T(8,128)(2,1)S(1)} %broadcast_select_fusion.1), channel_id=1, source_target_pairs={{0,2},{1,3},{2,0},{3,1},{4,6},{5,7},{6,4},{7,5},{8,10},{9,11},{10,... | collective-permute-start | bytes 417800 | tf_op jit(solution)/shard_map/ppermute | solution.py:22
  12.7 0.0 collective-permute-done.3.refs_1_
  12.7 1.5 %collective-permute-done.5.refs_3_ = bf16[272,256]{1,0:T(8,128)(2,1)S(1)} collective-permute-done((bf16[272,256]{1,0:T(8,128)(2,1)S(1)}, bf16[272,256]{1,0:T(8,128)(2,1)S(1)}, u32[]{:S(2)}, u32[]{:S(2)}) %collective-permute-start.5) | collective-permute-done | bytes 139296 | tf_op jit(solution)/shard_map/ppermute | solution.py:22
  14.3 2.4 %collective-permute-start.8 = (bf16[272,256]{1,0:T(8,128)(2,1)S(1)}, bf16[272,256]{1,0:T(8,128)(2,1)S(1)}, u32[]{:S(2)}, u32[]{:S(2)}) collective-permute-start(bf16[272,256]{1,0:T(8,128)(2,1)S(1)} %broadcast_select_fusion), channel_id=1, source_target_pairs={{0,2},{1,3},{2,0},{3,1},{4,6},{5,7},{6,4},{7,5},{8,10},{9,11},{10,... | collective-permute-start | bytes 417800 | tf_op jit(solution)/shard_map/ppermute | solution.py:22
  16.6 0.0 copy-done
  16.6 0.0 copy-done.3
  16.6 0.0 copy-done.5
  16.6 0.0 copy-done.6
  16.6 0.0 copy-done.7
  16.7 0.0 copy-done.1
  16.7 0.0 copy-done.2
  16.7 3.1 %lower_physics.1 = (bf16[256,256]{1,0:T(8,128)(2,1)S(1)}, bf16[256,256]{1,0:T(8,128)(2,1)S(1)}, bf16[1024,512]{1,0:T(8,128)(2,1)}, bf16[512,1024]{1,0:T(8,128)(2,1)S(1)}) custom-call(s32[5]{0:T(128)S(1)} %stack.23.ids_ref, s32[8,512]{1,0:T(8,128)S(1)} %get-tuple-element.17.order_ref, bf16[272,256]{1,0:T(8,128)(2,1)S(1)} %get-tuple-element.18.refs_0_, ...), custom_call_target="tpu_custom_call" | custom-call | flops 4600000000 | tf_op jit(solution)/shard_map/lower_physics/pallas_call | solution.py:248
  19.8 4.9 %collective-permute-done.8.lent_ref = bf16[272,256]{1,0:T(8,128)(2,1)S(1)} collective-permute-done((bf16[272,256]{1,0:T(8,128)(2,1)S(1)}, bf16[272,256]{1,0:T(8,128)(2,1)S(1)}, u32[]{:S(2)}, u32[]{:S(2)}) %collective-permute-start.8) | collective-permute-done | bytes 139296 | tf_op jit(solution)/shard_map/ppermute | solution.py:22
  24.8 1.3 %upper_physics.3 = (bf16[256,256]{1,0:T(8,128)(2,1)S(1)}, bf16[256,256]{1,0:T(8,128)(2,1)S(1)}, bf16[256,512]{1,0:T(8,128)(2,1)S(1)}) custom-call(s32[5]{0:T(128)S(1)} %stack.50.ids_ref, bf16[272,256]{1,0:T(8,128)(2,1)S(1)} %collective-permute-done.8.lent_ref, bf16[256,256]{1,0:T(8,128)(2,1)S(1)} %get-tuple-element.25.lower_answer_ref, ...), custom_call_target="tpu_custom_call" | custom-call | flops 3449999872 | tf_op jit(solution)/shard_map/upper_physics/pallas_call | solution.py:264
  26.1 0.3 collective-permute-start.9
  26.4 1.4 %collective-permute-start.11 = (bf16[256,256]{1,0:T(8,128)(2,1)S(1)}, bf16[256,256]{1,0:T(8,128)(2,1)S(1)}, u32[]{:S(2)}, u32[]{:S(2)}) collective-permute-start(bf16[256,256]{1,0:T(8,128)(2,1)S(1)} %get-tuple-element.28), channel_id=1, source_target_pairs={{0,26},{1,27},{2,24},{3,25},{4,30},{5,31},{6,28},{7,29},{8,18},{9,... | collective-permute-start | bytes 393224 | tf_op jit(solution)/shard_map/ppermute | solution.py:22
  27.8 0.0 collective-permute-done.6.lent_ref
  27.8 1.3 %upper_physics.2 = (bf16[256,256]{1,0:T(8,128)(2,1)S(1)}, bf16[256,256]{1,0:T(8,128)(2,1)S(1)}, bf16[256,512]{1,0:T(8,128)(2,1)S(1)}) custom-call(s32[5]{0:T(128)S(1)} %stack.23.ids_ref, bf16[272,256]{1,0:T(8,128)(2,1)S(1)} %collective-permute-done.6.lent_ref, bf16[256,256]{1,0:T(8,128)(2,1)S(1)} %get-tuple-element.23.lower_answer_ref, ...), custom_call_target="tpu_custom_call" | custom-call | flops 3449999872 | tf_op jit(solution)/shard_map/upper_physics/pallas_call | solution.py:264
  29.2 3.6 %collective-permute-start.7 = (bf16[256,256]{1,0:T(8,128)(2,1)S(1)}, bf16[256,256]{1,0:T(8,128)(2,1)S(1)}, u32[]{:S(2)}, u32[]{:S(2)}) collective-permute-start(bf16[256,256]{1,0:T(8,128)(2,1)S(1)} %get-tuple-element.24), channel_id=1, source_target_pairs={{0,0},{1,1},{2,2},{3,3},{4,4},{5,5},{6,6},{7,7},{8,8},{9,9},{10,10... | collective-permute-start | bytes 393224 | tf_op jit(solution)/shard_map/ppermute | solution.py:22
  32.7 0.1 collective-permute-start.10
  32.8 0.0 collective-permute-done.9.refs_1_
  32.8 5.7 %collective-permute-start.13 = (bf16[256,256]{1,0:T(8,128)(2,1)S(1)}, bf16[256,256]{1,0:T(8,128)(2,1)S(1)}, u32[]{:S(2)}, u32[]{:S(2)}) collective-permute-start(bf16[256,256]{1,0:T(8,128)(2,1)S(1)} %collective-permute-done.9.refs_1_), channel_id=1, source_target_pairs={{0,4},{1,5},{2,6},{3,7},{4,0},{5,1},{6,2},{7,3},{8,12},{9,13},{10,... | collective-permute-start | bytes 393224 | tf_op jit(solution)/shard_map/ppermute | solution.py:22
  38.5 0.0 collective-permute-done.11.refs_3_
  38.5 0.0 collective-permute-start.15
  38.5 0.0 collective-permute-done.7.refs_0_
  38.5 3.8 %collective-permute-start.12 = (bf16[256,256]{1,0:T(8,128)(2,1)S(1)}, bf16[256,256]{1,0:T(8,128)(2,1)S(1)}, u32[]{:S(2)}, u32[]{:S(2)}) collective-permute-start(bf16[256,256]{1,0:T(8,128)(2,1)S(1)} %collective-permute-done.7.refs_0_), channel_id=1, source_target_pairs={{0,4},{1,5},{2,6},{3,7},{4,0},{5,1},{6,2},{7,3},{8,12},{9,13},{10,... | collective-permute-start | bytes 393224 | tf_op jit(solution)/shard_map/ppermute | solution.py:22
  42.3 0.7 %collective-permute-done.10.refs_2_ = bf16[256,256]{1,0:T(8,128)(2,1)S(1)} collective-permute-done((bf16[256,256]{1,0:T(8,128)(2,1)S(1)}, bf16[256,256]{1,0:T(8,128)(2,1)S(1)}, u32[]{:S(2)}, u32[]{:S(2)}) %collective-permute-start.10) | collective-permute-done | bytes 131104 | tf_op jit(solution)/shard_map/ppermute | solution.py:22
  43.1 1.6 %collective-permute-start.14 = (bf16[256,256]{1,0:T(8,128)(2,1)S(1)}, bf16[256,256]{1,0:T(8,128)(2,1)S(1)}, u32[]{:S(2)}, u32[]{:S(2)}) collective-permute-start(bf16[256,256]{1,0:T(8,128)(2,1)S(1)} %collective-permute-done.10.refs_2_), channel_id=1, source_target_pairs={{0,4},{1,5},{2,6},{3,7},{4,0},{5,1},{6,2},{7,3},{8,12},{9,13},{10,... | collective-permute-start | bytes 393224 | tf_op jit(solution)/shard_map/ppermute | solution.py:22
  44.7 0.0 collective-permute-done.13.refs_5_
  44.7 0.0 collective-permute-done.15.refs_7_
  44.7 0.0 collective-permute-done.12.refs_4_
  44.7 1.0 %collective-permute-done.14.refs_6_ = bf16[256,256]{1,0:T(8,128)(2,1)S(1)} collective-permute-done((bf16[256,256]{1,0:T(8,128)(2,1)S(1)}, bf16[256,256]{1,0:T(8,128)(2,1)S(1)}, u32[]{:S(2)}, u32[]{:S(2)}) %collective-permute-start.14) | collective-permute-done | bytes 131104 | tf_op jit(solution)/shard_map/ppermute | solution.py:22
  45.7 2.4 %collect_columns.1 = (bf16[512,256]{1,0:T(8,128)(2,1)}, bf16[1024,512]{1,0:T(8,128)(2,1)}) custom-call(s32[5]{0:T(128)S(1)} %stack.23.ids_ref, bf16[512,1024]{1,0:T(8,128)(2,1)S(1)} %get-tuple-element.22.hot_ref, bf16[256,256]{1,0:T(8,128)(2,1)S(1)} %collective-permute-done.7.refs_0_, ...), custom_call_target="tpu_custom_call", output_to_operand_aliasing={{1}: (12, {})} | custom-call | flops 3449999872 | tf_op jit(solution)/shard_map/collect_columns/pallas_call | solution.py:289
  (2 shorter events, 0.0 us)
Async XLA Ops:
  0.6 0.8 %copy-start.9 = (s32[512,1]{0,1:T(1,128)S(1)}, s32[512,1]{0,1:T(1,128)}, u32[]{:S(2)}) copy-start(s32[512,1]{0,1:T(1,128)} %param.12) | copy-start | bytes 6148
  0.6 2.2 %collective-permute-start.2 = (bf16[512,256]{1,0:T(8,128)(2,1)}, bf16[512,256]{1,0:T(8,128)(2,1)S(1)}, u32[]{:S(2)}, u32[]{:S(2)}) collective-permute-start(bf16[512,256]{1,0:T(8,128)(2,1)} %refs_2_.3), channel_id=1, source_target_pairs={{0,4},{1,5},{2,6},{3,7},{4,0},{5,1},{6,2},{7,3},{8,12},{9,13},{10,... | collective-permute-start | bytes 786440 | tf_op jit(solution)/shard_map/ppermute | solution.py:22
  1.4 1.4 %collective-permute-start = (s32[4,128]{1,0:T(4,128)}, s32[4,128]{1,0:T(4,128)S(1)}, u32[]{:S(2)}, u32[]{:S(2)}) collective-permute-start(s32[4,128]{1,0:T(4,128)} %bitcast.9), channel_id=1, source_target_pairs={{0,4},{1,5},{2,6},{3,7},{4,0},{5,1},{6,2},{7,3},{8,12},{9,13},{10,... | collective-permute-start | bytes 6152 | tf_op jit(solution)/shard_map/ppermute | solution.py:22
  1.5 1.3 %collective-permute-start.1 = (s32[4,128]{1,0:T(4,128)S(1)}, s32[4,128]{1,0:T(4,128)S(1)}, u32[]{:S(2)}, u32[]{:S(2)}) collective-permute-start(s32[4,128]{1,0:T(4,128)S(1)} %bitcast.11), channel_id=1, source_target_pairs={{0,4},{1,5},{2,6},{3,7},{4,0},{5,1},{6,2},{7,3},{8,12},{9,13},{10,... | collective-permute-start | bytes 6152 | tf_op jit(solution)/shard_map/ppermute | solution.py:22
  2.0 0.8 %copy-start.8 = (s32[512,1]{0,1:T(1,128)S(1)}, s32[512,1]{0,1:T(1,128)}, u32[]{:S(2)}) copy-start(s32[512,1]{0,1:T(1,128)} %param.11) | copy-start | bytes 6148
  2.1 14.6 %copy-start = (bf16[1024,512]{1,0:T(8,128)(2,1)S(1)}, bf16[1024,512]{1,0:T(8,128)(2,1)}, u32[]{:S(2)}) copy-start(bf16[1024,512]{1,0:T(8,128)(2,1)} %cloud_ref.3) | copy-start | bytes 3145732
  2.8 1.0 %copy-start.4 = (bf16[512,256]{1,0:T(8,128)(2,1)S(1)}, bf16[512,256]{1,0:T(8,128)(2,1)}, u32[]{:S(2)}) copy-start(bf16[512,256]{1,0:T(8,128)(2,1)} %refs_2_.3) | copy-start | bytes 786436
  3.8 12.9 %copy-start.3 = (bf16[768,256]{1,0:T(8,128)(2,1)S(1)}, bf16[768,256]{1,0:T(8,128)(2,1)}, u32[]{:S(2)}) copy-start(bf16[768,256]{1,0:T(8,128)(2,1)} %refs_3_.3) | copy-start | bytes 1179652
  3.8 12.9 %copy-start.5 = (bf16[256,256]{1,0:T(8,128)(2,1)S(1)}, bf16[256,256]{1,0:T(8,128)(2,1)}, u32[]{:S(2)}) copy-start(bf16[256,256]{1,0:T(8,128)(2,1)} %refs_1_.3) | copy-start | bytes 393220
  3.8 12.9 %copy-start.6 = (bf16[256,256]{1,0:T(8,128)(2,1)S(1)}, bf16[256,256]{1,0:T(8,128)(2,1)}, u32[]{:S(2)}) copy-start(bf16[256,256]{1,0:T(8,128)(2,1)} %refs_4_.5) | copy-start | bytes 393220
  3.8 12.9 %copy-start.7 = (bf16[256,128]{1,0:T(8,128)(2,1)S(1)}, bf16[256,128]{1,0:T(8,128)(2,1)}, u32[]{:S(2)}) copy-start(bf16[256,128]{1,0:T(8,128)(2,1)} %refs_5_.5) | copy-start | bytes 196612
  5.3 5.0 %collective-permute-start.4 = (bf16[272,256]{1,0:T(8,128)(2,1)S(1)}, bf16[272,256]{1,0:T(8,128)(2,1)S(1)}, u32[]{:S(2)}, u32[]{:S(2)}) collective-permute-start(bf16[272,256]{1,0:T(8,128)(2,1)S(1)} %get-tuple-element.20), channel_id=1, source_target_pairs={{0,16},{1,17},{2,18},{3,19},{4,20},{5,21},{6,22},{7,23},{8,24},{9,... | collective-permute-start | bytes 417800 | tf_op jit(solution)/shard_map/ppermute | solution.py:22
  5.5 7.2 %collective-permute-start.3 = (bf16[272,256]{1,0:T(8,128)(2,1)S(1)}, bf16[272,256]{1,0:T(8,128)(2,1)S(1)}, u32[]{:S(2)}, u32[]{:S(2)}) collective-permute-start(bf16[272,256]{1,0:T(8,128)(2,1)S(1)} %get-tuple-element.19), channel_id=1, source_target_pairs={{0,8},{1,9},{2,10},{3,11},{4,12},{5,13},{6,14},{7,15},{8,0},{9,1},... | collective-permute-start | bytes 417800 | tf_op jit(solution)/shard_map/ppermute | solution.py:22
  6.9 7.3 %collective-permute-start.5 = (bf16[272,256]{1,0:T(8,128)(2,1)S(1)}, bf16[272,256]{1,0:T(8,128)(2,1)S(1)}, u32[]{:S(2)}, u32[]{:S(2)}) collective-permute-start(bf16[272,256]{1,0:T(8,128)(2,1)S(1)} %get-tuple-element.21), channel_id=1, source_target_pairs={{0,24},{1,25},{2,26},{3,27},{4,28},{5,29},{6,30},{7,31},{8,16},{9,... | collective-permute-start | bytes 417800 | tf_op jit(solution)/shard_map/ppermute | solution.py:22
  10.3 6.3 %copy-start.1 = (bf16[768,256]{1,0:T(8,128)(2,1)S(1)}, bf16[768,256]{1,0:T(8,128)(2,1)}, u32[]{:S(2)}) copy-start(bf16[768,256]{1,0:T(8,128)(2,1)} %refs_0_.3) | copy-start | bytes 1179652
  10.3 6.4 %copy-start.2 = (bf16[256,768]{1,0:T(8,128)(2,1)S(1)}, bf16[256,768]{1,0:T(8,128)(2,1)}, u32[]{:S(2)}) copy-start(bf16[256,768]{1,0:T(8,128)(2,1)} %refs_2_.5) | copy-start | bytes 1179652
  10.3 17.5 %collective-permute-start.6 = (bf16[272,256]{1,0:T(8,128)(2,1)S(1)}, bf16[272,256]{1,0:T(8,128)(2,1)S(1)}, u32[]{:S(2)}, u32[]{:S(2)}) collective-permute-start(bf16[272,256]{1,0:T(8,128)(2,1)S(1)} %broadcast_select_fusion.1), channel_id=1, source_target_pairs={{0,2},{1,3},{2,0},{3,1},{4,6},{5,7},{6,4},{7,5},{8,10},{9,11},{10,... | collective-permute-start | bytes 417800 | tf_op jit(solution)/shard_map/ppermute | solution.py:22
  14.3 10.5 %collective-permute-start.8 = (bf16[272,256]{1,0:T(8,128)(2,1)S(1)}, bf16[272,256]{1,0:T(8,128)(2,1)S(1)}, u32[]{:S(2)}, u32[]{:S(2)}) collective-permute-start(bf16[272,256]{1,0:T(8,128)(2,1)S(1)} %broadcast_select_fusion), channel_id=1, source_target_pairs={{0,2},{1,3},{2,0},{3,1},{4,6},{5,7},{6,4},{7,5},{8,10},{9,11},{10,... | collective-permute-start | bytes 417800 | tf_op jit(solution)/shard_map/ppermute | solution.py:22
  26.1 6.7 %collective-permute-start.9 = (bf16[256,256]{1,0:T(8,128)(2,1)S(1)}, bf16[256,256]{1,0:T(8,128)(2,1)S(1)}, u32[]{:S(2)}, u32[]{:S(2)}) collective-permute-start(bf16[256,256]{1,0:T(8,128)(2,1)S(1)} %get-tuple-element.26), channel_id=1, source_target_pairs={{0,8},{1,9},{2,10},{3,11},{4,12},{5,13},{6,14},{7,15},{8,0},{9,1},... | collective-permute-start | bytes 393224 | tf_op jit(solution)/shard_map/ppermute | solution.py:22
  26.4 12.2 %collective-permute-start.11 = (bf16[256,256]{1,0:T(8,128)(2,1)S(1)}, bf16[256,256]{1,0:T(8,128)(2,1)S(1)}, u32[]{:S(2)}, u32[]{:S(2)}) collective-permute-start(bf16[256,256]{1,0:T(8,128)(2,1)S(1)} %get-tuple-element.28), channel_id=1, source_target_pairs={{0,26},{1,27},{2,24},{3,25},{4,30},{5,31},{6,28},{7,29},{8,18},{9,... | collective-permute-start | bytes 393224 | tf_op jit(solution)/shard_map/ppermute | solution.py:22
  29.2 9.4 %collective-permute-start.7 = (bf16[256,256]{1,0:T(8,128)(2,1)S(1)}, bf16[256,256]{1,0:T(8,128)(2,1)S(1)}, u32[]{:S(2)}, u32[]{:S(2)}) collective-permute-start(bf16[256,256]{1,0:T(8,128)(2,1)S(1)} %get-tuple-element.24), channel_id=1, source_target_pairs={{0,0},{1,1},{2,2},{3,3},{4,4},{5,5},{6,6},{7,7},{8,8},{9,9},{10,10... | collective-permute-start | bytes 393224 | tf_op jit(solution)/shard_map/ppermute | solution.py:22
  32.7 10.3 %collective-permute-start.10 = (bf16[256,256]{1,0:T(8,128)(2,1)S(1)}, bf16[256,256]{1,0:T(8,128)(2,1)S(1)}, u32[]{:S(2)}, u32[]{:S(2)}) collective-permute-start(bf16[256,256]{1,0:T(8,128)(2,1)S(1)} %get-tuple-element.27), channel_id=1, source_target_pairs={{0,18},{1,19},{2,16},{3,17},{4,22},{5,23},{6,20},{7,21},{8,26},{9,... | collective-permute-start | bytes 393224 | tf_op jit(solution)/shard_map/ppermute | solution.py:22
  32.8 11.8 %collective-permute-start.13 = (bf16[256,256]{1,0:T(8,128)(2,1)S(1)}, bf16[256,256]{1,0:T(8,128)(2,1)S(1)}, u32[]{:S(2)}, u32[]{:S(2)}) collective-permute-start(bf16[256,256]{1,0:T(8,128)(2,1)S(1)} %collective-permute-done.9.refs_1_), channel_id=1, source_target_pairs={{0,4},{1,5},{2,6},{3,7},{4,0},{5,1},{6,2},{7,3},{8,12},{9,13},{10,... | collective-permute-start | bytes 393224 | tf_op jit(solution)/shard_map/ppermute | solution.py:22
  38.5 6.1 %collective-permute-start.15 = (bf16[256,256]{1,0:T(8,128)(2,1)S(1)}, bf16[256,256]{1,0:T(8,128)(2,1)S(1)}, u32[]{:S(2)}, u32[]{:S(2)}) collective-permute-start(bf16[256,256]{1,0:T(8,128)(2,1)S(1)} %collective-permute-done.11.refs_3_), channel_id=1, source_target_pairs={{0,4},{1,5},{2,6},{3,7},{4,0},{5,1},{6,2},{7,3},{8,12},{9,13},{10,... | collective-permute-start | bytes 393224 | tf_op jit(solution)/shard_map/ppermute | solution.py:22
  38.5 6.1 %collective-permute-start.12 = (bf16[256,256]{1,0:T(8,128)(2,1)S(1)}, bf16[256,256]{1,0:T(8,128)(2,1)S(1)}, u32[]{:S(2)}, u32[]{:S(2)}) collective-permute-start(bf16[256,256]{1,0:T(8,128)(2,1)S(1)} %collective-permute-done.7.refs_0_), channel_id=1, source_target_pairs={{0,4},{1,5},{2,6},{3,7},{4,0},{5,1},{6,2},{7,3},{8,12},{9,13},{10,... | collective-permute-start | bytes 393224 | tf_op jit(solution)/shard_map/ppermute | solution.py:22
  43.1 2.6 %collective-permute-start.14 = (bf16[256,256]{1,0:T(8,128)(2,1)S(1)}, bf16[256,256]{1,0:T(8,128)(2,1)S(1)}, u32[]{:S(2)}, u32[]{:S(2)}) collective-permute-start(bf16[256,256]{1,0:T(8,128)(2,1)S(1)} %collective-permute-done.10.refs_2_), channel_id=1, source_target_pairs={{0,4},{1,5},{2,6},{3,7},{4,0},{5,1},{6,2},{7,3},{8,12},{9,13},{10,... | collective-permute-start | bytes 393224 | tf_op jit(solution)/shard_map/ppermute | solution.py:22

commit v3 on v2

--- a/solution.py
+++ b/solution.py
@@ -51,22 +51,25 @@
     return jnp.concatenate(parts, axis=1).astype(jnp.int32)
 
 
-def place_kernel(groups, cap, ids_ref, far_dest_ref, far_day_ref, far_state_ref, *refs):
+def targets_kernel(groups, cap, ids_ref, dest_ref, day_ref, far_dest_ref, far_day_ref, out_ref):
+    core, unit = ids_ref[0], ids_ref[1]
+    rows = []
+    for dest_table, day_table in ((dest_ref, day_ref), (far_dest_ref, far_day_ref)):
+        dest = as_row(dest_table[...])
+        order = orders(dest, groups)
+        step = lax.bitwise_xor(lax.shift_right_logical(dest, 1), jnp.full_like(dest, unit))
+        rows += [jnp.where(lax.bitwise_and(dest, 1) == core, step * cap + order, -1), as_row(day_table[...]), dest, order]
+    out_ref[...] = jnp.concatenate(rows, axis=0)
+
+
+def place_kernel(groups, cap, ids_ref, targets_ref, state_ref, far_state_ref, *out_refs):
+    core = ids_ref[0]
     units = groups // 2
-    dest_ref, day_ref, state_ref, order_ref, *out_refs = refs
-    core, unit = ids_ref[0], ids_ref[1]
     columns, features = state_ref.shape
     flags = []
-    for far, (dest_table, day_table, rows) in enumerate(
-        ((dest_ref, day_ref, state_ref), (far_dest_ref, far_day_ref, far_state_ref))
-    ):
+    for far, rows in enumerate((state_ref, far_state_ref)):
         source_core = core if far == 0 else 1 - core
-        dest, day = as_row(dest_table[...]), as_row(day_table[...])
-        order = orders(dest, groups)
-        if far == 0:
-            order_ref[...] = jnp.concatenate([dest, order] + [jnp.zeros_like(dest)] * 6, axis=0)
-        step = lax.bitwise_xor(lax.shift_right_logical(dest, 1), jnp.full_like(dest, unit))
-        row = jnp.where(lax.bitwise_and(dest, 1) == core, step * cap + order, -1)
+        row, day = targets_ref[4 * far : 4 * far + 1, :], targets_ref[4 * far + 1 : 4 * far + 2, :]
         hot = (lax.broadcasted_iota(jnp.int32, (units * cap, columns), 0) == row).astype(jnp.bfloat16)
         sun = jnp.broadcast_to(day.astype(jnp.float32), (FLAG_ROWS, columns)).astype(jnp.bfloat16)
         flags.append(
@@ -118,7 +121,7 @@
     return pl.ds(pl.multiple_of(unit * 2 * cap, 2 * cap), 2 * cap)
 
 
-def lower_kernel(groups, cap, base, pick, ids_ref, order_ref, *refs):
+def lower_kernel(groups, cap, base, pick, ids_ref, targets_ref, *refs):
     near, cross, cloud_ref, weights, refs = refs[0:2], refs[2:4], refs[4], refs[5:11], refs[11 + base :]
     answers, new_ref, refs = refs[0:2], refs[2], refs[3:]
     core, unit, upper, lower_unit = ids_ref[0], ids_ref[1], ids_ref[2], ids_ref[3]
@@ -140,8 +143,8 @@
         copies[-1].start()
     if pick:
         hot_ref = refs[0]
-        table = jnp.transpose(order_ref[...].astype(jnp.float32)).astype(jnp.int32)
-        dest, order = table[:, 0:1], table[:, 1:2]
+        table = jnp.transpose(targets_ref[...].astype(jnp.float32)).astype(jnp.int32)
+        dest, order = table[:, 2:3], table[:, 3:4]
         step = lax.bitwise_xor(lax.shift_right_logical(dest, 1), jnp.full_like(dest, unit))
         side = jnp.where(lax.bitwise_and(dest, 1) == core, 0, 1)
         row = (step * 2 + side) * cap + order
@@ -166,26 +169,27 @@
         crossed_ref[...] = lower_answer_ref[...]
 
 
+def store_kernel(cap, ids_ref, *refs):
+    news, (new_ref, sems) = refs[:-3], refs[-2:]
+    copies = []
+    for low, piece in enumerate(news):
+        served = lax.bitwise_xor(ids_ref[4], low)
+        copies.append(pltpu.make_async_copy(piece, new_ref.at[rows_of(served, cap), :], sems.at[low]))
+        copies[-1].start()
+    for copy in copies:
+        copy.wait()
+
+
 def collect_kernel(groups, cap, ids_ref, hot_ref, *refs):
     units = groups // 2
-    half = units // 2
-    own, far, news, refs = refs[:units], refs[units : 2 * units], refs[2 * units : 2 * units + half], refs[2 * units + half + 1 :]
-    out_ref, new_ref, sems = refs
-    core, upper_unit = ids_ref[0], ids_ref[4]
-    copies = []
-    for low, piece in enumerate(news):
-        served = lax.bitwise_xor(upper_unit, low)
-        copies.append(pltpu.make_async_copy(piece, new_ref.at[rows_of(served, cap), :], sems.at[low]))
-        copies[-1].start()
-    offset = pl.multiple_of(core * cap, cap)
+    own, far, out_ref = refs[:units], refs[units : 2 * units], refs[2 * units]
+    offset = pl.multiple_of(ids_ref[0] * cap, cap)
     total = None
     for du in range(units):
         block = jnp.concatenate([own[du][pl.ds(offset, cap), :], far[du][pl.ds(offset, cap), :]], axis=0)
         part = dot(hot_ref[:, 2 * du * cap : 2 * (du + 1) * cap], block)
         total = part if total is None else total + part
     out_ref[...] = total.astype(jnp.bfloat16)
-    for copy in copies:
-        copy.wait()
 
 
 def per_device(state, dest_map, day_mask, cloud, conv_in, conv_mid, conv_out, rad_in, rad_mid, rad_out):
@@ -218,15 +222,24 @@
     far_dest, far_day = swapped(dest_table), swapped(day_table)
 
     packet = jax.ShapeDtypeStruct((2 * cap + FLAG_ROWS, features), jnp.bfloat16)
-    order, *packets = pl.pallas_call(
+    targets = pl.pallas_call(
+        functools.partial(targets_kernel, groups, cap),
+        out_shape=jax.ShapeDtypeStruct((8, columns), jnp.int32),
+        in_specs=[smem] + [vmem] * 4,
+        out_specs=vmem,
+        compiler_params=params,
+        cost_estimate=work(4),
+        name="column_targets",
+    )(ids, dest_table, day_table, far_dest, far_day)
+    packets = pl.pallas_call(
         functools.partial(place_kernel, groups, cap),
-        out_shape=[jax.ShapeDtypeStruct((8, columns), jnp.int32)] + [packet] * units,
-        in_specs=[smem] + [vmem] * 6,
-        out_specs=[vmem] * (units + 1),
+        out_shape=[packet] * units,
+        in_specs=[smem] + [vmem] * 3,
+        out_specs=[vmem] * units,
         compiler_params=params,
         cost_estimate=work(4),
         name="place_columns",
-    )(ids, far_dest, far_day, far_state, dest_table, day_table, state)
+    )(ids, targets, state, far_state)
 
     came = [packets[0]] + [None] * (units - 1)
     for low in range(half):
@@ -255,7 +268,7 @@
             compiler_params=params,
             cost_estimate=work(4),
             name="lower_physics",
-        )(ids_for(low), order, came[low], came[low + 1], came[half + low], came[half + low + 1], cloud, *weights, *base)
+        )(ids_for(low), targets, came[low], came[low + 1], came[half + low], came[half + low + 1], cloud, *weights, *base)
         lower_answers += outs[0:2]
         new_cloud = outs[2]
         if pick:
@@ -279,24 +292,34 @@
 
         return target
 
-    back, far_back = [None] * units, [None] * units
-    for low in range(half):
-        for du in (half + low, low):
-            back[du] = moved(answers[du], home(du))
-    for du in range(units):
+    back = [None] * units
+    sequence = [*range(half, units), *range(half)]
+    for du in sequence:
+        back[du] = moved(answers[du], home(du))
+    new_cloud = pl.pallas_call(
+        functools.partial(store_kernel, cap),
+        out_shape=like(cloud),
+        in_specs=[smem] + [vmem] * half + [hbm],
+        out_specs=hbm,
+        scratch_shapes=[pltpu.SemaphoreType.DMA((half,))],
+        input_output_aliases={1 + half: 0},
+        compiler_params=params,
+        cost_estimate=work(1),
+        name="store_cloud",
+    )(ids, *news, new_cloud)
+    back[half], new_cloud = lax.optimization_barrier((back[half], new_cloud))
+    far_back = [None] * units
+    for du in sequence:
         far_back[du] = swapped(back[du])
-
-    tendency, new_cloud = pl.pallas_call(
+    tendency = pl.pallas_call(
         functools.partial(collect_kernel, groups, cap),
-        out_shape=[like(state), like(cloud)],
-        in_specs=[smem] + [vmem] * (2 * units + half + 1) + [hbm],
-        out_specs=[vmem, hbm],
-        scratch_shapes=[pltpu.SemaphoreType.DMA((half,))],
-        input_output_aliases={2 + 2 * units + half: 1},
+        out_shape=like(state),
+        in_specs=[smem] + [vmem] * (2 * units + 1),
+        out_specs=vmem,
         compiler_params=params,
         cost_estimate=work(3),
         name="collect_columns",
-    )(ids, hot, *back, *far_back, *news, new_cloud)
+    )(ids, hot, *back, *far_back)
     return (tendency, new_cloud)
 
 

time: 48.2 us -> 46.2 us (0.959)
  waiting for transfers between devices: 11.1 us -> 7.24 us
  starting transfers between devices: 25.2 us -> 26.9 us
  Pallas kernels: 9.71 us -> 10.8 us
  local copies, waits for them, and re-layouts: 1.15 us -> 0.21 us
    ppermute x16, waiting for transfers between devices: 11.1 us -> 7.24 us  [moved(): return lax.ppermute(block, ('elem', 'band'), route)]
    pallas_call x1 -> x3, Pallas kernels: 1.53 us -> 3.33 us  [the longest x1 1.35 us: per_device(): pl.pallas_call(functools.partial(store_kernel, cap), out_shape=like(cloud...]
    ppermute x16, starting transfers between devices: 25.2 us -> 26.9 us  [moved(): return lax.ppermute(block, ('elem', 'band'), route)]
    unnamed x20, local copies, waits for them, and re-layouts: 0.98 us -> 0.04 us
    pallas_call x1, Pallas kernels: 2.36 us -> 1.69 us  [per_device(): pl.pallas_call(functools.partial(collect_kernel, groups, cap), out_shape=...]
  transfers between devices with their start and end apart: 16 -> 16, of which waited for: 7 -> 7; matrix products, arithmetic and copies ran while one was open for 0% -> 0% of each run, Pallas kernels for 12% -> 17%
where the time goes in v3:
time: 46.2 us; the launch traced here: 46 us
  starting transfers between devices  26.9 us (58%)
  Pallas kernels  10.8 us (23%)
  waiting for transfers between devices  7.24 us (16%)
  between operations  0.81 us (2%)
    ppermute x16, starting transfers between devices, moved(): return lax.ppermute(block, ('elem', 'band'), route)  26.9 us
    ppermute x16, waiting for transfers between devices, moved(): return lax.ppermute(block, ('elem', 'band'), route)  7.24 us
    pallas_call x1, Pallas kernels, per_device(): pl.pallas_call(functools.partial(lower_kernel, groups, cap, len(base), pi...  3.11 us
    pallas_call x2, Pallas kernels, per_device(): pl.pallas_call(functools.partial(upper_kernel, cap), out_shape=[tile, til...  2.7 us
    pallas_call x1, Pallas kernels, per_device(): pl.pallas_call(functools.partial(collect_kernel, groups, cap), out_shape=...  1.69 us
    pallas_call x1, Pallas kernels, per_device(): pl.pallas_call(functools.partial(store_kernel, cap), out_shape=like(cloud...  1.35 us
    pallas_call x1, Pallas kernels, per_device(): pl.pallas_call(functools.partial(place_kernel, groups, cap), out_shape=[p...  1.24 us
  transfers between devices with their start and end apart: 16, of which 7 were waited for; matrix products, arithmetic and copies ran while one was open for 0% of the time, Pallas kernels for 17%

profile of v3, /device:TPU:5, one launch (start us, length us, event | category | flops | bytes accessed | tf_op | source)
XLA Modules:
  0.0 46.0 jit_solution(4268998452501965815)
XLA Ops:
  0.6 0.0 copy-start.9
  0.6 0.7 %collective-permute-start = (s32[4,128]{1,0:T(4,128)}, s32[4,128]{1,0:T(4,128)S(1)}, u32[]{:S(2)}, u32[]{:S(2)}) collective-permute-start(s32[4,128]{1,0:T(4,128)} %bitcast.9), channel_id=1, source_target_pairs={{0,4},{1,5},{2,6},{3,7},{4,0},{5,1},{6,2},{7,3},{8,12},{9,13},{10,... | collective-permute-start | bytes 6152 | tf_op jit(solution)/shard_map/ppermute | solution.py:22
  1.4 0.0 copy-done.9
  1.4 0.6 %collective-permute-start.1 = (s32[4,128]{1,0:T(4,128)S(1)}, s32[4,128]{1,0:T(4,128)S(1)}, u32[]{:S(2)}, u32[]{:S(2)}) collective-permute-start(s32[4,128]{1,0:T(4,128)S(1)} %bitcast.11), channel_id=1, source_target_pairs={{0,4},{1,5},{2,6},{3,7},{4,0},{5,1},{6,2},{7,3},{8,12},{9,13},{10,... | collective-permute-start | bytes 6152 | tf_op jit(solution)/shard_map/ppermute | solution.py:22
  2.0 0.0 collective-permute-start.2
  2.0 0.0 copy-start.8
  2.0 0.1 stack.23.ids_ref
  2.1 0.0 copy-start.4
  2.1 0.3 collective-permute-done.far_dest_ref
  2.4 0.4 collective-permute-done.1.far_day_ref
  2.8 0.0 copy-done.8
  2.8 0.7 %column_targets.1.targets_ref = s32[8,512]{1,0:T(8,128)S(1)} custom-call(s32[5]{0:T(128)S(1)} %stack.23.ids_ref, s32[4,128]{1,0:T(4,128)S(1)} %bitcast.10, s32[4,128]{1,0:T(4,128)S(1)} %bitcast.12, s32[4,128]{1,0:T(4,128)S(1)} %collective-permute-done.far_dest_ref, s32[4,128]{1,0:T(4,128)S(1)} %collective-permute-done.1.far_day_ref), custom_call_target="tpu_custom_call" | custom-call | flops 4600000000 | tf_op jit(solution)/shard_map/column_targets/pallas_call | solution.py:225
  3.6 0.0 copy-start
  3.6 0.2 collective-permute-done.2.far_state_ref
  3.7 0.0 copy-done.4
  3.7 0.0 copy-start.3
  3.7 0.0 copy-start.5
  3.7 0.0 copy-start.6
  3.7 0.0 copy-start.7
  3.8 1.2 %place_columns.1 = (bf16[272,256]{1,0:T(8,128)(2,1)S(1)}, bf16[272,256]{1,0:T(8,128)(2,1)S(1)}, bf16[272,256]{1,0:T(8,128)(2,1)S(1)}, bf16[272,256]{1,0:T(8,128)(2,1)S(1)}) custom-call(s32[5]{0:T(128)S(1)} %stack.23.ids_ref, s32[8,512]{1,0:T(8,128)S(1)} %column_targets.1.targets_ref, bf16[512,256]{1,0:T(8,128)(2,1)S(1)} %copy-done.4, ...), custom_call_target="tpu_custom_call" | custom-call | flops 4600000000 | tf_op jit(solution)/shard_map/place_columns/pallas_call | solution.py:234
  5.0 0.1 collective-permute-start.4
  5.1 0.1 stack.50.ids_ref
  5.2 1.4 %collective-permute-start.3 = (bf16[272,256]{1,0:T(8,128)(2,1)S(1)}, bf16[272,256]{1,0:T(8,128)(2,1)S(1)}, u32[]{:S(2)}, u32[]{:S(2)}) collective-permute-start(bf16[272,256]{1,0:T(8,128)(2,1)S(1)} %get-tuple-element.19), channel_id=1, source_target_pairs={{0,8},{1,9},{2,10},{3,11},{4,12},{5,13},{6,14},{7,15},{8,0},{9,1},... | collective-permute-start | bytes 417800 | tf_op jit(solution)/shard_map/ppermute | solution.py:22
  6.6 1.2 %collective-permute-start.5 = (bf16[272,256]{1,0:T(8,128)(2,1)S(1)}, bf16[272,256]{1,0:T(8,128)(2,1)S(1)}, u32[]{:S(2)}, u32[]{:S(2)}) collective-permute-start(bf16[272,256]{1,0:T(8,128)(2,1)S(1)} %get-tuple-element.21), channel_id=1, source_target_pairs={{0,24},{1,25},{2,26},{3,27},{4,28},{5,29},{6,30},{7,31},{8,16},{9,... | collective-permute-start | bytes 417800 | tf_op jit(solution)/shard_map/ppermute | solution.py:22
  7.8 2.3 %collective-permute-done.4.refs_2_ = bf16[272,256]{1,0:T(8,128)(2,1)S(1)} collective-permute-done((bf16[272,256]{1,0:T(8,128)(2,1)S(1)}, bf16[272,256]{1,0:T(8,128)(2,1)S(1)}, u32[]{:S(2)}, u32[]{:S(2)}) %collective-permute-start.4) | collective-permute-done | bytes 139296 | tf_op jit(solution)/shard_map/ppermute | solution.py:22
  10.1 0.0 copy-start.1
  10.1 0.0 copy-start.2
  10.1 2.4 %collective-permute-start.6 = (bf16[272,256]{1,0:T(8,128)(2,1)S(1)}, bf16[272,256]{1,0:T(8,128)(2,1)S(1)}, u32[]{:S(2)}, u32[]{:S(2)}) collective-permute-start(bf16[272,256]{1,0:T(8,128)(2,1)S(1)} %broadcast_select_fusion.1), channel_id=1, source_target_pairs={{0,2},{1,3},{2,0},{3,1},{4,6},{5,7},{6,4},{7,5},{8,10},{9,11},{10,... | collective-permute-start | bytes 417800 | tf_op jit(solution)/shard_map/ppermute | solution.py:22
  12.5 0.0 collective-permute-done.3.refs_1_
  12.5 1.5 %collective-permute-done.5.refs_3_ = bf16[272,256]{1,0:T(8,128)(2,1)S(1)} collective-permute-done((bf16[272,256]{1,0:T(8,128)(2,1)S(1)}, bf16[272,256]{1,0:T(8,128)(2,1)S(1)}, u32[]{:S(2)}, u32[]{:S(2)}) %collective-permute-start.5) | collective-permute-done | bytes 139296 | tf_op jit(solution)/shard_map/ppermute | solution.py:22
  14.1 2.4 %collective-permute-start.8 = (bf16[272,256]{1,0:T(8,128)(2,1)S(1)}, bf16[272,256]{1,0:T(8,128)(2,1)S(1)}, u32[]{:S(2)}, u32[]{:S(2)}) collective-permute-start(bf16[272,256]{1,0:T(8,128)(2,1)S(1)} %broadcast_select_fusion), channel_id=1, source_target_pairs={{0,2},{1,3},{2,0},{3,1},{4,6},{5,7},{6,4},{7,5},{8,10},{9,11},{10,... | collective-permute-start | bytes 417800 | tf_op jit(solution)/shard_map/ppermute | solution.py:22
  16.5 0.0 copy-done
  16.5 0.0 copy-done.3
  16.5 0.0 copy-done.5
  16.5 0.0 copy-done.6
  16.5 0.0 copy-done.7
  16.5 0.0 copy-done.1
  16.5 0.0 copy-done.2
  16.5 3.1 %lower_physics.1 = (bf16[256,256]{1,0:T(8,128)(2,1)S(1)}, bf16[256,256]{1,0:T(8,128)(2,1)S(1)}, bf16[1024,512]{1,0:T(8,128)(2,1)}, bf16[512,1024]{1,0:T(8,128)(2,1)S(1)}) custom-call(s32[5]{0:T(128)S(1)} %stack.23.ids_ref, s32[8,512]{1,0:T(8,128)S(1)} %column_targets.1.targets_ref, bf16[272,256]{1,0:T(8,128)(2,1)S(1)} %get-tuple-element.18.refs_0_, ...), custom_call_target="tpu_custom_call" | custom-call | flops 4600000000 | tf_op jit(solution)/shard_map/lower_physics/pallas_call | solution.py:261
  19.6 0.0 collective-permute-done.6.lent_ref
  19.6 1.4 %upper_physics.2 = (bf16[256,256]{1,0:T(8,128)(2,1)S(1)}, bf16[256,256]{1,0:T(8,128)(2,1)S(1)}, bf16[256,512]{1,0:T(8,128)(2,1)S(1)}) custom-call(s32[5]{0:T(128)S(1)} %stack.23.ids_ref, bf16[272,256]{1,0:T(8,128)(2,1)S(1)} %collective-permute-done.6.lent_ref, bf16[256,256]{1,0:T(8,128)(2,1)S(1)} %get-tuple-element.23.lower_answer_ref, ...), custom_call_target="tpu_custom_call" | custom-call | flops 3449999872 | tf_op jit(solution)/shard_map/upper_physics/pallas_call | solution.py:277
  21.0 1.9 %collective-permute-start.7 = (bf16[256,256]{1,0:T(8,128)(2,1)S(1)}, bf16[256,256]{1,0:T(8,128)(2,1)S(1)}, u32[]{:S(2)}, u32[]{:S(2)}) collective-permute-start(bf16[256,256]{1,0:T(8,128)(2,1)S(1)} %get-tuple-element.24), channel_id=1, source_target_pairs={{0,0},{1,1},{2,2},{3,3},{4,4},{5,5},{6,6},{7,7},{8,8},{9,9},{10,10... | collective-permute-start | bytes 393224 | tf_op jit(solution)/shard_map/ppermute | solution.py:22
  22.9 0.1 collective-permute-start.10
  23.0 1.5 %collective-permute-done.8.lent_ref = bf16[272,256]{1,0:T(8,128)(2,1)S(1)} collective-permute-done((bf16[272,256]{1,0:T(8,128)(2,1)S(1)}, bf16[272,256]{1,0:T(8,128)(2,1)S(1)}, u32[]{:S(2)}, u32[]{:S(2)}) %collective-permute-start.8) | collective-permute-done | bytes 139296 | tf_op jit(solution)/shard_map/ppermute | solution.py:22
  24.6 1.3 %upper_physics.3 = (bf16[256,256]{1,0:T(8,128)(2,1)S(1)}, bf16[256,256]{1,0:T(8,128)(2,1)S(1)}, bf16[256,512]{1,0:T(8,128)(2,1)S(1)}) custom-call(s32[5]{0:T(128)S(1)} %stack.50.ids_ref, bf16[272,256]{1,0:T(8,128)(2,1)S(1)} %collective-permute-done.8.lent_ref, bf16[256,256]{1,0:T(8,128)(2,1)S(1)} %get-tuple-element.25.lower_answer_ref, ...), custom_call_target="tpu_custom_call" | custom-call | flops 3449999872 | tf_op jit(solution)/shard_map/upper_physics/pallas_call | solution.py:277
  25.9 1.8 %collective-permute-start.9 = (bf16[256,256]{1,0:T(8,128)(2,1)S(1)}, bf16[256,256]{1,0:T(8,128)(2,1)S(1)}, u32[]{:S(2)}, u32[]{:S(2)}) collective-permute-start(bf16[256,256]{1,0:T(8,128)(2,1)S(1)} %get-tuple-element.26), channel_id=1, source_target_pairs={{0,8},{1,9},{2,10},{3,11},{4,12},{5,13},{6,14},{7,15},{8,0},{9,1},... | collective-permute-start | bytes 393224 | tf_op jit(solution)/shard_map/ppermute | solution.py:22
  27.7 1.4 %collective-permute-start.11 = (bf16[256,256]{1,0:T(8,128)(2,1)S(1)}, bf16[256,256]{1,0:T(8,128)(2,1)S(1)}, u32[]{:S(2)}, u32[]{:S(2)}) collective-permute-start(bf16[256,256]{1,0:T(8,128)(2,1)S(1)} %get-tuple-element.32), channel_id=1, source_target_pairs={{0,26},{1,27},{2,24},{3,25},{4,30},{5,31},{6,28},{7,29},{8,18},{9,... | collective-permute-start | bytes 393224 | tf_op jit(solution)/shard_map/ppermute | solution.py:22
  29.1 1.3 %store_cloud.1 = bf16[1024,512]{1,0:T(8,128)(2,1)} custom-call(s32[5]{0:T(128)S(1)} %stack.23.ids_ref, bf16[256,512]{1,0:T(8,128)(2,1)S(1)} %get-tuple-element.28.refs_0_, bf16[256,512]{1,0:T(8,128)(2,1)S(1)} %get-tuple-element.29.refs_1_, bf16[1024,512]{1,0:T(8,128)(2,1)} %get-tuple-element.30.refs_2_), custom_call_target="tpu_custom_call", output_to_operand_aliasing={{}: (3, {})} | custom-call | flops 1150000000 | tf_op jit(solution)/shard_map/store_cloud/pallas_call | solution.py:299
  30.5 0.0 collective-permute-done.10.refs_2_
  30.5 10.5 %collective-permute-start.14 = (bf16[256,256]{1,0:T(8,128)(2,1)S(1)}, bf16[256,256]{1,0:T(8,128)(2,1)S(1)}, u32[]{:S(2)}, u32[]{:S(2)}) collective-permute-start(bf16[256,256]{1,0:T(8,128)(2,1)S(1)} %collective-permute-done.10.refs_2_), channel_id=1, source_target_pairs={{0,4},{1,5},{2,6},{3,7},{4,0},{5,1},{6,2},{7,3},{8,12},{9,13},{10,... | collective-permute-start | bytes 393224 | tf_op jit(solution)/shard_map/ppermute | solution.py:22
  41.0 0.0 collective-permute-done.7.refs_0_
  41.0 0.0 collective-permute-start.12
  41.0 0.0 collective-permute-done.9.refs_1_
  41.0 0.5 %collective-permute-start.13 = (bf16[256,256]{1,0:T(8,128)(2,1)S(1)}, bf16[256,256]{1,0:T(8,128)(2,1)S(1)}, u32[]{:S(2)}, u32[]{:S(2)}) collective-permute-start(bf16[256,256]{1,0:T(8,128)(2,1)S(1)} %collective-permute-done.9.refs_1_), channel_id=1, source_target_pairs={{0,4},{1,5},{2,6},{3,7},{4,0},{5,1},{6,2},{7,3},{8,12},{9,13},{10,... | collective-permute-start | bytes 393224 | tf_op jit(solution)/shard_map/ppermute | solution.py:22
  41.5 0.0 collective-permute-done.11.refs_3_
  41.5 1.8 %collective-permute-start.15 = (bf16[256,256]{1,0:T(8,128)(2,1)S(1)}, bf16[256,256]{1,0:T(8,128)(2,1)S(1)}, u32[]{:S(2)}, u32[]{:S(2)}) collective-permute-start(bf16[256,256]{1,0:T(8,128)(2,1)S(1)} %collective-permute-done.11.refs_3_), channel_id=1, source_target_pairs={{0,4},{1,5},{2,6},{3,7},{4,0},{5,1},{6,2},{7,3},{8,12},{9,13},{10,... | collective-permute-start | bytes 393224 | tf_op jit(solution)/shard_map/ppermute | solution.py:22
  43.3 0.0 collective-permute-done.12.refs_4_
  43.3 0.0 collective-permute-done.13.refs_5_
  43.3 0.0 collective-permute-done.14.refs_6_
  43.3 1.0 %collective-permute-done.15.refs_7_ = bf16[256,256]{1,0:T(8,128)(2,1)S(1)} collective-permute-done((bf16[256,256]{1,0:T(8,128)(2,1)S(1)}, bf16[256,256]{1,0:T(8,128)(2,1)S(1)}, u32[]{:S(2)}, u32[]{:S(2)}) %collective-permute-start.15) | collective-permute-done | bytes 131104 | tf_op jit(solution)/shard_map/ppermute | solution.py:22
  44.3 1.7 %collect_columns.1 = bf16[512,256]{1,0:T(8,128)(2,1)} custom-call(s32[5]{0:T(128)S(1)} %stack.23.ids_ref, bf16[512,1024]{1,0:T(8,128)(2,1)S(1)} %get-tuple-element.22.hot_ref, bf16[256,256]{1,0:T(8,128)(2,1)S(1)} %collective-permute-done.7.refs_0_, bf16[256,256]{1,0:T(8,128)(2,1)S(1)} %collective-permute-done.9.refs_1_, ...), custom_call_target="tpu_custom_call" | custom-call | flops 3449999872 | tf_op jit(solution)/shard_map/collect_columns/pallas_call | solution.py:314
  (2 shorter events, 0.0 us)
Async XLA Ops:
  0.6 0.8 %copy-start.9 = (s32[512,1]{0,1:T(1,128)S(1)}, s32[512,1]{0,1:T(1,128)}, u32[]{:S(2)}) copy-start(s32[512,1]{0,1:T(1,128)} %param.12) | copy-start | bytes 6148
  0.6 1.8 %collective-permute-start = (s32[4,128]{1,0:T(4,128)}, s32[4,128]{1,0:T(4,128)S(1)}, u32[]{:S(2)}, u32[]{:S(2)}) collective-permute-start(s32[4,128]{1,0:T(4,128)} %bitcast.9), channel_id=1, source_target_pairs={{0,4},{1,5},{2,6},{3,7},{4,0},{5,1},{6,2},{7,3},{8,12},{9,13},{10,... | collective-permute-start | bytes 6152 | tf_op jit(solution)/shard_map/ppermute | solution.py:22
  1.4 1.4 %collective-permute-start.1 = (s32[4,128]{1,0:T(4,128)S(1)}, s32[4,128]{1,0:T(4,128)S(1)}, u32[]{:S(2)}, u32[]{:S(2)}) collective-permute-start(s32[4,128]{1,0:T(4,128)S(1)} %bitcast.11), channel_id=1, source_target_pairs={{0,4},{1,5},{2,6},{3,7},{4,0},{5,1},{6,2},{7,3},{8,12},{9,13},{10,... | collective-permute-start | bytes 6152 | tf_op jit(solution)/shard_map/ppermute | solution.py:22
  2.0 1.7 %collective-permute-start.2 = (bf16[512,256]{1,0:T(8,128)(2,1)}, bf16[512,256]{1,0:T(8,128)(2,1)S(1)}, u32[]{:S(2)}, u32[]{:S(2)}) collective-permute-start(bf16[512,256]{1,0:T(8,128)(2,1)} %state_ref.1), channel_id=1, source_target_pairs={{0,4},{1,5},{2,6},{3,7},{4,0},{5,1},{6,2},{7,3},{8,12},{9,13},{10,... | collective-permute-start | bytes 786440 | tf_op jit(solution)/shard_map/ppermute | solution.py:22
  2.0 0.8 %copy-start.8 = (s32[512,1]{0,1:T(1,128)S(1)}, s32[512,1]{0,1:T(1,128)}, u32[]{:S(2)}) copy-start(s32[512,1]{0,1:T(1,128)} %param.11) | copy-start | bytes 6148
  2.1 1.7 %copy-start.4 = (bf16[512,256]{1,0:T(8,128)(2,1)S(1)}, bf16[512,256]{1,0:T(8,128)(2,1)}, u32[]{:S(2)}) copy-start(bf16[512,256]{1,0:T(8,128)(2,1)} %state_ref.1) | copy-start | bytes 786436
  3.6 12.9 %copy-start = (bf16[1024,512]{1,0:T(8,128)(2,1)S(1)}, bf16[1024,512]{1,0:T(8,128)(2,1)}, u32[]{:S(2)}) copy-start(bf16[1024,512]{1,0:T(8,128)(2,1)} %cloud_ref.3) | copy-start | bytes 3145732
  3.7 12.7 %copy-start.3 = (bf16[768,256]{1,0:T(8,128)(2,1)S(1)}, bf16[768,256]{1,0:T(8,128)(2,1)}, u32[]{:S(2)}) copy-start(bf16[768,256]{1,0:T(8,128)(2,1)} %refs_3_.3) | copy-start | bytes 1179652
  3.7 12.7 %copy-start.5 = (bf16[256,256]{1,0:T(8,128)(2,1)S(1)}, bf16[256,256]{1,0:T(8,128)(2,1)}, u32[]{:S(2)}) copy-start(bf16[256,256]{1,0:T(8,128)(2,1)} %refs_1_.3) | copy-start | bytes 393220
  3.7 12.7 %copy-start.6 = (bf16[256,256]{1,0:T(8,128)(2,1)S(1)}, bf16[256,256]{1,0:T(8,128)(2,1)}, u32[]{:S(2)}) copy-start(bf16[256,256]{1,0:T(8,128)(2,1)} %refs_4_.5) | copy-start | bytes 393220
  3.7 12.7 %copy-start.7 = (bf16[256,128]{1,0:T(8,128)(2,1)S(1)}, bf16[256,128]{1,0:T(8,128)(2,1)}, u32[]{:S(2)}) copy-start(bf16[256,128]{1,0:T(8,128)(2,1)} %refs_5_.5) | copy-start | bytes 196612
  5.0 5.1 %collective-permute-start.4 = (bf16[272,256]{1,0:T(8,128)(2,1)S(1)}, bf16[272,256]{1,0:T(8,128)(2,1)S(1)}, u32[]{:S(2)}, u32[]{:S(2)}) collective-permute-start(bf16[272,256]{1,0:T(8,128)(2,1)S(1)} %get-tuple-element.20), channel_id=1, source_target_pairs={{0,16},{1,17},{2,18},{3,19},{4,20},{5,21},{6,22},{7,23},{8,24},{9,... | collective-permute-start | bytes 417800 | tf_op jit(solution)/shard_map/ppermute | solution.py:22
  5.2 7.3 %collective-permute-start.3 = (bf16[272,256]{1,0:T(8,128)(2,1)S(1)}, bf16[272,256]{1,0:T(8,128)(2,1)S(1)}, u32[]{:S(2)}, u32[]{:S(2)}) collective-permute-start(bf16[272,256]{1,0:T(8,128)(2,1)S(1)} %get-tuple-element.19), channel_id=1, source_target_pairs={{0,8},{1,9},{2,10},{3,11},{4,12},{5,13},{6,14},{7,15},{8,0},{9,1},... | collective-permute-start | bytes 417800 | tf_op jit(solution)/shard_map/ppermute | solution.py:22
  6.6 7.4 %collective-permute-start.5 = (bf16[272,256]{1,0:T(8,128)(2,1)S(1)}, bf16[272,256]{1,0:T(8,128)(2,1)S(1)}, u32[]{:S(2)}, u32[]{:S(2)}) collective-permute-start(bf16[272,256]{1,0:T(8,128)(2,1)S(1)} %get-tuple-element.21), channel_id=1, source_target_pairs={{0,24},{1,25},{2,26},{3,27},{4,28},{5,29},{6,30},{7,31},{8,16},{9,... | collective-permute-start | bytes 417800 | tf_op jit(solution)/shard_map/ppermute | solution.py:22
  10.1 6.4 %copy-start.1 = (bf16[768,256]{1,0:T(8,128)(2,1)S(1)}, bf16[768,256]{1,0:T(8,128)(2,1)}, u32[]{:S(2)}) copy-start(bf16[768,256]{1,0:T(8,128)(2,1)} %refs_0_.3) | copy-start | bytes 1179652
  10.1 6.4 %copy-start.2 = (bf16[256,768]{1,0:T(8,128)(2,1)S(1)}, bf16[256,768]{1,0:T(8,128)(2,1)}, u32[]{:S(2)}) copy-start(bf16[256,768]{1,0:T(8,128)(2,1)} %refs_2_.3) | copy-start | bytes 1179652
  10.1 9.5 %collective-permute-start.6 = (bf16[272,256]{1,0:T(8,128)(2,1)S(1)}, bf16[272,256]{1,0:T(8,128)(2,1)S(1)}, u32[]{:S(2)}, u32[]{:S(2)}) collective-permute-start(bf16[272,256]{1,0:T(8,128)(2,1)S(1)} %broadcast_select_fusion.1), channel_id=1, source_target_pairs={{0,2},{1,3},{2,0},{3,1},{4,6},{5,7},{6,4},{7,5},{8,10},{9,11},{10,... | collective-permute-start | bytes 417800 | tf_op jit(solution)/shard_map/ppermute | solution.py:22
  14.1 10.5 %collective-permute-start.8 = (bf16[272,256]{1,0:T(8,128)(2,1)S(1)}, bf16[272,256]{1,0:T(8,128)(2,1)S(1)}, u32[]{:S(2)}, u32[]{:S(2)}) collective-permute-start(bf16[272,256]{1,0:T(8,128)(2,1)S(1)} %broadcast_select_fusion), channel_id=1, source_target_pairs={{0,2},{1,3},{2,0},{3,1},{4,6},{5,7},{6,4},{7,5},{8,10},{9,11},{10,... | collective-permute-start | bytes 417800 | tf_op jit(solution)/shard_map/ppermute | solution.py:22
  21.0 20.0 %collective-permute-start.7 = (bf16[256,256]{1,0:T(8,128)(2,1)S(1)}, bf16[256,256]{1,0:T(8,128)(2,1)S(1)}, u32[]{:S(2)}, u32[]{:S(2)}) collective-permute-start(bf16[256,256]{1,0:T(8,128)(2,1)S(1)} %get-tuple-element.24), channel_id=1, source_target_pairs={{0,0},{1,1},{2,2},{3,3},{4,4},{5,5},{6,6},{7,7},{8,8},{9,9},{10,10... | collective-permute-start | bytes 393224 | tf_op jit(solution)/shard_map/ppermute | solution.py:22
  22.9 7.5 %collective-permute-start.10 = (bf16[256,256]{1,0:T(8,128)(2,1)S(1)}, bf16[256,256]{1,0:T(8,128)(2,1)S(1)}, u32[]{:S(2)}, u32[]{:S(2)}) collective-permute-start(bf16[256,256]{1,0:T(8,128)(2,1)S(1)} %get-tuple-element.27), channel_id=1, source_target_pairs={{0,18},{1,19},{2,16},{3,17},{4,22},{5,23},{6,20},{7,21},{8,26},{9,... | collective-permute-start | bytes 393224 | tf_op jit(solution)/shard_map/ppermute | solution.py:22
  25.9 15.1 %collective-permute-start.9 = (bf16[256,256]{1,0:T(8,128)(2,1)S(1)}, bf16[256,256]{1,0:T(8,128)(2,1)S(1)}, u32[]{:S(2)}, u32[]{:S(2)}) collective-permute-start(bf16[256,256]{1,0:T(8,128)(2,1)S(1)} %get-tuple-element.26), channel_id=1, source_target_pairs={{0,8},{1,9},{2,10},{3,11},{4,12},{5,13},{6,14},{7,15},{8,0},{9,1},... | collective-permute-start | bytes 393224 | tf_op jit(solution)/shard_map/ppermute | solution.py:22
  27.7 13.8 %collective-permute-start.11 = (bf16[256,256]{1,0:T(8,128)(2,1)S(1)}, bf16[256,256]{1,0:T(8,128)(2,1)S(1)}, u32[]{:S(2)}, u32[]{:S(2)}) collective-permute-start(bf16[256,256]{1,0:T(8,128)(2,1)S(1)} %get-tuple-element.32), channel_id=1, source_target_pairs={{0,26},{1,27},{2,24},{3,25},{4,30},{5,31},{6,28},{7,29},{8,18},{9,... | collective-permute-start | bytes 393224 | tf_op jit(solution)/shard_map/ppermute | solution.py:22
  30.5 12.8 %collective-permute-start.14 = (bf16[256,256]{1,0:T(8,128)(2,1)S(1)}, bf16[256,256]{1,0:T(8,128)(2,1)S(1)}, u32[]{:S(2)}, u32[]{:S(2)}) collective-permute-start(bf16[256,256]{1,0:T(8,128)(2,1)S(1)} %collective-permute-done.10.refs_2_), channel_id=1, source_target_pairs={{0,4},{1,5},{2,6},{3,7},{4,0},{5,1},{6,2},{7,3},{8,12},{9,13},{10,... | collective-permute-start | bytes 393224 | tf_op jit(solution)/shard_map/ppermute | solution.py:22
  41.0 2.3 %collective-permute-start.12 = (bf16[256,256]{1,0:T(8,128)(2,1)S(1)}, bf16[256,256]{1,0:T(8,128)(2,1)S(1)}, u32[]{:S(2)}, u32[]{:S(2)}) collective-permute-start(bf16[256,256]{1,0:T(8,128)(2,1)S(1)} %collective-permute-done.7.refs_0_), channel_id=1, source_target_pairs={{0,4},{1,5},{2,6},{3,7},{4,0},{5,1},{6,2},{7,3},{8,12},{9,13},{10,... | collective-permute-start | bytes 393224 | tf_op jit(solution)/shard_map/ppermute | solution.py:22
  41.0 2.3 %collective-permute-start.13 = (bf16[256,256]{1,0:T(8,128)(2,1)S(1)}, bf16[256,256]{1,0:T(8,128)(2,1)S(1)}, u32[]{:S(2)}, u32[]{:S(2)}) collective-permute-start(bf16[256,256]{1,0:T(8,128)(2,1)S(1)} %collective-permute-done.9.refs_1_), channel_id=1, source_target_pairs={{0,4},{1,5},{2,6},{3,7},{4,0},{5,1},{6,2},{7,3},{8,12},{9,13},{10,... | collective-permute-start | bytes 393224 | tf_op jit(solution)/shard_map/ppermute | solution.py:22
  41.5 2.8 %collective-permute-start.15 = (bf16[256,256]{1,0:T(8,128)(2,1)S(1)}, bf16[256,256]{1,0:T(8,128)(2,1)S(1)}, u32[]{:S(2)}, u32[]{:S(2)}) collective-permute-start(bf16[256,256]{1,0:T(8,128)(2,1)S(1)} %collective-permute-done.11.refs_3_), channel_id=1, source_target_pairs={{0,4},{1,5},{2,6},{3,7},{4,0},{5,1},{6,2},{7,3},{8,12},{9,13},{10,... | collective-permute-start | bytes 393224 | tf_op jit(solution)/shard_map/ppermute | solution.py:22

commit v4 on v3

--- a/solution.py
+++ b/solution.py
@@ -180,16 +180,39 @@
         copy.wait()
 
 
-def collect_kernel(groups, cap, ids_ref, hot_ref, *refs):
-    units = groups // 2
-    own, far, out_ref = refs[:units], refs[units : 2 * units], refs[2 * units]
-    offset = pl.multiple_of(ids_ref[0] * cap, cap)
+def gathered(cap, hot_ref, pieces):
     total = None
-    for du in range(units):
-        block = jnp.concatenate([own[du][pl.ds(offset, cap), :], far[du][pl.ds(offset, cap), :]], axis=0)
-        part = dot(hot_ref[:, 2 * du * cap : 2 * (du + 1) * cap], block)
+    for place, blocks in pieces:
+        block = blocks[0] if len(blocks) == 1 else jnp.concatenate(blocks, axis=0)
+        part = dot(hot_ref[:, place * cap : (place + len(blocks)) * cap], block)
         total = part if total is None else total + part
-    out_ref[...] = total.astype(jnp.bfloat16)
+    return total
+
+
+def gather_kernel(cap, sequence, ids_ref, hot_ref, *refs):
+    count = len(sequence)
+    own, far, out_ref = refs[:count], refs[count:-1], refs[-1]
+    rows = pl.ds(pl.multiple_of(ids_ref[0] * cap, cap), cap)
+    pieces = []
+    for i, du in enumerate(sequence):
+        blocks = [own[i][rows, :]] + ([far[i][rows, :]] if i < count - 1 else [])
+        pieces.append((2 * du, blocks))
+    out_ref[...] = gathered(cap, hot_ref, pieces).astype(jnp.bfloat16)
+
+
+def finish_kernel(cap, last, ids_ref, hot_ref, gathered_ref, far_ref, out_ref, buffer_ref, sems):
+    block = far_ref[pl.ds(pl.multiple_of(ids_ref[0] * cap, cap), cap), :]
+    parts = sems.shape[0]
+    step = out_ref.shape[0] // parts
+    copies = []
+    for i in range(parts):
+        span = pl.ds(i * step, step)
+        part = dot(hot_ref[span, (2 * last + 1) * cap : (2 * last + 2) * cap], block)
+        buffer_ref[span, :] = (gathered_ref[span, :].astype(jnp.float32) + part).astype(jnp.bfloat16)
+        copies.append(pltpu.make_async_copy(buffer_ref.at[span, :], out_ref.at[span, :], sems.at[i]))
+        copies[-1].start()
+    for copy in copies:
+        copy.wait()
 
 
 def per_device(state, dest_map, day_mask, cloud, conv_in, conv_mid, conv_out, rad_in, rad_mid, rad_out):
@@ -293,9 +316,8 @@
         return target
 
     back = [None] * units
-    sequence = [*range(half, units), *range(half)]
-    for du in sequence:
-        back[du] = moved(answers[du], home(du))
+    sequence = [du for low in range(half) for du in (half + low, low)]
+    back = [moved(answers[du], home(du)) for du in sequence]
     new_cloud = pl.pallas_call(
         functools.partial(store_kernel, cap),
         out_shape=like(cloud),
@@ -307,19 +329,27 @@
         cost_estimate=work(1),
         name="store_cloud",
     )(ids, *news, new_cloud)
-    back[half], new_cloud = lax.optimization_barrier((back[half], new_cloud))
-    far_back = [None] * units
-    for du in sequence:
-        far_back[du] = swapped(back[du])
+    back[0], new_cloud = lax.optimization_barrier((back[0], new_cloud))
+    far_back = [swapped(block) for block in back]
+    most = pl.pallas_call(
+        functools.partial(gather_kernel, cap, sequence),
+        out_shape=like(state),
+        in_specs=[smem] + [vmem] * (2 * units),
+        out_specs=vmem,
+        compiler_params=params,
+        cost_estimate=work(2),
+        name="gather_most",
+    )(ids, hot, *back, *far_back[:-1])
     tendency = pl.pallas_call(
-        functools.partial(collect_kernel, groups, cap),
+        functools.partial(finish_kernel, cap, sequence[-1]),
         out_shape=like(state),
-        in_specs=[smem] + [vmem] * (2 * units + 1),
-        out_specs=vmem,
-        compiler_params=params,
-        cost_estimate=work(3),
-        name="collect_columns",
-    )(ids, hot, *back, *far_back)
+        in_specs=[smem] + [vmem] * 3,
+        out_specs=hbm,
+        scratch_shapes=[pltpu.VMEM(state.shape, jnp.bfloat16), pltpu.SemaphoreType.DMA((2,))],
+        compiler_params=params,
+        cost_estimate=work(1),
+        name="gather_last",
+    )(ids, hot, most, far_back[-1])
     return (tendency, new_cloud)
 
 

time: 46.2 us -> 44.5 us (0.963)
  waiting for transfers between devices: 7.24 us -> 5.91 us
  starting transfers between devices: 26.9 us -> 25.7 us
  Pallas kernels: 10.8 us -> 11.6 us
    ppermute x16, waiting for transfers between devices: 7.24 us -> 5.91 us  [moved(): return lax.ppermute(block, ('elem', 'band'), route)]
    ppermute x16, starting transfers between devices: 26.9 us -> 25.7 us  [moved(): return lax.ppermute(block, ('elem', 'band'), route)]
    pallas_call x1 -> x2, Pallas kernels: 1.69 us -> 2.47 us  [the longest x1 1.48 us: per_device(): pl.pallas_call(functools.partial(finish_kernel, cap, sequence[-1]), out_s...]
  transfers between devices with their start and end apart: 16 -> 16, of which waited for: 7 -> 6; matrix products, arithmetic and copies ran while one was open for 0% -> 0% of each run, Pallas kernels for 17% -> 20%
where the time goes in v4:
time: 44.5 us; the launch traced here: 44.3 us
  starting transfers between devices  25.7 us (58%)
  Pallas kernels  11.6 us (26%)
  waiting for transfers between devices  5.91 us (13%)
  between operations  0.81 us (2%)
    ppermute x16, starting transfers between devices, moved(): return lax.ppermute(block, ('elem', 'band'), route)  25.7 us
    ppermute x16, waiting for transfers between devices, moved(): return lax.ppermute(block, ('elem', 'band'), route)  5.91 us
    pallas_call x1, Pallas kernels, per_device(): pl.pallas_call(functools.partial(lower_kernel, groups, cap, len(base), pi...  3.11 us
    pallas_call x2, Pallas kernels, per_device(): pl.pallas_call(functools.partial(upper_kernel, cap), out_shape=[tile, til...  2.7 us
    pallas_call x1, Pallas kernels, per_device(): pl.pallas_call(functools.partial(finish_kernel, cap, sequence[-1]), out_s...  1.48 us
    pallas_call x1, Pallas kernels, per_device(): pl.pallas_call(functools.partial(store_kernel, cap), out_shape=like(cloud...  1.35 us
    pallas_call x1, Pallas kernels, per_device(): pl.pallas_call(functools.partial(place_kernel, groups, cap), out_shape=[p...  1.24 us
    pallas_call x1, Pallas kernels, per_device(): pl.pallas_call(functools.partial(gather_kernel, cap, sequence), out_shape...  0.99 us
  transfers between devices with their start and end apart: 16, of which 6 were waited for; matrix products, arithmetic and copies ran while one was open for 0% of the time, Pallas kernels for 20%

profile of v4, /device:TPU:5, one launch (start us, length us, event | category | flops | bytes accessed | tf_op | source)
XLA Modules:
  0.0 44.3 jit_solution(53353376327278735)
XLA Ops:
  0.6 0.0 copy-start.9
  0.6 0.7 %collective-permute-start = (s32[4,128]{1,0:T(4,128)}, s32[4,128]{1,0:T(4,128)S(1)}, u32[]{:S(2)}, u32[]{:S(2)}) collective-permute-start(s32[4,128]{1,0:T(4,128)} %bitcast.9), channel_id=1, source_target_pairs={{0,4},{1,5},{2,6},{3,7},{4,0},{5,1},{6,2},{7,3},{8,12},{9,13},{10,... | collective-permute-start | bytes 6152 | tf_op jit(solution)/shard_map/ppermute | solution.py:22
  1.4 0.0 copy-done.9
  1.4 0.6 %collective-permute-start.1 = (s32[4,128]{1,0:T(4,128)S(1)}, s32[4,128]{1,0:T(4,128)S(1)}, u32[]{:S(2)}, u32[]{:S(2)}) collective-permute-start(s32[4,128]{1,0:T(4,128)S(1)} %bitcast.11), channel_id=1, source_target_pairs={{0,4},{1,5},{2,6},{3,7},{4,0},{5,1},{6,2},{7,3},{8,12},{9,13},{10,... | collective-permute-start | bytes 6152 | tf_op jit(solution)/shard_map/ppermute | solution.py:22
  2.0 0.0 collective-permute-start.2
  2.0 0.0 copy-start.8
  2.0 0.1 stack.23.ids_ref
  2.1 0.0 copy-start.4
  2.1 0.3 collective-permute-done.far_dest_ref
  2.4 0.4 collective-permute-done.1.far_day_ref
  2.8 0.0 copy-done.8
  2.8 0.7 %column_targets.1.targets_ref = s32[8,512]{1,0:T(8,128)S(1)} custom-call(s32[5]{0:T(128)S(1)} %stack.23.ids_ref, s32[4,128]{1,0:T(4,128)S(1)} %bitcast.10, s32[4,128]{1,0:T(4,128)S(1)} %bitcast.12, s32[4,128]{1,0:T(4,128)S(1)} %collective-permute-done.far_dest_ref, s32[4,128]{1,0:T(4,128)S(1)} %collective-permute-done.1.far_day_ref), custom_call_target="tpu_custom_call" | custom-call | flops 4600000000 | tf_op jit(solution)/shard_map/column_targets/pallas_call | solution.py:248
  3.6 0.0 copy-start
  3.6 0.2 collective-permute-done.2.far_state_ref
  3.7 0.0 copy-done.4
  3.7 0.0 copy-start.3
  3.7 0.0 copy-start.5
  3.7 0.0 copy-start.6
  3.7 0.0 copy-start.7
  3.8 1.2 %place_columns.1 = (bf16[272,256]{1,0:T(8,128)(2,1)S(1)}, bf16[272,256]{1,0:T(8,128)(2,1)S(1)}, bf16[272,256]{1,0:T(8,128)(2,1)S(1)}, bf16[272,256]{1,0:T(8,128)(2,1)S(1)}) custom-call(s32[5]{0:T(128)S(1)} %stack.23.ids_ref, s32[8,512]{1,0:T(8,128)S(1)} %column_targets.1.targets_ref, bf16[512,256]{1,0:T(8,128)(2,1)S(1)} %copy-done.4, ...), custom_call_target="tpu_custom_call" | custom-call | flops 4600000000 | tf_op jit(solution)/shard_map/place_columns/pallas_call | solution.py:257
  5.0 0.1 collective-permute-start.4
  5.1 0.1 stack.50.ids_ref
  5.2 1.4 %collective-permute-start.3 = (bf16[272,256]{1,0:T(8,128)(2,1)S(1)}, bf16[272,256]{1,0:T(8,128)(2,1)S(1)}, u32[]{:S(2)}, u32[]{:S(2)}) collective-permute-start(bf16[272,256]{1,0:T(8,128)(2,1)S(1)} %get-tuple-element.19), channel_id=1, source_target_pairs={{0,8},{1,9},{2,10},{3,11},{4,12},{5,13},{6,14},{7,15},{8,0},{9,1},... | collective-permute-start | bytes 417800 | tf_op jit(solution)/shard_map/ppermute | solution.py:22
  6.6 1.2 %collective-permute-start.5 = (bf16[272,256]{1,0:T(8,128)(2,1)S(1)}, bf16[272,256]{1,0:T(8,128)(2,1)S(1)}, u32[]{:S(2)}, u32[]{:S(2)}) collective-permute-start(bf16[272,256]{1,0:T(8,128)(2,1)S(1)} %get-tuple-element.21), channel_id=1, source_target_pairs={{0,24},{1,25},{2,26},{3,27},{4,28},{5,29},{6,30},{7,31},{8,16},{9,... | collective-permute-start | bytes 417800 | tf_op jit(solution)/shard_map/ppermute | solution.py:22
  7.8 2.3 %collective-permute-done.4.refs_2_ = bf16[272,256]{1,0:T(8,128)(2,1)S(1)} collective-permute-done((bf16[272,256]{1,0:T(8,128)(2,1)S(1)}, bf16[272,256]{1,0:T(8,128)(2,1)S(1)}, u32[]{:S(2)}, u32[]{:S(2)}) %collective-permute-start.4) | collective-permute-done | bytes 139296 | tf_op jit(solution)/shard_map/ppermute | solution.py:22
  10.1 0.0 copy-start.1
  10.1 0.0 copy-start.2
  10.1 2.4 %collective-permute-start.6 = (bf16[272,256]{1,0:T(8,128)(2,1)S(1)}, bf16[272,256]{1,0:T(8,128)(2,1)S(1)}, u32[]{:S(2)}, u32[]{:S(2)}) collective-permute-start(bf16[272,256]{1,0:T(8,128)(2,1)S(1)} %broadcast_select_fusion.1), channel_id=1, source_target_pairs={{0,2},{1,3},{2,0},{3,1},{4,6},{5,7},{6,4},{7,5},{8,10},{9,11},{10,... | collective-permute-start | bytes 417800 | tf_op jit(solution)/shard_map/ppermute | solution.py:22
  12.5 0.0 collective-permute-done.3.refs_1_
  12.5 1.5 %collective-permute-done.5.refs_3_ = bf16[272,256]{1,0:T(8,128)(2,1)S(1)} collective-permute-done((bf16[272,256]{1,0:T(8,128)(2,1)S(1)}, bf16[272,256]{1,0:T(8,128)(2,1)S(1)}, u32[]{:S(2)}, u32[]{:S(2)}) %collective-permute-start.5) | collective-permute-done | bytes 139296 | tf_op jit(solution)/shard_map/ppermute | solution.py:22
  14.1 2.4 %collective-permute-start.8 = (bf16[272,256]{1,0:T(8,128)(2,1)S(1)}, bf16[272,256]{1,0:T(8,128)(2,1)S(1)}, u32[]{:S(2)}, u32[]{:S(2)}) collective-permute-start(bf16[272,256]{1,0:T(8,128)(2,1)S(1)} %broadcast_select_fusion), channel_id=1, source_target_pairs={{0,2},{1,3},{2,0},{3,1},{4,6},{5,7},{6,4},{7,5},{8,10},{9,11},{10,... | collective-permute-start | bytes 417800 | tf_op jit(solution)/shard_map/ppermute | solution.py:22
  16.5 0.0 copy-done
  16.5 0.0 copy-done.3
  16.5 0.0 copy-done.5
  16.5 0.0 copy-done.6
  16.5 0.0 copy-done.7
  16.5 0.0 copy-done.1
  16.5 0.0 copy-done.2
  16.5 3.1 %lower_physics.1 = (bf16[256,256]{1,0:T(8,128)(2,1)S(1)}, bf16[256,256]{1,0:T(8,128)(2,1)S(1)}, bf16[1024,512]{1,0:T(8,128)(2,1)}, bf16[512,1024]{1,0:T(8,128)(2,1)S(1)}) custom-call(s32[5]{0:T(128)S(1)} %stack.23.ids_ref, s32[8,512]{1,0:T(8,128)S(1)} %column_targets.1.targets_ref, bf16[272,256]{1,0:T(8,128)(2,1)S(1)} %get-tuple-element.18.refs_0_, ...), custom_call_target="tpu_custom_call" | custom-call | flops 4600000000 | tf_op jit(solution)/shard_map/lower_physics/pallas_call | solution.py:284
  19.6 0.0 collective-permute-done.6.lent_ref
  19.6 1.4 %upper_physics.2 = (bf16[256,256]{1,0:T(8,128)(2,1)S(1)}, bf16[256,256]{1,0:T(8,128)(2,1)S(1)}, bf16[256,512]{1,0:T(8,128)(2,1)S(1)}) custom-call(s32[5]{0:T(128)S(1)} %stack.23.ids_ref, bf16[272,256]{1,0:T(8,128)(2,1)S(1)} %collective-permute-done.6.lent_ref, bf16[256,256]{1,0:T(8,128)(2,1)S(1)} %get-tuple-element.23.lower_answer_ref, ...), custom_call_target="tpu_custom_call" | custom-call | flops 3449999872 | tf_op jit(solution)/shard_map/upper_physics/pallas_call | solution.py:300
  21.0 0.4 collective-permute-start.7
  21.4 1.9 %collective-permute-start.9 = (bf16[256,256]{1,0:T(8,128)(2,1)S(1)}, bf16[256,256]{1,0:T(8,128)(2,1)S(1)}, u32[]{:S(2)}, u32[]{:S(2)}) collective-permute-start(bf16[256,256]{1,0:T(8,128)(2,1)S(1)} %get-tuple-element.30), channel_id=1, source_target_pairs={{0,0},{1,1},{2,2},{3,3},{4,4},{5,5},{6,6},{7,7},{8,8},{9,9},{10,10... | collective-permute-start | bytes 393224 | tf_op jit(solution)/shard_map/ppermute | solution.py:22
  23.4 1.2 %collective-permute-done.8.lent_ref = bf16[272,256]{1,0:T(8,128)(2,1)S(1)} collective-permute-done((bf16[272,256]{1,0:T(8,128)(2,1)S(1)}, bf16[272,256]{1,0:T(8,128)(2,1)S(1)}, u32[]{:S(2)}, u32[]{:S(2)}) %collective-permute-start.8) | collective-permute-done | bytes 139296 | tf_op jit(solution)/shard_map/ppermute | solution.py:22
  24.6 1.3 %upper_physics.3 = (bf16[256,256]{1,0:T(8,128)(2,1)S(1)}, bf16[256,256]{1,0:T(8,128)(2,1)S(1)}, bf16[256,512]{1,0:T(8,128)(2,1)S(1)}) custom-call(s32[5]{0:T(128)S(1)} %stack.50.ids_ref, bf16[272,256]{1,0:T(8,128)(2,1)S(1)} %collective-permute-done.8.lent_ref, bf16[256,256]{1,0:T(8,128)(2,1)S(1)} %get-tuple-element.26.lower_answer_ref, ...), custom_call_target="tpu_custom_call" | custom-call | flops 3449999872 | tf_op jit(solution)/shard_map/upper_physics/pallas_call | solution.py:300
  25.9 1.2 %collective-permute-start.10 = (bf16[256,256]{1,0:T(8,128)(2,1)S(1)}, bf16[256,256]{1,0:T(8,128)(2,1)S(1)}, u32[]{:S(2)}, u32[]{:S(2)}) collective-permute-start(bf16[256,256]{1,0:T(8,128)(2,1)S(1)} %get-tuple-element.31), channel_id=1, source_target_pairs={{0,26},{1,27},{2,24},{3,25},{4,30},{5,31},{6,28},{7,29},{8,18},{9,... | collective-permute-start | bytes 393224 | tf_op jit(solution)/shard_map/ppermute | solution.py:22
  27.1 0.8 %collective-permute-start.11 = (bf16[256,256]{1,0:T(8,128)(2,1)S(1)}, bf16[256,256]{1,0:T(8,128)(2,1)S(1)}, u32[]{:S(2)}, u32[]{:S(2)}) collective-permute-start(bf16[256,256]{1,0:T(8,128)(2,1)S(1)} %get-tuple-element.32), channel_id=1, source_target_pairs={{0,8},{1,9},{2,10},{3,11},{4,12},{5,13},{6,14},{7,15},{8,0},{9,1},... | collective-permute-start | bytes 393224 | tf_op jit(solution)/shard_map/ppermute | solution.py:22
  28.0 1.3 %store_cloud.1 = bf16[1024,512]{1,0:T(8,128)(2,1)} custom-call(s32[5]{0:T(128)S(1)} %stack.23.ids_ref, bf16[256,512]{1,0:T(8,128)(2,1)S(1)} %get-tuple-element.25.refs_0_, bf16[256,512]{1,0:T(8,128)(2,1)S(1)} %get-tuple-element.27.refs_1_, bf16[1024,512]{1,0:T(8,128)(2,1)} %get-tuple-element.28.refs_2_), custom_call_target="tpu_custom_call", output_to_operand_aliasing={{}: (3, {})} | custom-call | flops 1150000000 | tf_op jit(solution)/shard_map/store_cloud/pallas_call | solution.py:321
  29.3 0.0 collective-permute-done.7.refs_0_
  29.3 5.6 %collective-permute-start.12 = (bf16[256,256]{1,0:T(8,128)(2,1)S(1)}, bf16[256,256]{1,0:T(8,128)(2,1)S(1)}, u32[]{:S(2)}, u32[]{:S(2)}) collective-permute-start(bf16[256,256]{1,0:T(8,128)(2,1)S(1)} %collective-permute-done.7.refs_0_), channel_id=1, source_target_pairs={{0,4},{1,5},{2,6},{3,7},{4,0},{5,1},{6,2},{7,3},{8,12},{9,13},{10,... | collective-permute-start | bytes 393224 | tf_op jit(solution)/shard_map/ppermute | solution.py:22
  34.9 0.0 collective-permute-done.9.refs_1_
  34.9 4.6 %collective-permute-start.13 = (bf16[256,256]{1,0:T(8,128)(2,1)S(1)}, bf16[256,256]{1,0:T(8,128)(2,1)S(1)}, u32[]{:S(2)}, u32[]{:S(2)}) collective-permute-start(bf16[256,256]{1,0:T(8,128)(2,1)S(1)} %collective-permute-done.9.refs_1_), channel_id=1, source_target_pairs={{0,4},{1,5},{2,6},{3,7},{4,0},{5,1},{6,2},{7,3},{8,12},{9,13},{10,... | collective-permute-start | bytes 393224 | tf_op jit(solution)/shard_map/ppermute | solution.py:22
  39.5 0.0 collective-permute-done.10.refs_2_
  39.5 0.5 %collective-permute-start.14 = (bf16[256,256]{1,0:T(8,128)(2,1)S(1)}, bf16[256,256]{1,0:T(8,128)(2,1)S(1)}, u32[]{:S(2)}, u32[]{:S(2)}) collective-permute-start(bf16[256,256]{1,0:T(8,128)(2,1)S(1)} %collective-permute-done.10.refs_2_), channel_id=1, source_target_pairs={{0,4},{1,5},{2,6},{3,7},{4,0},{5,1},{6,2},{7,3},{8,12},{9,13},{10,... | collective-permute-start | bytes 393224 | tf_op jit(solution)/shard_map/ppermute | solution.py:22
  40.0 0.0 collective-permute-done.11.refs_3_
  40.0 1.8 %collective-permute-start.15 = (bf16[256,256]{1,0:T(8,128)(2,1)S(1)}, bf16[256,256]{1,0:T(8,128)(2,1)S(1)}, u32[]{:S(2)}, u32[]{:S(2)}) collective-permute-start(bf16[256,256]{1,0:T(8,128)(2,1)S(1)} %collective-permute-done.11.refs_3_), channel_id=1, source_target_pairs={{0,4},{1,5},{2,6},{3,7},{4,0},{5,1},{6,2},{7,3},{8,12},{9,13},{10,... | collective-permute-start | bytes 393224 | tf_op jit(solution)/shard_map/ppermute | solution.py:22
  41.8 0.0 collective-permute-done.12.refs_4_
  41.8 0.0 collective-permute-done.13.refs_5_
  41.8 0.0 collective-permute-done.14.refs_6_
  41.8 1.0 %gather_most.1.gathered_ref = bf16[512,256]{1,0:T(8,128)(2,1)S(1)} custom-call(s32[5]{0:T(128)S(1)} %stack.23.ids_ref, bf16[512,1024]{1,0:T(8,128)(2,1)S(1)} %get-tuple-element.22.hot_ref, bf16[256,256]{1,0:T(8,128)(2,1)S(1)} %collective-permute-done.7.refs_0_, bf16[256,256]{1,0:T(8,128)(2,1)S(1)} %collective-permute-done.9.refs_1_, ...), custom_call_target="tpu_custom_call" | custom-call | flops 2300000000 | tf_op jit(solution)/shard_map/gather_most/pallas_call | solution.py:334
  42.8 0.0 collective-permute-done.15.far_ref
  42.8 1.5 %gather_last.1 = bf16[512,256]{1,0:T(8,128)(2,1)} custom-call(s32[5]{0:T(128)S(1)} %stack.23.ids_ref, bf16[512,1024]{1,0:T(8,128)(2,1)S(1)} %get-tuple-element.22.hot_ref, bf16[512,256]{1,0:T(8,128)(2,1)S(1)} %gather_most.1.gathered_ref, bf16[256,256]{1,0:T(8,128)(2,1)S(1)} %collective-permute-done.15.far_ref), custom_call_target="tpu_custom_call" | custom-call | flops 1150000000 | tf_op jit(solution)/shard_map/gather_last/pallas_call | solution.py:343
  (2 shorter events, 0.0 us)
Async XLA Ops:
  0.6 0.8 %copy-start.9 = (s32[512,1]{0,1:T(1,128)S(1)}, s32[512,1]{0,1:T(1,128)}, u32[]{:S(2)}) copy-start(s32[512,1]{0,1:T(1,128)} %param.12) | copy-start | bytes 6148
  0.6 1.8 %collective-permute-start = (s32[4,128]{1,0:T(4,128)}, s32[4,128]{1,0:T(4,128)S(1)}, u32[]{:S(2)}, u32[]{:S(2)}) collective-permute-start(s32[4,128]{1,0:T(4,128)} %bitcast.9), channel_id=1, source_target_pairs={{0,4},{1,5},{2,6},{3,7},{4,0},{5,1},{6,2},{7,3},{8,12},{9,13},{10,... | collective-permute-start | bytes 6152 | tf_op jit(solution)/shard_map/ppermute | solution.py:22
  1.4 1.4 %collective-permute-start.1 = (s32[4,128]{1,0:T(4,128)S(1)}, s32[4,128]{1,0:T(4,128)S(1)}, u32[]{:S(2)}, u32[]{:S(2)}) collective-permute-start(s32[4,128]{1,0:T(4,128)S(1)} %bitcast.11), channel_id=1, source_target_pairs={{0,4},{1,5},{2,6},{3,7},{4,0},{5,1},{6,2},{7,3},{8,12},{9,13},{10,... | collective-permute-start | bytes 6152 | tf_op jit(solution)/shard_map/ppermute | solution.py:22
  2.0 1.7 %collective-permute-start.2 = (bf16[512,256]{1,0:T(8,128)(2,1)}, bf16[512,256]{1,0:T(8,128)(2,1)S(1)}, u32[]{:S(2)}, u32[]{:S(2)}) collective-permute-start(bf16[512,256]{1,0:T(8,128)(2,1)} %state_ref.1), channel_id=1, source_target_pairs={{0,4},{1,5},{2,6},{3,7},{4,0},{5,1},{6,2},{7,3},{8,12},{9,13},{10,... | collective-permute-start | bytes 786440 | tf_op jit(solution)/shard_map/ppermute | solution.py:22
  2.0 0.8 %copy-start.8 = (s32[512,1]{0,1:T(1,128)S(1)}, s32[512,1]{0,1:T(1,128)}, u32[]{:S(2)}) copy-start(s32[512,1]{0,1:T(1,128)} %param.11) | copy-start | bytes 6148
  2.1 1.7 %copy-start.4 = (bf16[512,256]{1,0:T(8,128)(2,1)S(1)}, bf16[512,256]{1,0:T(8,128)(2,1)}, u32[]{:S(2)}) copy-start(bf16[512,256]{1,0:T(8,128)(2,1)} %state_ref.1) | copy-start | bytes 786436
  3.6 12.9 %copy-start = (bf16[1024,512]{1,0:T(8,128)(2,1)S(1)}, bf16[1024,512]{1,0:T(8,128)(2,1)}, u32[]{:S(2)}) copy-start(bf16[1024,512]{1,0:T(8,128)(2,1)} %cloud_ref.3) | copy-start | bytes 3145732
  3.7 12.7 %copy-start.3 = (bf16[768,256]{1,0:T(8,128)(2,1)S(1)}, bf16[768,256]{1,0:T(8,128)(2,1)}, u32[]{:S(2)}) copy-start(bf16[768,256]{1,0:T(8,128)(2,1)} %refs_3_.3) | copy-start | bytes 1179652
  3.7 12.7 %copy-start.5 = (bf16[256,256]{1,0:T(8,128)(2,1)S(1)}, bf16[256,256]{1,0:T(8,128)(2,1)}, u32[]{:S(2)}) copy-start(bf16[256,256]{1,0:T(8,128)(2,1)} %refs_1_.3) | copy-start | bytes 393220
  3.7 12.7 %copy-start.6 = (bf16[256,256]{1,0:T(8,128)(2,1)S(1)}, bf16[256,256]{1,0:T(8,128)(2,1)}, u32[]{:S(2)}) copy-start(bf16[256,256]{1,0:T(8,128)(2,1)} %refs_4_.5) | copy-start | bytes 393220
  3.7 12.7 %copy-start.7 = (bf16[256,128]{1,0:T(8,128)(2,1)S(1)}, bf16[256,128]{1,0:T(8,128)(2,1)}, u32[]{:S(2)}) copy-start(bf16[256,128]{1,0:T(8,128)(2,1)} %refs_5_.5) | copy-start | bytes 196612
  5.0 5.1 %collective-permute-start.4 = (bf16[272,256]{1,0:T(8,128)(2,1)S(1)}, bf16[272,256]{1,0:T(8,128)(2,1)S(1)}, u32[]{:S(2)}, u32[]{:S(2)}) collective-permute-start(bf16[272,256]{1,0:T(8,128)(2,1)S(1)} %get-tuple-element.20), channel_id=1, source_target_pairs={{0,16},{1,17},{2,18},{3,19},{4,20},{5,21},{6,22},{7,23},{8,24},{9,... | collective-permute-start | bytes 417800 | tf_op jit(solution)/shard_map/ppermute | solution.py:22
  5.2 7.3 %collective-permute-start.3 = (bf16[272,256]{1,0:T(8,128)(2,1)S(1)}, bf16[272,256]{1,0:T(8,128)(2,1)S(1)}, u32[]{:S(2)}, u32[]{:S(2)}) collective-permute-start(bf16[272,256]{1,0:T(8,128)(2,1)S(1)} %get-tuple-element.19), channel_id=1, source_target_pairs={{0,8},{1,9},{2,10},{3,11},{4,12},{5,13},{6,14},{7,15},{8,0},{9,1},... | collective-permute-start | bytes 417800 | tf_op jit(solution)/shard_map/ppermute | solution.py:22
  6.6 7.4 %collective-permute-start.5 = (bf16[272,256]{1,0:T(8,128)(2,1)S(1)}, bf16[272,256]{1,0:T(8,128)(2,1)S(1)}, u32[]{:S(2)}, u32[]{:S(2)}) collective-permute-start(bf16[272,256]{1,0:T(8,128)(2,1)S(1)} %get-tuple-element.21), channel_id=1, source_target_pairs={{0,24},{1,25},{2,26},{3,27},{4,28},{5,29},{6,30},{7,31},{8,16},{9,... | collective-permute-start | bytes 417800 | tf_op jit(solution)/shard_map/ppermute | solution.py:22
  10.1 6.4 %copy-start.1 = (bf16[768,256]{1,0:T(8,128)(2,1)S(1)}, bf16[768,256]{1,0:T(8,128)(2,1)}, u32[]{:S(2)}) copy-start(bf16[768,256]{1,0:T(8,128)(2,1)} %refs_0_.3) | copy-start | bytes 1179652
  10.1 6.4 %copy-start.2 = (bf16[256,768]{1,0:T(8,128)(2,1)S(1)}, bf16[256,768]{1,0:T(8,128)(2,1)}, u32[]{:S(2)}) copy-start(bf16[256,768]{1,0:T(8,128)(2,1)} %refs_2_.3) | copy-start | bytes 1179652
  10.1 9.5 %collective-permute-start.6 = (bf16[272,256]{1,0:T(8,128)(2,1)S(1)}, bf16[272,256]{1,0:T(8,128)(2,1)S(1)}, u32[]{:S(2)}, u32[]{:S(2)}) collective-permute-start(bf16[272,256]{1,0:T(8,128)(2,1)S(1)} %broadcast_select_fusion.1), channel_id=1, source_target_pairs={{0,2},{1,3},{2,0},{3,1},{4,6},{5,7},{6,4},{7,5},{8,10},{9,11},{10,... | collective-permute-start | bytes 417800 | tf_op jit(solution)/shard_map/ppermute | solution.py:22
  14.1 10.5 %collective-permute-start.8 = (bf16[272,256]{1,0:T(8,128)(2,1)S(1)}, bf16[272,256]{1,0:T(8,128)(2,1)S(1)}, u32[]{:S(2)}, u32[]{:S(2)}) collective-permute-start(bf16[272,256]{1,0:T(8,128)(2,1)S(1)} %broadcast_select_fusion), channel_id=1, source_target_pairs={{0,2},{1,3},{2,0},{3,1},{4,6},{5,7},{6,4},{7,5},{8,10},{9,11},{10,... | collective-permute-start | bytes 417800 | tf_op jit(solution)/shard_map/ppermute | solution.py:22
  21.0 8.3 %collective-permute-start.7 = (bf16[256,256]{1,0:T(8,128)(2,1)S(1)}, bf16[256,256]{1,0:T(8,128)(2,1)S(1)}, u32[]{:S(2)}, u32[]{:S(2)}) collective-permute-start(bf16[256,256]{1,0:T(8,128)(2,1)S(1)} %get-tuple-element.24), channel_id=1, source_target_pairs={{0,18},{1,19},{2,16},{3,17},{4,22},{5,23},{6,20},{7,21},{8,26},{9,... | collective-permute-start | bytes 393224 | tf_op jit(solution)/shard_map/ppermute | solution.py:22
  21.4 13.5 %collective-permute-start.9 = (bf16[256,256]{1,0:T(8,128)(2,1)S(1)}, bf16[256,256]{1,0:T(8,128)(2,1)S(1)}, u32[]{:S(2)}, u32[]{:S(2)}) collective-permute-start(bf16[256,256]{1,0:T(8,128)(2,1)S(1)} %get-tuple-element.30), channel_id=1, source_target_pairs={{0,0},{1,1},{2,2},{3,3},{4,4},{5,5},{6,6},{7,7},{8,8},{9,9},{10,10... | collective-permute-start | bytes 393224 | tf_op jit(solution)/shard_map/ppermute | solution.py:22
  25.9 13.6 %collective-permute-start.10 = (bf16[256,256]{1,0:T(8,128)(2,1)S(1)}, bf16[256,256]{1,0:T(8,128)(2,1)S(1)}, u32[]{:S(2)}, u32[]{:S(2)}) collective-permute-start(bf16[256,256]{1,0:T(8,128)(2,1)S(1)} %get-tuple-element.31), channel_id=1, source_target_pairs={{0,26},{1,27},{2,24},{3,25},{4,30},{5,31},{6,28},{7,29},{8,18},{9,... | collective-permute-start | bytes 393224 | tf_op jit(solution)/shard_map/ppermute | solution.py:22
  27.1 12.9 %collective-permute-start.11 = (bf16[256,256]{1,0:T(8,128)(2,1)S(1)}, bf16[256,256]{1,0:T(8,128)(2,1)S(1)}, u32[]{:S(2)}, u32[]{:S(2)}) collective-permute-start(bf16[256,256]{1,0:T(8,128)(2,1)S(1)} %get-tuple-element.32), channel_id=1, source_target_pairs={{0,8},{1,9},{2,10},{3,11},{4,12},{5,13},{6,14},{7,15},{8,0},{9,1},... | collective-permute-start | bytes 393224 | tf_op jit(solution)/shard_map/ppermute | solution.py:22
  29.3 12.5 %collective-permute-start.12 = (bf16[256,256]{1,0:T(8,128)(2,1)S(1)}, bf16[256,256]{1,0:T(8,128)(2,1)S(1)}, u32[]{:S(2)}, u32[]{:S(2)}) collective-permute-start(bf16[256,256]{1,0:T(8,128)(2,1)S(1)} %collective-permute-done.7.refs_0_), channel_id=1, source_target_pairs={{0,4},{1,5},{2,6},{3,7},{4,0},{5,1},{6,2},{7,3},{8,12},{9,13},{10,... | collective-permute-start | bytes 393224 | tf_op jit(solution)/shard_map/ppermute | solution.py:22
  34.9 6.9 %collective-permute-start.13 = (bf16[256,256]{1,0:T(8,128)(2,1)S(1)}, bf16[256,256]{1,0:T(8,128)(2,1)S(1)}, u32[]{:S(2)}, u32[]{:S(2)}) collective-permute-start(bf16[256,256]{1,0:T(8,128)(2,1)S(1)} %collective-permute-done.9.refs_1_), channel_id=1, source_target_pairs={{0,4},{1,5},{2,6},{3,7},{4,0},{5,1},{6,2},{7,3},{8,12},{9,13},{10,... | collective-permute-start | bytes 393224 | tf_op jit(solution)/shard_map/ppermute | solution.py:22
  39.5 2.3 %collective-permute-start.14 = (bf16[256,256]{1,0:T(8,128)(2,1)S(1)}, bf16[256,256]{1,0:T(8,128)(2,1)S(1)}, u32[]{:S(2)}, u32[]{:S(2)}) collective-permute-start(bf16[256,256]{1,0:T(8,128)(2,1)S(1)} %collective-permute-done.10.refs_2_), channel_id=1, source_target_pairs={{0,4},{1,5},{2,6},{3,7},{4,0},{5,1},{6,2},{7,3},{8,12},{9,13},{10,... | collective-permute-start | bytes 393224 | tf_op jit(solution)/shard_map/ppermute | solution.py:22
  40.0 2.8 %collective-permute-start.15 = (bf16[256,256]{1,0:T(8,128)(2,1)S(1)}, bf16[256,256]{1,0:T(8,128)(2,1)S(1)}, u32[]{:S(2)}, u32[]{:S(2)}) collective-permute-start(bf16[256,256]{1,0:T(8,128)(2,1)S(1)} %collective-permute-done.11.refs_3_), channel_id=1, source_target_pairs={{0,4},{1,5},{2,6},{3,7},{4,0},{5,1},{6,2},{7,3},{8,12},{9,13},{10,... | collective-permute-start | bytes 393224 | tf_op jit(solution)/shard_map/ppermute | solution.py:22

commit v5 on v4

v5 whole, which is shorter than its diff:
```python
import functools

import jax
import jax.numpy as jnp
from jax import lax
from jax.experimental import pallas as pl
from jax.experimental.pallas import tpu as pltpu
from jax.sharding import PartitionSpec as P

VMEM_BYTES = 24 * 1024 * 1024
FLAG_ROWS = 16


def moved(block, target):
    groups, bands = lax.axis_size("elem"), lax.axis_size("band")
    route = []
    for e in range(groups):
        for b in range(bands):
            to = target(e, b)
            if to is not None:
                route.append((e * bands + b, to[0] * bands + to[1]))
    return lax.ppermute(block, ("elem", "band"), route)


def work(microseconds):
    return pl.CostEstimate(flops=int(microseconds * 1.15e9), bytes_accessed=0, transcendentals=0)


def position():
    elem, half = lax.axis_index("elem"), lax.axis_size("elem") // 4
    unit = elem // 2
    return elem % 2, unit, unit // half, unit % half


def dot(a, b):
    return jnp.dot(a, b, preferred_element_type=jnp.float32)


def as_row(table):
    return jnp.concatenate([table[r : r + 1, :] for r in range(table.shape[0])], axis=1)


def orders(dest, groups):
    count = dest.shape[1]
    lanes = 128
    hot = (lax.broadcasted_iota(jnp.int32, (groups, count), 0) == dest).astype(jnp.float32)
    before = (
        lax.broadcasted_iota(jnp.int32, (lanes, lanes), 0)
        < lax.broadcasted_iota(jnp.int32, (lanes, lanes), 1)
    ).astype(jnp.bfloat16)
    parts, seen = [], jnp.zeros((groups, 1), jnp.float32)
    for start in range(0, count, lanes):
        piece = hot[:, start : start + lanes]
        inside = dot(piece.astype(jnp.bfloat16), before)
        parts.append(jnp.sum(piece * (inside + seen), axis=0, keepdims=True))
        seen = seen + jnp.sum(piece, axis=1, keepdims=True)
    return jnp.concatenate(parts, axis=1).astype(jnp.int32)


def targets_kernel(groups, cap, dest_ref, far_dest_ref, out_ref):
    core, unit, _, _ = position()
    rows = []
    for dest_table in (dest_ref, far_dest_ref):
        dest = as_row(dest_table[...])
        order = orders(dest, groups)
        step = lax.bitwise_xor(lax.shift_right_logical(dest, 1), jnp.full_like(dest, unit))
        rows += [jnp.where(lax.bitwise_and(dest, 1) == core, step * cap + order, -1), dest, order, dest]
    out_ref[...] = jnp.concatenate(rows, axis=0)


def place_kernel(cap, units, first_du, targets_ref, state_ref, far_state_ref, day_ref, far_day_ref, *refs):
    core, _, _, _ = position()
    out_refs = refs if len(refs) == 1 else refs[1:]
    count = len(out_refs) * cap
    columns, features = state_ref.shape
    flags = []
    for far, (rows, day_table) in enumerate(((state_ref, day_ref), (far_state_ref, far_day_ref))):
        source_core = core if far == 0 else 1 - core
        row, day = targets_ref[4 * far : 4 * far + 1, :], as_row(day_table[...])
        row = jnp.where(row < first_du * cap, jnp.where(row < 0, row, row + units * cap), row) - first_du * cap
        hot = (lax.broadcasted_iota(jnp.int32, (count, columns), 0) == row).astype(jnp.bfloat16)
        sun = jnp.broadcast_to(day.astype(jnp.float32), (FLAG_ROWS, columns)).astype(jnp.bfloat16)
        flags.append(
            lax.dot_general(sun, hot, (((1,), (1,)), ((), ())), preferred_element_type=jnp.float32)
        )
        placed = dot(hot, rows[...]).astype(jnp.bfloat16)
        for i, out_ref in enumerate(out_refs):
            out_ref[pl.ds(pl.multiple_of(source_core * cap, cap), cap), :] = placed[i * cap : (i + 1) * cap, :]
    first = jnp.where(core == 0, flags[0], flags[1]).astype(jnp.bfloat16)
    second = jnp.where(core == 0, flags[1], flags[0]).astype(jnp.bfloat16)
    middle = features // 2
    for i, out_ref in enumerate(out_refs):
        if cap < middle:
            out_ref[2 * cap :, :] = jnp.zeros((FLAG_ROWS, features), jnp.bfloat16)
        out_ref[2 * cap :, 0:cap] = first[:, i * cap : (i + 1) * cap]
        out_ref[2 * cap :, middle : middle + cap] = second[:, i * cap : (i + 1) * cap]


def silu(v):
    return (0.5 * v) * (1.0 + jnp.tanh(0.5 * v))


def as_column(row, cap):
    same = lax.broadcasted_iota(jnp.int32, (cap, cap), 0) == lax.broadcasted_iota(jnp.int32, (cap, cap), 1)
    return jnp.sum(jnp.where(same, jnp.broadcast_to(row, (cap, cap)), 0.0), axis=1, keepdims=True)


def cloud_part(cloud, weights, features):
    return [dot(cloud, weights[i][features:, :]) for i in (0, 3)]


def serve(cap, packet, cloud, first, weights):
    conv_in, conv_mid, conv_out, rad_in, rad_mid, rad_out = weights
    features, levels = packet.shape[1], rad_out.shape[1]
    state = packet[0 : 2 * cap, :]
    conv = silu(dot(state, conv_in[:features, :]) + first[0]).astype(jnp.bfloat16)
    rad = silu(dot(state, rad_in[:features, :]) + first[1]).astype(jnp.bfloat16)
    conv = silu(dot(conv, conv_mid[...])).astype(jnp.bfloat16)
    rad = silu(dot(rad, rad_mid[...])).astype(jnp.bfloat16)
    conv = dot(conv, conv_out[...])
    rad = dot(rad, rad_out[...])
    updated = (cloud.astype(jnp.float32) + conv[:, 2 * levels :]).astype(jnp.bfloat16)
    flags = packet[2 * cap : 2 * cap + FLAG_ROWS, :].astype(jnp.float32)[0:1, :]
    middle = features // 2
    day = jnp.concatenate(
        [as_column(flags[:, 0:cap], cap), as_column(flags[:, middle : middle + cap], cap)], axis=0
    )
    heated = conv[:, :levels] + day * rad
    return jnp.concatenate([heated, conv[:, levels : 2 * levels]], axis=1).astype(jnp.bfloat16), updated


def rows_of(unit, cap):
    return pl.ds(pl.multiple_of(unit * 2 * cap, 2 * cap), 2 * cap)


def lower_kernel(cap, base, pick, low, targets_ref, *refs):
    near, cross, cloud_ref, weights, refs = refs[0:2], refs[2:4], refs[4], refs[5:11], refs[11 + base :]
    answers, new_ref, firsts, refs = refs[0:2], refs[2], refs[3:5], refs[5:]
    core, unit, upper, inner = position()
    half = lax.axis_size("elem") // 4
    packet_ref, updated_ref, sems = refs[-3:]
    copies = []
    for i in range(2):

        @pl.when(upper == 0)
        def _():
            packet_ref[...] = near[i][...]

        @pl.when(upper == 1)
        def _():
            packet_ref[...] = cross[i][...]

        served = rows_of(lax.bitwise_xor(inner, low + i), cap)
        cloud = cloud_ref[served, :]
        answers[i][...], updated_ref[i] = serve(cap, packet_ref, cloud, cloud_part(cloud, weights, packet_ref.shape[1]), weights)
        copies.append(pltpu.make_async_copy(updated_ref.at[i], new_ref.at[served, :], sems.at[i]))
        copies[-1].start()
    for i, first_ref in enumerate(firsts):
        cloud = cloud_ref[rows_of(half + lax.bitwise_xor(inner, low + i), cap), :]
        for j, part in enumerate(cloud_part(cloud, weights, packet_ref.shape[1])):
            first_ref[j] = part
    if pick:
        hot_ref = refs[0]
        table = jnp.transpose(targets_ref[...].astype(jnp.float32)).astype(jnp.int32)
        dest, order = table[:, 1:2], table[:, 2:3]
        step = lax.bitwise_xor(lax.shift_right_logical(dest, 1), jnp.full_like(dest, unit))
        side = jnp.where(lax.bitwise_and(dest, 1) == core, 0, 1)
        row = (step * 2 + side) * cap + order
        hot_ref[...] = (lax.broadcasted_iota(jnp.int32, hot_ref.shape, 1) == row).astype(jnp.bfloat16)
    for copy in copies:
        copy.wait()


def upper_kernel(cap, low, lent_ref, lower_answer_ref, first_ref, cloud_ref, *refs):
    weights, (straight_ref, crossed_ref, new_ref) = refs[:6], refs[6:]
    _, _, upper, inner = position()
    upper_unit = lax.axis_size("elem") // 4 + lax.bitwise_xor(inner, low)
    answer, new_ref[...] = serve(cap, lent_ref, cloud_ref[rows_of(upper_unit, cap), :], first_ref, weights)

    @pl.when(upper == 0)
    def _():
        crossed_ref[...] = answer
        straight_ref[...] = lower_answer_ref[...]

    @pl.when(upper == 1)
    def _():
        straight_ref[...] = answer
        crossed_ref[...] = lower_answer_ref[...]


def store_kernel(cap, *refs):
    news, (new_ref, sems) = refs[:-3], refs[-2:]
    _, _, _, inner = position()
    copies = []
    for low, piece in enumerate(news):
        served = lax.axis_size("elem") // 4 + lax.bitwise_xor(inner, low)
        copies.append(pltpu.make_async_copy(piece, new_ref.at[rows_of(served, cap), :], sems.at[low]))
        copies[-1].start()
    for copy in copies:
        copy.wait()


def gathered(cap, hot_ref, pieces):
    total = None
    for place, blocks in pieces:
        block = blocks[0] if len(blocks) == 1 else jnp.concatenate(blocks, axis=0)
        part = dot(hot_ref[:, place * cap : (place + len(blocks)) * cap], block)
        total = part if total is None else total + part
    return total


def gather_kernel(cap, sequence, hot_ref, *refs):
    count = len(sequence)
    own, far, out_ref = refs[:count], refs[count:-1], refs[-1]
    rows = pl.ds(pl.multiple_of(position()[0] * cap, cap), cap)
    pieces = []
    for i, du in enumerate(sequence):
        blocks = [own[i][rows, :]] + ([far[i][rows, :]] if i < count - 1 else [])
        pieces.append((2 * du, blocks))
    out_ref[...] = gathered(cap, hot_ref, pieces).astype(jnp.bfloat16)


def finish_kernel(cap, last, hot_ref, gathered_ref, far_ref, out_ref, buffer_ref, sems):
    block = far_ref[pl.ds(pl.multiple_of(position()[0] * cap, cap), cap), :]
    parts = sems.shape[0]
    step = out_ref.shape[0] // parts
    copies = []
    for i in range(parts):
        span = pl.ds(i * step, step)
        part = dot(hot_ref[span, (2 * last + 1) * cap : (2 * last + 2) * cap], block)
        buffer_ref[span, :] = (gathered_ref[span, :].astype(jnp.float32) + part).astype(jnp.bfloat16)
        copies.append(pltpu.make_async_copy(buffer_ref.at[span, :], out_ref.at[span, :], sems.at[i]))
        copies[-1].start()
    for copy in copies:
        copy.wait()


def per_device(state, dest_map, day_mask, cloud, conv_in, conv_mid, conv_out, rad_in, rad_mid, rad_out):
    groups, bands = lax.axis_size("elem"), lax.axis_size("band")
    units, half, away = groups // 2, groups // 4, bands // 2
    cap = cloud.shape[0] // groups
    columns, features = state.shape
    elem = lax.axis_index("elem")
    upper = elem // (groups // 2)
    vmem = pl.BlockSpec(memory_space=pltpu.VMEM)
    hbm = pl.BlockSpec(memory_space=pltpu.HBM)
    params = pltpu.CompilerParams(vmem_limit_bytes=VMEM_BYTES)
    weights = (conv_in, conv_mid, conv_out, rad_in, rad_mid, rad_out)

    def like(a):
        return jax.ShapeDtypeStruct(a.shape, a.dtype)

    def swapped(block):
        return moved(block, lambda e, b: (e ^ 1, b))

    dest_table, day_table = dest_map.reshape(columns // 128, 128), day_mask.reshape(columns // 128, 128)
    far_state = swapped(state)
    far_dest, far_day = swapped(dest_table), swapped(day_table)

    packet = jax.ShapeDtypeStruct((2 * cap + FLAG_ROWS, features), jnp.bfloat16)
    targets = pl.pallas_call(
        functools.partial(targets_kernel, groups, cap),
        out_shape=jax.ShapeDtypeStruct((8, columns), jnp.int32),
        in_specs=[vmem] * 2,
        out_specs=vmem,
        compiler_params=params,
        cost_estimate=work(4),
        name="column_targets",
    )(dest_table, far_dest)
    packets = [None] * units
    for chosen in ([half], [*range(half + 1, units), *range(half)]):
        earlier = [packets[half]] if packets[half] is not None else []
        outs = pl.pallas_call(
            functools.partial(place_kernel, cap, units, chosen[0]),
            out_shape=[packet] * len(chosen),
            in_specs=[vmem] * (5 + len(earlier)),
            out_specs=[vmem] * len(chosen),
            compiler_params=params,
            cost_estimate=work(3),
            name="place_columns",
        )(targets, state, far_state, day_table, far_day, *earlier)
        for du, out in zip(chosen, outs):
            packets[du] = out

    came = [packets[0]] + [None] * (units - 1)
    for low in range(half):
        for du in (half + low, low):
            if du:
                came[du] = moved(packets[du], lambda e, b: (e ^ (2 * du), b))
    lent = []
    for low in range(half):
        leaving = jnp.where(upper == 0, came[half + low], came[low])
        lent.append(moved(leaving, lambda e, b: (e, (b + away) % bands)))

    tile = jax.ShapeDtypeStruct((2 * cap, features), jnp.bfloat16)
    new_tile = jax.ShapeDtypeStruct((2 * cap, cloud.shape[1]), jnp.bfloat16)
    first_shape = jax.ShapeDtypeStruct((2, 2 * cap, conv_in.shape[1]), jnp.float32)
    firsts = []
    hot_shape = jax.ShapeDtypeStruct((columns, groups * cap), jnp.bfloat16)
    packet_buffer = pltpu.VMEM(packet.shape, jnp.bfloat16)
    answers, lower_answers, news, new_cloud = [None] * units, [], [], None
    for low in range(0, half, 2):
        pick, base = low == 0, () if low == 0 else (new_cloud,)
        outs = pl.pallas_call(
            functools.partial(lower_kernel, cap, len(base), pick, low),
            out_shape=[tile, tile, like(cloud), first_shape, first_shape] + [hot_shape] * pick,
            in_specs=[vmem] * 12 + [hbm] * len(base),
            out_specs=[vmem, vmem, hbm, vmem, vmem] + [vmem] * pick,
            scratch_shapes=[packet_buffer, pltpu.VMEM((2,) + new_tile.shape, jnp.bfloat16), pltpu.SemaphoreType.DMA((2,))],
            input_output_aliases={12: 2} if base else {},
            compiler_params=params,
            cost_estimate=work(4),
            name="lower_physics",
        )(targets, came[low], came[low + 1], came[half + low], came[half + low + 1], cloud, *weights, *base)
        lower_answers += outs[0:2]
        new_cloud = outs[2]
        firsts += outs[3:5]
        if pick:
            hot = outs[5]
    for low in range(half):
        answers[low], answers[half + low], new = pl.pallas_call(
            functools.partial(upper_kernel, cap, low),
            out_shape=[tile, tile, new_tile],
            in_specs=[vmem] * 10,
            out_specs=[vmem] * 3,
            compiler_params=params,
            cost_estimate=work(3),
            name="upper_physics",
        )(lent[low], lower_answers[low], firsts[low], cloud, *weights)
        news.append(new)

    def home(du):
        def target(e, b):
            to_elem = e ^ (2 * du)
            return to_elem, (b + away) % bands if to_elem >= groups // 2 else b

        return target

    back = [None] * units
    sequence = [du for low in range(half) for du in (half + low, low)]
    back = [moved(answers[du], home(du)) for du in sequence]
    new_cloud = pl.pallas_call(
        functools.partial(store_kernel, cap),
        out_shape=like(cloud),
        in_specs=[vmem] * half + [hbm],
        out_specs=hbm,
        scratch_shapes=[pltpu.SemaphoreType.DMA((half,))],
        input_output_aliases={half: 0},
        compiler_params=params,
        cost_estimate=work(1),
        name="store_cloud",
    )(*news, new_cloud)
    back[0], new_cloud = lax.optimization_barrier((back[0], new_cloud))
    far_back = [swapped(block) for block in back]
    most = pl.pallas_call(
        functools.partial(gather_kernel, cap, sequence),
        out_shape=like(state),
        in_specs=[vmem] * (2 * units),
        out_specs=vmem,
        compiler_params=params,
        cost_estimate=work(2),
        name="gather_most",
    )(hot, *back, *far_back[:-1])
    tendency = pl.pallas_call(
        functools.partial(finish_kernel, cap, sequence[-1]),
        out_shape=like(state),
        in_specs=[vmem] * 3,
        out_specs=hbm,
        scratch_shapes=[pltpu.VMEM(state.shape, jnp.bfloat16), pltpu.SemaphoreType.DMA((2,))],
        compiler_params=params,
        cost_estimate=work(1),
        name="gather_last",
    )(hot, most, far_back[-1])
    return (tendency, new_cloud)


def solution(mesh):
    rows = P(("elem", "band"), None)
    return jax.shard_map(
        per_device,
        mesh=mesh,
        in_specs=(rows,) * 4 + (P(),) * 6,
        out_specs=(rows, rows),
        check_vma=False,
    )
```

time: 44.5 us -> 42.4 us (0.953)
  Pallas kernels: 11.6 us -> 6.87 us
  waiting for transfers between devices: 5.91 us -> 7.84 us
  starting transfers between devices: 25.7 us -> 26.3 us
    pallas_call x4 -> x5, Pallas kernels: 7.06 us -> 4.49 us  [the longest x1 2.46 us: per_device(): pl.pallas_call(functools.partial(lower_kernel, cap, len(base), pick, low)...]
    ppermute x16, waiting for transfers between devices: 5.91 us -> 7.84 us  [moved(): return lax.ppermute(block, ('elem', 'band'), route)]
    ppermute x16, starting transfers between devices: 25.7 us -> 26.3 us  [moved(): return lax.ppermute(block, ('elem', 'band'), route)]
    pallas_call x1, Pallas kernels: 0.99 us -> 0.44 us  [per_device(): pl.pallas_call(functools.partial(gather_kernel, cap, sequence), out_shape...]
    pallas_call x1, Pallas kernels: 1.35 us -> 0.8 us  [per_device(): pl.pallas_call(functools.partial(store_kernel, cap), out_shape=like(cloud...]
    pallas_call x1, Pallas kernels: 0.74 us -> 0.2 us  [per_device(): pl.pallas_call(functools.partial(targets_kernel, groups, cap), out_shape=...]
    pallas_call x1, Pallas kernels: 1.48 us -> 0.94 us  [per_device(): pl.pallas_call(functools.partial(finish_kernel, cap, sequence[-1]), out_s...]
  transfers between devices with their start and end apart: 16 -> 16, of which waited for: 6 -> 7; matrix products, arithmetic and copies ran while one was open for 0% -> 0% of each run, Pallas kernels for 20% -> 13%
where the time goes in v5:
time: 42.4 us; the launch traced here: 42.2 us
  starting transfers between devices  26.3 us (62%)
  waiting for transfers between devices  7.84 us (18%)
  Pallas kernels  6.87 us (16%)
  between operations  0.82 us (2%)
    ppermute x16, starting transfers between devices, moved(): return lax.ppermute(block, ('elem', 'band'), route)  26.3 us
    ppermute x16, waiting for transfers between devices, moved(): return lax.ppermute(block, ('elem', 'band'), route)  7.84 us
    pallas_call x1, Pallas kernels, per_device(): pl.pallas_call(functools.partial(lower_kernel, cap, len(base), pick, low)...  2.46 us
    pallas_call x2, Pallas kernels, per_device(): pl.pallas_call(functools.partial(upper_kernel, cap, low), out_shape=[tile...  1.21 us
    pallas_call x1, Pallas kernels, per_device(): pl.pallas_call(functools.partial(finish_kernel, cap, sequence[-1]), out_s...  0.94 us
  transfers between devices with their start and end apart: 16, of which 7 were waited for; matrix products, arithmetic and copies ran while one was open for 0% of the time, Pallas kernels for 13%

profile of v5, /device:TPU:5, one launch (start us, length us, event | category | flops | bytes accessed | tf_op | source)
XLA Modules:
  0.0 42.2 jit_solution(2845306602903041047)
XLA Ops:
  0.6 0.0 copy-start.9
  0.6 0.7 %collective-permute-start = (s32[4,128]{1,0:T(4,128)}, s32[4,128]{1,0:T(4,128)S(1)}, u32[]{:S(2)}, u32[]{:S(2)}) collective-permute-start(s32[4,128]{1,0:T(4,128)} %bitcast.2), channel_id=1, source_target_pairs={{0,4},{1,5},{2,6},{3,7},{4,0},{5,1},{6,2},{7,3},{8,12},{9,13},{10,... | collective-permute-start | bytes 6152 | tf_op jit(solution)/shard_map/ppermute | solution.py:22
  1.4 0.0 copy-done.9
  1.4 0.6 %collective-permute-start.2 = (s32[4,128]{1,0:T(4,128)S(1)}, s32[4,128]{1,0:T(4,128)S(1)}, u32[]{:S(2)}, u32[]{:S(2)}) collective-permute-start(s32[4,128]{1,0:T(4,128)S(1)} %bitcast.4), channel_id=1, source_target_pairs={{0,4},{1,5},{2,6},{3,7},{4,0},{5,1},{6,2},{7,3},{8,12},{9,13},{10,... | collective-permute-start | bytes 6152 | tf_op jit(solution)/shard_map/ppermute | solution.py:22
  2.0 0.0 collective-permute-start.1
  2.0 0.0 copy-start.8
  2.0 0.0 copy-start.4
  2.0 0.4 collective-permute-done.far_dest_ref
  2.4 0.3 copy-done.8
  2.7 0.2 column_targets.1.targets_ref
  2.9 0.0 collective-permute-done.2.far_day_ref
  2.9 0.9 %collective-permute-done.1.far_state_ref = bf16[512,256]{1,0:T(8,128)(2,1)S(1)} collective-permute-done((bf16[512,256]{1,0:T(8,128)(2,1)}, bf16[512,256]{1,0:T(8,128)(2,1)S(1)}, u32[]{:S(2)}, u32[]{:S(2)}) %collective-permute-start.1) | collective-permute-done | bytes 262176 | tf_op jit(solution)/shard_map/ppermute | solution.py:22
  3.7 0.0 copy-done.4
  3.7 0.3 place_columns.2.refs_0_
  4.0 0.0 copy-start
  4.0 0.1 collective-permute-start.4
  4.1 0.0 copy-start.3
  4.1 0.0 copy-start.5
  4.1 0.0 copy-start.6
  4.2 0.0 copy-start.7
  4.2 0.5 %place_columns.3 = (bf16[272,256]{1,0:T(8,128)(2,1)S(1)}, bf16[272,256]{1,0:T(8,128)(2,1)S(1)}, bf16[272,256]{1,0:T(8,128)(2,1)S(1)}) custom-call(s32[8,512]{1,0:T(8,128)S(1)} %column_targets.1.targets_ref, bf16[512,256]{1,0:T(8,128)(2,1)S(1)} %copy-done.4, bf16[512,256]{1,0:T(8,128)(2,1)S(1)} %collective-permute-done.1.far_state_ref, s32[4,128]{1,0:T(4,128)S(1)} %bitcast.6, ...), custom_call_target="tpu_custom_call" | custom-call | flops 3449999872 | tf_op jit(solution)/shard_map/place_columns/pallas_call | solution.py:273
  4.7 1.5 %collective-permute-start.3 = (bf16[272,256]{1,0:T(8,128)(2,1)S(1)}, bf16[272,256]{1,0:T(8,128)(2,1)S(1)}, u32[]{:S(2)}, u32[]{:S(2)}) collective-permute-start(bf16[272,256]{1,0:T(8,128)(2,1)S(1)} %get-tuple-element.20), channel_id=1, source_target_pairs={{0,8},{1,9},{2,10},{3,11},{4,12},{5,13},{6,14},{7,15},{8,0},{9,1},... | collective-permute-start | bytes 417800 | tf_op jit(solution)/shard_map/ppermute | solution.py:22
  6.2 1.2 %collective-permute-start.5 = (bf16[272,256]{1,0:T(8,128)(2,1)S(1)}, bf16[272,256]{1,0:T(8,128)(2,1)S(1)}, u32[]{:S(2)}, u32[]{:S(2)}) collective-permute-start(bf16[272,256]{1,0:T(8,128)(2,1)S(1)} %get-tuple-element.21), channel_id=1, source_target_pairs={{0,24},{1,25},{2,26},{3,27},{4,28},{5,29},{6,30},{7,31},{8,16},{9,... | collective-permute-start | bytes 417800 | tf_op jit(solution)/shard_map/ppermute | solution.py:22
  7.4 1.9 %collective-permute-done.4.refs_2_ = bf16[272,256]{1,0:T(8,128)(2,1)S(1)} collective-permute-done((bf16[272,256]{1,0:T(8,128)(2,1)S(1)}, bf16[272,256]{1,0:T(8,128)(2,1)S(1)}, u32[]{:S(2)}, u32[]{:S(2)}) %collective-permute-start.4) | collective-permute-done | bytes 139296 | tf_op jit(solution)/shard_map/ppermute | solution.py:22
  9.2 0.0 copy-start.1
  9.2 0.0 copy-start.2
  9.3 2.4 %collective-permute-start.6 = (bf16[272,256]{1,0:T(8,128)(2,1)S(1)}, bf16[272,256]{1,0:T(8,128)(2,1)S(1)}, u32[]{:S(2)}, u32[]{:S(2)}) collective-permute-start(bf16[272,256]{1,0:T(8,128)(2,1)S(1)} %broadcast_select_fusion.1), channel_id=1, source_target_pairs={{0,2},{1,3},{2,0},{3,1},{4,6},{5,7},{6,4},{7,5},{8,10},{9,11},{10,... | collective-permute-start | bytes 417800 | tf_op jit(solution)/shard_map/ppermute | solution.py:22
  11.6 0.0 collective-permute-done.3.refs_1_
  11.6 2.1 %collective-permute-done.5.refs_3_ = bf16[272,256]{1,0:T(8,128)(2,1)S(1)} collective-permute-done((bf16[272,256]{1,0:T(8,128)(2,1)S(1)}, bf16[272,256]{1,0:T(8,128)(2,1)S(1)}, u32[]{:S(2)}, u32[]{:S(2)}) %collective-permute-start.5) | collective-permute-done | bytes 139296 | tf_op jit(solution)/shard_map/ppermute | solution.py:22
  13.7 2.4 %collective-permute-start.8 = (bf16[272,256]{1,0:T(8,128)(2,1)S(1)}, bf16[272,256]{1,0:T(8,128)(2,1)S(1)}, u32[]{:S(2)}, u32[]{:S(2)}) collective-permute-start(bf16[272,256]{1,0:T(8,128)(2,1)S(1)} %broadcast_select_fusion), channel_id=1, source_target_pairs={{0,2},{1,3},{2,0},{3,1},{4,6},{5,7},{6,4},{7,5},{8,10},{9,11},{10,... | collective-permute-start | bytes 417800 | tf_op jit(solution)/shard_map/ppermute | solution.py:22
  16.1 0.0 copy-done
  16.1 0.0 copy-done.3
  16.1 0.0 copy-done.5
  16.1 0.0 copy-done.6
  16.1 0.0 copy-done.7
  16.1 0.0 copy-done.1
  16.1 0.0 copy-done.2
  16.1 2.5 %lower_physics.1 = (bf16[256,256]{1,0:T(8,128)(2,1)S(1)}, bf16[256,256]{1,0:T(8,128)(2,1)S(1)}, bf16[1024,512]{1,0:T(8,128)(2,1)}, f32[2,256,256]{2,1,0:T(8,128)...) custom-call(s32[8,512]{1,0:T(8,128)S(1)} %column_targets.1.targets_ref, ...), custom_call_target="tpu_custom_call" | custom-call | flops 4600000000 | tf_op jit(solution)/shard_map/lower_physics/pallas_call | solution.py:304
  18.6 0.0 collective-permute-done.6.lent_ref
  18.6 0.6 %upper_physics.2 = (bf16[256,256]{1,0:T(8,128)(2,1)S(1)}, bf16[256,256]{1,0:T(8,128)(2,1)S(1)}, bf16[256,512]{1,0:T(8,128)(2,1)S(1)}) custom-call(bf16[272,256]{1,0:T(8,128)(2,1)S(1)} %collective-permute-done.6.lent_ref, bf16[256,256]{1,0:T(8,128)(2,1)S(1)} %get-tuple-element.23.lower_answer_ref, f32[2,256,256]{2,1,0:T(8,128)S(1)} %get-tuple-element.24.first_ref, ...), custom_call_target="tpu_custom_call" | custom-call | flops 3449999872 | tf_op jit(solution)/shard_map/upper_physics/pallas_call | solution.py:321
  19.2 0.4 collective-permute-start.7
  19.6 2.0 %collective-permute-start.9 = (bf16[256,256]{1,0:T(8,128)(2,1)S(1)}, bf16[256,256]{1,0:T(8,128)(2,1)S(1)}, u32[]{:S(2)}, u32[]{:S(2)}) collective-permute-start(bf16[256,256]{1,0:T(8,128)(2,1)S(1)} %get-tuple-element.32), channel_id=1, source_target_pairs={{0,0},{1,1},{2,2},{3,3},{4,4},{5,5},{6,6},{7,7},{8,8},{9,9},{10,10... | collective-permute-start | bytes 393224 | tf_op jit(solution)/shard_map/ppermute | solution.py:22
  21.6 2.1 %collective-permute-done.8.lent_ref = bf16[272,256]{1,0:T(8,128)(2,1)S(1)} collective-permute-done((bf16[272,256]{1,0:T(8,128)(2,1)S(1)}, bf16[272,256]{1,0:T(8,128)(2,1)S(1)}, u32[]{:S(2)}, u32[]{:S(2)}) %collective-permute-start.8) | collective-permute-done | bytes 139296 | tf_op jit(solution)/shard_map/ppermute | solution.py:22
  23.7 0.6 %upper_physics.3 = (bf16[256,256]{1,0:T(8,128)(2,1)S(1)}, bf16[256,256]{1,0:T(8,128)(2,1)S(1)}, bf16[256,512]{1,0:T(8,128)(2,1)S(1)}) custom-call(bf16[272,256]{1,0:T(8,128)(2,1)S(1)} %collective-permute-done.8.lent_ref, bf16[256,256]{1,0:T(8,128)(2,1)S(1)} %get-tuple-element.27.lower_answer_ref, f32[2,256,256]{2,1,0:T(8,128)S(1)} %get-tuple-element.28.first_ref, ...), custom_call_target="tpu_custom_call" | custom-call | flops 3449999872 | tf_op jit(solution)/shard_map/upper_physics/pallas_call | solution.py:321
  24.3 1.2 %collective-permute-start.10 = (bf16[256,256]{1,0:T(8,128)(2,1)S(1)}, bf16[256,256]{1,0:T(8,128)(2,1)S(1)}, u32[]{:S(2)}, u32[]{:S(2)}) collective-permute-start(bf16[256,256]{1,0:T(8,128)(2,1)S(1)} %get-tuple-element.33), channel_id=1, source_target_pairs={{0,26},{1,27},{2,24},{3,25},{4,30},{5,31},{6,28},{7,29},{8,18},{9,... | collective-permute-start | bytes 393224 | tf_op jit(solution)/shard_map/ppermute | solution.py:22
  25.5 0.0 collective-permute-start.11
  25.5 0.8 %store_cloud.1 = bf16[1024,512]{1,0:T(8,128)(2,1)} custom-call(bf16[256,512]{1,0:T(8,128)(2,1)S(1)} %get-tuple-element.26.refs_0_, bf16[256,512]{1,0:T(8,128)(2,1)S(1)} %get-tuple-element.29.refs_1_, bf16[1024,512]{1,0:T(8,128)(2,1)} %get-tuple-element.30.refs_2_), custom_call_target="tpu_custom_call", output_to_operand_aliasing={{}: (2, {})} | custom-call | flops 1150000000 | tf_op jit(solution)/shard_map/store_cloud/pallas_call | solution.py:342
  26.3 0.0 collective-permute-done.7.refs_0_
  26.3 7.9 %collective-permute-start.12 = (bf16[256,256]{1,0:T(8,128)(2,1)S(1)}, bf16[256,256]{1,0:T(8,128)(2,1)S(1)}, u32[]{:S(2)}, u32[]{:S(2)}) collective-permute-start(bf16[256,256]{1,0:T(8,128)(2,1)S(1)} %collective-permute-done.7.refs_0_), channel_id=1, source_target_pairs={{0,4},{1,5},{2,6},{3,7},{4,0},{5,1},{6,2},{7,3},{8,12},{9,13},{10,... | collective-permute-start | bytes 393224 | tf_op jit(solution)/shard_map/ppermute | solution.py:22
  34.2 0.0 collective-permute-done.9.refs_1_
  34.2 2.4 %collective-permute-start.13 = (bf16[256,256]{1,0:T(8,128)(2,1)S(1)}, bf16[256,256]{1,0:T(8,128)(2,1)S(1)}, u32[]{:S(2)}, u32[]{:S(2)}) collective-permute-start(bf16[256,256]{1,0:T(8,128)(2,1)S(1)} %collective-permute-done.9.refs_1_), channel_id=1, source_target_pairs={{0,4},{1,5},{2,6},{3,7},{4,0},{5,1},{6,2},{7,3},{8,12},{9,13},{10,... | collective-permute-start | bytes 393224 | tf_op jit(solution)/shard_map/ppermute | solution.py:22
  36.6 0.0 collective-permute-done.10.refs_2_
  36.6 2.8 %collective-permute-start.14 = (bf16[256,256]{1,0:T(8,128)(2,1)S(1)}, bf16[256,256]{1,0:T(8,128)(2,1)S(1)}, u32[]{:S(2)}, u32[]{:S(2)}) collective-permute-start(bf16[256,256]{1,0:T(8,128)(2,1)S(1)} %collective-permute-done.10.refs_2_), channel_id=1, source_target_pairs={{0,4},{1,5},{2,6},{3,7},{4,0},{5,1},{6,2},{7,3},{8,12},{9,13},{10,... | collective-permute-start | bytes 393224 | tf_op jit(solution)/shard_map/ppermute | solution.py:22
  39.4 0.0 collective-permute-done.11.refs_3_
  39.4 0.8 %collective-permute-start.15 = (bf16[256,256]{1,0:T(8,128)(2,1)S(1)}, bf16[256,256]{1,0:T(8,128)(2,1)S(1)}, u32[]{:S(2)}, u32[]{:S(2)}) collective-permute-start(bf16[256,256]{1,0:T(8,128)(2,1)S(1)} %collective-permute-done.11.refs_3_), channel_id=1, source_target_pairs={{0,4},{1,5},{2,6},{3,7},{4,0},{5,1},{6,2},{7,3},{8,12},{9,13},{10,... | collective-permute-start | bytes 393224 | tf_op jit(solution)/shard_map/ppermute | solution.py:22
  40.3 0.0 collective-permute-done.12.refs_4_
  40.3 0.0 collective-permute-done.13.refs_5_
  40.3 0.1 collective-permute-done.14.refs_6_
  40.4 0.4 %gather_most.1.gathered_ref = bf16[512,256]{1,0:T(8,128)(2,1)S(1)} custom-call(bf16[512,1024]{1,0:T(8,128)(2,1)S(1)} %get-tuple-element.22.hot_ref, bf16[256,256]{1,0:T(8,128)(2,1)S(1)} %collective-permute-done.7.refs_0_, bf16[256,256]{1,0:T(8,128)(2,1)S(1)} %collective-permute-done.9.refs_1_, bf16[256,256]{1,0:T(8,128)(2,1)S(1)} %collective-permute-done.10.refs_2_, ...), custom_call_target="tpu_custom_call" | custom-call | flops 2300000000 | tf_op jit(solution)/shard_map/gather_most/pallas_call | solution.py:355
  40.8 0.4 collective-permute-done.15.far_ref
  41.2 0.9 %gather_last.1 = bf16[512,256]{1,0:T(8,128)(2,1)} custom-call(bf16[512,1024]{1,0:T(8,128)(2,1)S(1)} %get-tuple-element.22.hot_ref, bf16[512,256]{1,0:T(8,128)(2,1)S(1)} %gather_most.1.gathered_ref, bf16[256,256]{1,0:T(8,128)(2,1)S(1)} %collective-permute-done.15.far_ref), custom_call_target="tpu_custom_call" | custom-call | flops 1150000000 | tf_op jit(solution)/shard_map/gather_last/pallas_call | solution.py:364
  (2 shorter events, 0.0 us)
Async XLA Ops:
  0.6 0.8 %copy-start.9 = (s32[512,1]{0,1:T(1,128)S(1)}, s32[512,1]{0,1:T(1,128)}, u32[]{:S(2)}) copy-start(s32[512,1]{0,1:T(1,128)} %param.12) | copy-start | bytes 6148
  0.6 1.8 %collective-permute-start = (s32[4,128]{1,0:T(4,128)}, s32[4,128]{1,0:T(4,128)S(1)}, u32[]{:S(2)}, u32[]{:S(2)}) collective-permute-start(s32[4,128]{1,0:T(4,128)} %bitcast.2), channel_id=1, source_target_pairs={{0,4},{1,5},{2,6},{3,7},{4,0},{5,1},{6,2},{7,3},{8,12},{9,13},{10,... | collective-permute-start | bytes 6152 | tf_op jit(solution)/shard_map/ppermute | solution.py:22
  1.4 1.5 %collective-permute-start.2 = (s32[4,128]{1,0:T(4,128)S(1)}, s32[4,128]{1,0:T(4,128)S(1)}, u32[]{:S(2)}, u32[]{:S(2)}) collective-permute-start(s32[4,128]{1,0:T(4,128)S(1)} %bitcast.4), channel_id=1, source_target_pairs={{0,4},{1,5},{2,6},{3,7},{4,0},{5,1},{6,2},{7,3},{8,12},{9,13},{10,... | collective-permute-start | bytes 6152 | tf_op jit(solution)/shard_map/ppermute | solution.py:22
  2.0 1.7 %collective-permute-start.1 = (bf16[512,256]{1,0:T(8,128)(2,1)}, bf16[512,256]{1,0:T(8,128)(2,1)S(1)}, u32[]{:S(2)}, u32[]{:S(2)}) collective-permute-start(bf16[512,256]{1,0:T(8,128)(2,1)} %state_ref.3), channel_id=1, source_target_pairs={{0,4},{1,5},{2,6},{3,7},{4,0},{5,1},{6,2},{7,3},{8,12},{9,13},{10,... | collective-permute-start | bytes 786440 | tf_op jit(solution)/shard_map/ppermute | solution.py:22
  2.0 0.7 %copy-start.8 = (s32[512,1]{0,1:T(1,128)S(1)}, s32[512,1]{0,1:T(1,128)}, u32[]{:S(2)}) copy-start(s32[512,1]{0,1:T(1,128)} %param.11) | copy-start | bytes 6148
  2.0 1.7 %copy-start.4 = (bf16[512,256]{1,0:T(8,128)(2,1)S(1)}, bf16[512,256]{1,0:T(8,128)(2,1)}, u32[]{:S(2)}) copy-start(bf16[512,256]{1,0:T(8,128)(2,1)} %state_ref.3) | copy-start | bytes 786436
  4.0 12.1 %copy-start = (bf16[1024,512]{1,0:T(8,128)(2,1)S(1)}, bf16[1024,512]{1,0:T(8,128)(2,1)}, u32[]{:S(2)}) copy-start(bf16[1024,512]{1,0:T(8,128)(2,1)} %cloud_ref.3) | copy-start | bytes 3145732
  4.0 5.2 %collective-permute-start.4 = (bf16[272,256]{1,0:T(8,128)(2,1)S(1)}, bf16[272,256]{1,0:T(8,128)(2,1)S(1)}, u32[]{:S(2)}, u32[]{:S(2)}) collective-permute-start(bf16[272,256]{1,0:T(8,128)(2,1)S(1)} %place_columns.2.refs_0_), channel_id=1, source_target_pairs={{0,16},{1,17},{2,18},{3,19},{4,20},{5,21},{6,22},{7,23},{8,24},{9,... | collective-permute-start | bytes 417800 | tf_op jit(solution)/shard_map/ppermute | solution.py:22
  4.1 12.0 %copy-start.3 = (bf16[768,256]{1,0:T(8,128)(2,1)S(1)}, bf16[768,256]{1,0:T(8,128)(2,1)}, u32[]{:S(2)}) copy-start(bf16[768,256]{1,0:T(8,128)(2,1)} %refs_3_.3) | copy-start | bytes 1179652
  4.1 12.0 %copy-start.5 = (bf16[256,256]{1,0:T(8,128)(2,1)S(1)}, bf16[256,256]{1,0:T(8,128)(2,1)}, u32[]{:S(2)}) copy-start(bf16[256,256]{1,0:T(8,128)(2,1)} %refs_1_.3) | copy-start | bytes 393220
  4.1 12.0 %copy-start.6 = (bf16[256,256]{1,0:T(8,128)(2,1)S(1)}, bf16[256,256]{1,0:T(8,128)(2,1)}, u32[]{:S(2)}) copy-start(bf16[256,256]{1,0:T(8,128)(2,1)} %refs_4_.5) | copy-start | bytes 393220
  4.2 12.0 %copy-start.7 = (bf16[256,128]{1,0:T(8,128)(2,1)S(1)}, bf16[256,128]{1,0:T(8,128)(2,1)}, u32[]{:S(2)}) copy-start(bf16[256,128]{1,0:T(8,128)(2,1)} %refs_5_.5) | copy-start | bytes 196612
  4.7 6.9 %collective-permute-start.3 = (bf16[272,256]{1,0:T(8,128)(2,1)S(1)}, bf16[272,256]{1,0:T(8,128)(2,1)S(1)}, u32[]{:S(2)}, u32[]{:S(2)}) collective-permute-start(bf16[272,256]{1,0:T(8,128)(2,1)S(1)} %get-tuple-element.20), channel_id=1, source_target_pairs={{0,8},{1,9},{2,10},{3,11},{4,12},{5,13},{6,14},{7,15},{8,0},{9,1},... | collective-permute-start | bytes 417800 | tf_op jit(solution)/shard_map/ppermute | solution.py:22
  6.2 7.5 %collective-permute-start.5 = (bf16[272,256]{1,0:T(8,128)(2,1)S(1)}, bf16[272,256]{1,0:T(8,128)(2,1)S(1)}, u32[]{:S(2)}, u32[]{:S(2)}) collective-permute-start(bf16[272,256]{1,0:T(8,128)(2,1)S(1)} %get-tuple-element.21), channel_id=1, source_target_pairs={{0,24},{1,25},{2,26},{3,27},{4,28},{5,29},{6,30},{7,31},{8,16},{9,... | collective-permute-start | bytes 417800 | tf_op jit(solution)/shard_map/ppermute | solution.py:22
  9.2 6.9 %copy-start.1 = (bf16[768,256]{1,0:T(8,128)(2,1)S(1)}, bf16[768,256]{1,0:T(8,128)(2,1)}, u32[]{:S(2)}) copy-start(bf16[768,256]{1,0:T(8,128)(2,1)} %refs_0_.3) | copy-start | bytes 1179652
  9.2 6.9 %copy-start.2 = (bf16[256,768]{1,0:T(8,128)(2,1)S(1)}, bf16[256,768]{1,0:T(8,128)(2,1)}, u32[]{:S(2)}) copy-start(bf16[256,768]{1,0:T(8,128)(2,1)} %refs_2_.3) | copy-start | bytes 1179652
  9.3 9.4 %collective-permute-start.6 = (bf16[272,256]{1,0:T(8,128)(2,1)S(1)}, bf16[272,256]{1,0:T(8,128)(2,1)S(1)}, u32[]{:S(2)}, u32[]{:S(2)}) collective-permute-start(bf16[272,256]{1,0:T(8,128)(2,1)S(1)} %broadcast_select_fusion.1), channel_id=1, source_target_pairs={{0,2},{1,3},{2,0},{3,1},{4,6},{5,7},{6,4},{7,5},{8,10},{9,11},{10,... | collective-permute-start | bytes 417800 | tf_op jit(solution)/shard_map/ppermute | solution.py:22
  13.7 10.0 %collective-permute-start.8 = (bf16[272,256]{1,0:T(8,128)(2,1)S(1)}, bf16[272,256]{1,0:T(8,128)(2,1)S(1)}, u32[]{:S(2)}, u32[]{:S(2)}) collective-permute-start(bf16[272,256]{1,0:T(8,128)(2,1)S(1)} %broadcast_select_fusion), channel_id=1, source_target_pairs={{0,2},{1,3},{2,0},{3,1},{4,6},{5,7},{6,4},{7,5},{8,10},{9,11},{10,... | collective-permute-start | bytes 417800 | tf_op jit(solution)/shard_map/ppermute | solution.py:22
  19.2 7.1 %collective-permute-start.7 = (bf16[256,256]{1,0:T(8,128)(2,1)S(1)}, bf16[256,256]{1,0:T(8,128)(2,1)S(1)}, u32[]{:S(2)}, u32[]{:S(2)}) collective-permute-start(bf16[256,256]{1,0:T(8,128)(2,1)S(1)} %get-tuple-element.25), channel_id=1, source_target_pairs={{0,18},{1,19},{2,16},{3,17},{4,22},{5,23},{6,20},{7,21},{8,26},{9,... | collective-permute-start | bytes 393224 | tf_op jit(solution)/shard_map/ppermute | solution.py:22
  19.6 14.6 %collective-permute-start.9 = (bf16[256,256]{1,0:T(8,128)(2,1)S(1)}, bf16[256,256]{1,0:T(8,128)(2,1)S(1)}, u32[]{:S(2)}, u32[]{:S(2)}) collective-permute-start(bf16[256,256]{1,0:T(8,128)(2,1)S(1)} %get-tuple-element.32), channel_id=1, source_target_pairs={{0,0},{1,1},{2,2},{3,3},{4,4},{5,5},{6,6},{7,7},{8,8},{9,9},{10,10... | collective-permute-start | bytes 393224 | tf_op jit(solution)/shard_map/ppermute | solution.py:22
  24.3 12.3 %collective-permute-start.10 = (bf16[256,256]{1,0:T(8,128)(2,1)S(1)}, bf16[256,256]{1,0:T(8,128)(2,1)S(1)}, u32[]{:S(2)}, u32[]{:S(2)}) collective-permute-start(bf16[256,256]{1,0:T(8,128)(2,1)S(1)} %get-tuple-element.33), channel_id=1, source_target_pairs={{0,26},{1,27},{2,24},{3,25},{4,30},{5,31},{6,28},{7,29},{8,18},{9,... | collective-permute-start | bytes 393224 | tf_op jit(solution)/shard_map/ppermute | solution.py:22
  25.5 13.9 %collective-permute-start.11 = (bf16[256,256]{1,0:T(8,128)(2,1)S(1)}, bf16[256,256]{1,0:T(8,128)(2,1)S(1)}, u32[]{:S(2)}, u32[]{:S(2)}) collective-permute-start(bf16[256,256]{1,0:T(8,128)(2,1)S(1)} %get-tuple-element.34), channel_id=1, source_target_pairs={{0,8},{1,9},{2,10},{3,11},{4,12},{5,13},{6,14},{7,15},{8,0},{9,1},... | collective-permute-start | bytes 393224 | tf_op jit(solution)/shard_map/ppermute | solution.py:22
  26.3 13.9 %collective-permute-start.12 = (bf16[256,256]{1,0:T(8,128)(2,1)S(1)}, bf16[256,256]{1,0:T(8,128)(2,1)S(1)}, u32[]{:S(2)}, u32[]{:S(2)}) collective-permute-start(bf16[256,256]{1,0:T(8,128)(2,1)S(1)} %collective-permute-done.7.refs_0_), channel_id=1, source_target_pairs={{0,4},{1,5},{2,6},{3,7},{4,0},{5,1},{6,2},{7,3},{8,12},{9,13},{10,... | collective-permute-start | bytes 393224 | tf_op jit(solution)/shard_map/ppermute | solution.py:22
  34.2 6.0 %collective-permute-start.13 = (bf16[256,256]{1,0:T(8,128)(2,1)S(1)}, bf16[256,256]{1,0:T(8,128)(2,1)S(1)}, u32[]{:S(2)}, u32[]{:S(2)}) collective-permute-start(bf16[256,256]{1,0:T(8,128)(2,1)S(1)} %collective-permute-done.9.refs_1_), channel_id=1, source_target_pairs={{0,4},{1,5},{2,6},{3,7},{4,0},{5,1},{6,2},{7,3},{8,12},{9,13},{10,... | collective-permute-start | bytes 393224 | tf_op jit(solution)/shard_map/ppermute | solution.py:22
  36.6 3.8 %collective-permute-start.14 = (bf16[256,256]{1,0:T(8,128)(2,1)S(1)}, bf16[256,256]{1,0:T(8,128)(2,1)S(1)}, u32[]{:S(2)}, u32[]{:S(2)}) collective-permute-start(bf16[256,256]{1,0:T(8,128)(2,1)S(1)} %collective-permute-done.10.refs_2_), channel_id=1, source_target_pairs={{0,4},{1,5},{2,6},{3,7},{4,0},{5,1},{6,2},{7,3},{8,12},{9,13},{10,... | collective-permute-start | bytes 393224 | tf_op jit(solution)/shard_map/ppermute | solution.py:22
  39.4 1.8 %collective-permute-start.15 = (bf16[256,256]{1,0:T(8,128)(2,1)S(1)}, bf16[256,256]{1,0:T(8,128)(2,1)S(1)}, u32[]{:S(2)}, u32[]{:S(2)}) collective-permute-start(bf16[256,256]{1,0:T(8,128)(2,1)S(1)} %collective-permute-done.11.refs_3_), channel_id=1, source_target_pairs={{0,4},{1,5},{2,6},{3,7},{4,0},{5,1},{6,2},{7,3},{8,12},{9,13},{10,... | collective-permute-start | bytes 393224 | tf_op jit(solution)/shard_map/ppermute | solution.py:22

commit v6 on v5

--- a/solution.py
+++ b/solution.py
@@ -68,7 +68,7 @@
     out_ref[...] = jnp.concatenate(rows, axis=0)
 
 
-def place_kernel(cap, units, first_du, targets_ref, state_ref, far_state_ref, day_ref, far_day_ref, *refs):
+def place_kernel(cap, units, first_du, far_state_ref, state_ref, targets_ref, far_day_ref, day_ref, *refs):
     core, _, _, _ = position()
     out_refs = refs if len(refs) == 1 else refs[1:]
     count = len(out_refs) * cap
@@ -133,42 +133,28 @@
     return pl.ds(pl.multiple_of(unit * 2 * cap, 2 * cap), 2 * cap)
 
 
-def lower_kernel(cap, base, pick, low, targets_ref, *refs):
-    near, cross, cloud_ref, weights, refs = refs[0:2], refs[2:4], refs[4], refs[5:11], refs[11 + base :]
-    answers, new_ref, firsts, refs = refs[0:2], refs[2], refs[3:5], refs[5:]
-    core, unit, upper, inner = position()
-    half = lax.axis_size("elem") // 4
-    packet_ref, updated_ref, sems = refs[-3:]
-    copies = []
-    for i in range(2):
-
-        @pl.when(upper == 0)
-        def _():
-            packet_ref[...] = near[i][...]
-
-        @pl.when(upper == 1)
-        def _():
-            packet_ref[...] = cross[i][...]
-
-        served = rows_of(lax.bitwise_xor(inner, low + i), cap)
-        cloud = cloud_ref[served, :]
-        answers[i][...], updated_ref[i] = serve(cap, packet_ref, cloud, cloud_part(cloud, weights, packet_ref.shape[1]), weights)
-        copies.append(pltpu.make_async_copy(updated_ref.at[i], new_ref.at[served, :], sems.at[i]))
-        copies[-1].start()
-    for i, first_ref in enumerate(firsts):
-        cloud = cloud_ref[rows_of(half + lax.bitwise_xor(inner, low + i), cap), :]
-        for j, part in enumerate(cloud_part(cloud, weights, packet_ref.shape[1])):
-            first_ref[j] = part
+def lower_kernel(cap, base, pick, low, targets_ref, packet_ref, cloud_ref, *refs):
+    weights, refs = refs[:6], refs[6 + base :]
+    (answer_ref, new_ref, first_ref), (updated_ref, sem) = refs[:3], refs[-2:]
+    core, unit, _, inner = position()
+    half, features = lax.axis_size("elem") // 4, packet_ref.shape[1]
+    place = lax.bitwise_xor(inner, low)
+    served = rows_of(place, cap)
+    cloud = cloud_ref[served, :]
+    answer_ref[...], updated_ref[...] = serve(cap, packet_ref, cloud, cloud_part(cloud, weights, features), weights)
+    copy = pltpu.make_async_copy(updated_ref, new_ref.at[served, :], sem)
+    copy.start()
+    for j, part in enumerate(cloud_part(cloud_ref[rows_of(half + place, cap), :], weights, features)):
+        first_ref[j] = part
     if pick:
-        hot_ref = refs[0]
+        hot_ref = refs[3]
         table = jnp.transpose(targets_ref[...].astype(jnp.float32)).astype(jnp.int32)
         dest, order = table[:, 1:2], table[:, 2:3]
         step = lax.bitwise_xor(lax.shift_right_logical(dest, 1), jnp.full_like(dest, unit))
         side = jnp.where(lax.bitwise_and(dest, 1) == core, 0, 1)
         row = (step * 2 + side) * cap + order
         hot_ref[...] = (lax.broadcasted_iota(jnp.int32, hot_ref.shape, 1) == row).astype(jnp.bfloat16)
-    for copy in copies:
-        copy.wait()
+    copy.wait()
 
 
 def upper_kernel(cap, low, lent_ref, lower_answer_ref, first_ref, cloud_ref, *refs):
@@ -209,9 +195,9 @@
     return total
 
 
-def gather_kernel(cap, sequence, hot_ref, *refs):
+def gather_kernel(cap, sequence, *refs):
     count = len(sequence)
-    own, far, out_ref = refs[:count], refs[count:-1], refs[-1]
+    own, far, (hot_ref, out_ref) = refs[:count], refs[count:-2], refs[-2:]
     rows = pl.ds(pl.multiple_of(position()[0] * cap, cap), cap)
     pieces = []
     for i, du in enumerate(sequence):
@@ -220,7 +206,7 @@
     out_ref[...] = gathered(cap, hot_ref, pieces).astype(jnp.bfloat16)
 
 
-def finish_kernel(cap, last, hot_ref, gathered_ref, far_ref, out_ref, buffer_ref, sems):
+def finish_kernel(cap, last, gathered_ref, far_ref, hot_ref, out_ref, buffer_ref, sems):
     block = far_ref[pl.ds(pl.multiple_of(position()[0] * cap, cap), cap), :]
     parts = sems.shape[0]
     step = out_ref.shape[0] // parts
@@ -278,45 +264,41 @@
             compiler_params=params,
             cost_estimate=work(3),
             name="place_columns",
-        )(targets, state, far_state, day_table, far_day, *earlier)
+        )(far_state, state, targets, far_day, day_table, *earlier)
         for du, out in zip(chosen, outs):
             packets[du] = out
 
-    came = [packets[0]] + [None] * (units - 1)
-    for low in range(half):
-        for du in (half + low, low):
-            if du:
-                came[du] = moved(packets[du], lambda e, b: (e ^ (2 * du), b))
-    lent = []
-    for low in range(half):
-        leaving = jnp.where(upper == 0, came[half + low], came[low])
-        lent.append(moved(leaving, lambda e, b: (e, (b + away) % bands)))
+    def onward(low, far):
+        return lambda e, b: (e ^ (2 * low), (b + away * far) % bands)
+
+    hopped = [moved(packets[half + low], onward(half, 0)) for low in range(half)]
+    lent = [moved(jnp.where(upper == 0, hopped[low], packets[low]), onward(low, 1)) for low in range(half)]
+    kept = [jnp.where(upper == 0, packets[low], hopped[low]) for low in range(half)]
+    lower = [kept[low] if low == 0 else moved(kept[low], onward(low, 0)) for low in range(half)]
 
     tile = jax.ShapeDtypeStruct((2 * cap, features), jnp.bfloat16)
     new_tile = jax.ShapeDtypeStruct((2 * cap, cloud.shape[1]), jnp.bfloat16)
     first_shape = jax.ShapeDtypeStruct((2, 2 * cap, conv_in.shape[1]), jnp.float32)
     firsts = []
     hot_shape = jax.ShapeDtypeStruct((columns, groups * cap), jnp.bfloat16)
-    packet_buffer = pltpu.VMEM(packet.shape, jnp.bfloat16)
     answers, lower_answers, news, new_cloud = [None] * units, [], [], None
-    for low in range(0, half, 2):
+    for low in range(half):
         pick, base = low == 0, () if low == 0 else (new_cloud,)
-        outs = pl.pallas_call(
+        answer, new_cloud, first, *picked = pl.pallas_call(
             functools.partial(lower_kernel, cap, len(base), pick, low),
-            out_shape=[tile, tile, like(cloud), first_shape, first_shape] + [hot_shape] * pick,
-            in_specs=[vmem] * 12 + [hbm] * len(base),
-            out_specs=[vmem, vmem, hbm, vmem, vmem] + [vmem] * pick,
-            scratch_shapes=[packet_buffer, pltpu.VMEM((2,) + new_tile.shape, jnp.bfloat16), pltpu.SemaphoreType.DMA((2,))],
-            input_output_aliases={12: 2} if base else {},
+            out_shape=[tile, like(cloud), first_shape] + [hot_shape] * pick,
+            in_specs=[vmem] * 9 + [hbm] * len(base),
+            out_specs=[vmem, hbm, vmem] + [vmem] * pick,
+            scratch_shapes=[pltpu.VMEM(new_tile.shape, jnp.bfloat16), pltpu.SemaphoreType.DMA],
+            input_output_aliases={9: 1} if base else {},
             compiler_params=params,
-            cost_estimate=work(4),
+            cost_estimate=work(3),
             name="lower_physics",
-        )(targets, came[low], came[low + 1], came[half + low], came[half + low + 1], cloud, *weights, *base)
-        lower_answers += outs[0:2]
-        new_cloud = outs[2]
-        firsts += outs[3:5]
+        )(targets, lower[low], cloud, *weights, *base)
+        lower_answers.append(answer)
+        firsts.append(first)
         if pick:
-            hot = outs[5]
+            hot = picked[0]
     for low in range(half):
         answers[low], answers[half + low], new = pl.pallas_call(
             functools.partial(upper_kernel, cap, low),
@@ -360,7 +342,7 @@
         compiler_params=params,
         cost_estimate=work(2),
         name="gather_most",
-    )(hot, *back, *far_back[:-1])
+    )(*back, *far_back[:-1], hot)
     tendency = pl.pallas_call(
         functools.partial(finish_kernel, cap, sequence[-1]),
         out_shape=like(state),
@@ -370,7 +352,7 @@
         compiler_params=params,
         cost_estimate=work(1),
         name="gather_last",
-    )(hot, most, far_back[-1])
+    )(most, far_back[-1], hot)
     return (tendency, new_cloud)
 
 

time: 42.4 us -> 41.8 us (0.986)
  the two profiles are of different devices: /device:TPU:5 before, /device:TPU:13 now
where the time goes in v6:
time: 41.8 us; the launch traced here: 41.6 us
  starting transfers between devices  23.9 us (57%)
  waiting for transfers between devices  8.9 us (21%)
  Pallas kernels  7.62 us (18%)
  between operations  0.83 us (2%)
    ppermute x16, starting transfers between devices, moved(): return lax.ppermute(block, ('elem', 'band'), route)  23.9 us
    ppermute x16, waiting for transfers between devices, moved(): return lax.ppermute(block, ('elem', 'band'), route)  8.9 us
    pallas_call x2, Pallas kernels, per_device(): pl.pallas_call(functools.partial(lower_kernel, cap, len(base), pick, low)...  3.19 us
    pallas_call x2, Pallas kernels, per_device(): pl.pallas_call(functools.partial(upper_kernel, cap, low), out_shape=[tile...  1.21 us
    pallas_call x1, Pallas kernels, per_device(): pl.pallas_call(functools.partial(finish_kernel, cap, sequence[-1]), out_s...  0.95 us
  transfers between devices with their start and end apart: 16, of which 7 were waited for; matrix products, arithmetic and copies ran while one was open for 0% of the time, Pallas kernels for 15%

profile of v6, /device:TPU:13, one launch (start us, length us, event | category | flops | bytes accessed | tf_op | source)
XLA Modules:
  0.0 41.6 jit_solution(15534994555756509365)
XLA Ops:
  0.6 0.0 copy-start.9
  0.6 0.7 %collective-permute-start.1 = (s32[4,128]{1,0:T(4,128)}, s32[4,128]{1,0:T(4,128)S(1)}, u32[]{:S(2)}, u32[]{:S(2)}) collective-permute-start(s32[4,128]{1,0:T(4,128)} %bitcast.2), channel_id=1, source_target_pairs={{0,4},{1,5},{2,6},{3,7},{4,0},{5,1},{6,2},{7,3},{8,12},{9,13},{10,... | collective-permute-start | bytes 6152 | tf_op jit(solution)/shard_map/ppermute | solution.py:22
  1.4 0.1 collective-permute-start
  1.5 0.0 copy-done.9
  1.5 0.5 %collective-permute-start.2 = (s32[4,128]{1,0:T(4,128)S(1)}, s32[4,128]{1,0:T(4,128)S(1)}, u32[]{:S(2)}, u32[]{:S(2)}) collective-permute-start(s32[4,128]{1,0:T(4,128)S(1)} %bitcast.4), channel_id=1, source_target_pairs={{0,4},{1,5},{2,6},{3,7},{4,0},{5,1},{6,2},{7,3},{8,12},{9,13},{10,... | collective-permute-start | bytes 6152 | tf_op jit(solution)/shard_map/ppermute | solution.py:22
  2.0 0.0 copy-start.8
  2.0 0.0 copy-start.4
  2.0 0.4 %collective-permute-done.1.far_dest_ref = s32[4,128]{1,0:T(4,128)S(1)} collective-permute-done((s32[4,128]{1,0:T(4,128)}, s32[4,128]{1,0:T(4,128)S(1)}, u32[]{:S(2)}, u32[]{:S(2)}) %collective-permute-start.1) | collective-permute-done | bytes 2080 | tf_op jit(solution)/shard_map/ppermute | solution.py:22
  2.4 0.3 copy-done.8
  2.7 0.2 column_targets.1.targets_ref
  2.9 0.0 collective-permute-done.2.far_day_ref
  2.9 0.2 collective-permute-done.far_state_ref
  3.1 0.0 copy-done.4
  3.1 0.3 place_columns.2.refs_0_
  3.4 0.3 collective-permute-start.3
  3.7 0.0 copy-start.1
  3.7 0.0 copy-start.2
  3.7 0.0 copy-start.3
  3.7 0.0 copy-start.5
  3.7 0.0 copy-start.6
  3.7 0.5 %place_columns.3 = (bf16[272,256]{1,0:T(8,128)(2,1)S(1)}, bf16[272,256]{1,0:T(8,128)(2,1)S(1)}, bf16[272,256]{1,0:T(8,128)(2,1)S(1)}) custom-call(bf16[512,256]{1,0:T(8,128)(2,1)S(1)} %collective-permute-done.far_state_ref, bf16[512,256]{1,0:T(8,128)(2,1)S(1)} %copy-done.4, s32[8,512]{1,0:T(8,128)S(1)} %column_targets.1.targets_ref, ...), custom_call_target="tpu_custom_call" | custom-call | flops 3449999872 | tf_op jit(solution)/shard_map/place_columns/pallas_call | solution.py:259
  4.3 0.0 copy-start
  4.3 1.3 %collective-permute-start.6 = (bf16[272,256]{1,0:T(8,128)(2,1)S(1)}, bf16[272,256]{1,0:T(8,128)(2,1)S(1)}, u32[]{:S(2)}, u32[]{:S(2)}) collective-permute-start(bf16[272,256]{1,0:T(8,128)(2,1)S(1)} %get-tuple-element.25), channel_id=1, source_target_pairs={{0,16},{1,17},{2,18},{3,19},{4,20},{5,21},{6,22},{7,23},{8,24},{9,... | collective-permute-start | bytes 417800 | tf_op jit(solution)/shard_map/ppermute | solution.py:22
  5.6 3.0 %collective-permute-done.3 = bf16[272,256]{1,0:T(8,128)(2,1)S(1)} collective-permute-done((bf16[272,256]{1,0:T(8,128)(2,1)S(1)}, bf16[272,256]{1,0:T(8,128)(2,1)S(1)}, u32[]{:S(2)}, u32[]{:S(2)}) %collective-permute-start.3) | collective-permute-done | bytes 139296 | tf_op jit(solution)/shard_map/ppermute | solution.py:22
  8.6 2.4 %collective-permute-start.4 = (bf16[272,256]{1,0:T(8,128)(2,1)S(1)}, bf16[272,256]{1,0:T(8,128)(2,1)S(1)}, u32[]{:S(2)}, u32[]{:S(2)}) collective-permute-start(bf16[272,256]{1,0:T(8,128)(2,1)S(1)} %get-tuple-element.41), channel_id=1, source_target_pairs={{0,2},{1,3},{2,0},{3,1},{4,6},{5,7},{6,4},{7,5},{8,10},{9,11},{10,... | collective-permute-start | bytes 417800 | tf_op jit(solution)/shard_map/ppermute | solution.py:22
  11.0 0.6 %collective-permute-done.6 = bf16[272,256]{1,0:T(8,128)(2,1)S(1)} collective-permute-done((bf16[272,256]{1,0:T(8,128)(2,1)S(1)}, bf16[272,256]{1,0:T(8,128)(2,1)S(1)}, u32[]{:S(2)}, u32[]{:S(2)}) %collective-permute-start.6) | collective-permute-done | bytes 139296 | tf_op jit(solution)/shard_map/ppermute | solution.py:22
  11.6 0.0 copy-start.7
  11.6 3.3 %collective-permute-start.7 = (bf16[272,256]{1,0:T(8,128)(2,1)S(1)}, bf16[272,256]{1,0:T(8,128)(2,1)S(1)}, u32[]{:S(2)}, u32[]{:S(2)}) collective-permute-start(bf16[272,256]{1,0:T(8,128)(2,1)S(1)} %get-tuple-element.39), channel_id=1, source_target_pairs={{0,10},{1,11},{2,8},{3,9},{4,14},{5,15},{6,12},{7,13},{8,2},{9,3},... | collective-permute-start | bytes 417800 | tf_op jit(solution)/shard_map/ppermute | solution.py:22
  14.9 0.3 collective-permute-start.8
  15.2 0.0 copy-done.1
  15.2 0.0 copy-done.2
  15.2 0.0 copy-done.3
  15.2 0.0 copy-done.5
  15.2 0.0 copy-done.6
  15.2 0.0 copy-done
  15.2 0.0 copy-done.7
  15.2 1.6 %lower_physics.2 = (bf16[256,256]{1,0:T(8,128)(2,1)S(1)}, bf16[1024,512]{1,0:T(8,128)(2,1)}, f32[2,256,256]{2,1,0:T(8,128)S(1)}, bf16[512,1024]{1,0:T(8,128)(2,1)S(1)}) custom-call(s32[8,512]{1,0:T(8,128)S(1)} %column_targets.1.targets_ref, bf16[272,256]{1,0:T(8,128)(2,1)S(1)} %get-tuple-element.40.packet_ref, bf16[1024,512]{1,0:T(8,128)(2,1)S(1)} %copy-done, ...), custom_call_target="tpu_custom_call" | custom-call | flops 3449999872 | tf_op jit(solution)/shard_map/lower_physics/pallas_call | solution.py:287
  16.9 3.0 %collective-permute-done.4.lent_ref = bf16[272,256]{1,0:T(8,128)(2,1)S(1)} collective-permute-done((bf16[272,256]{1,0:T(8,128)(2,1)S(1)}, bf16[272,256]{1,0:T(8,128)(2,1)S(1)}, u32[]{:S(2)}, u32[]{:S(2)}) %collective-permute-start.4) | collective-permute-done | bytes 139296 | tf_op jit(solution)/shard_map/ppermute | solution.py:22
  19.8 0.6 %upper_physics.2 = (bf16[256,256]{1,0:T(8,128)(2,1)S(1)}, bf16[256,256]{1,0:T(8,128)(2,1)S(1)}, bf16[256,512]{1,0:T(8,128)(2,1)S(1)}) custom-call(bf16[272,256]{1,0:T(8,128)(2,1)S(1)} %collective-permute-done.4.lent_ref, bf16[256,256]{1,0:T(8,128)(2,1)S(1)} %get-tuple-element.21.lower_answer_ref, f32[2,256,256]{2,1,0:T(8,128)S(1)} %get-tuple-element.22.first_ref, ...), custom_call_target="tpu_custom_call" | custom-call | flops 3449999872 | tf_op jit(solution)/shard_map/upper_physics/pallas_call | solution.py:303
  20.4 1.5 %collective-permute-start.5 = (bf16[256,256]{1,0:T(8,128)(2,1)S(1)}, bf16[256,256]{1,0:T(8,128)(2,1)S(1)}, u32[]{:S(2)}, u32[]{:S(2)}) collective-permute-start(bf16[256,256]{1,0:T(8,128)(2,1)S(1)} %get-tuple-element.23), channel_id=1, source_target_pairs={{0,18},{1,19},{2,16},{3,17},{4,22},{5,23},{6,20},{7,21},{8,26},{9,... | collective-permute-start | bytes 393224 | tf_op jit(solution)/shard_map/ppermute | solution.py:22
  22.0 5.1 %collective-permute-start.9 = (bf16[256,256]{1,0:T(8,128)(2,1)S(1)}, bf16[256,256]{1,0:T(8,128)(2,1)S(1)}, u32[]{:S(2)}, u32[]{:S(2)}) collective-permute-start(bf16[256,256]{1,0:T(8,128)(2,1)S(1)} %get-tuple-element.33), channel_id=1, source_target_pairs={{0,0},{1,1},{2,2},{3,3},{4,4},{5,5},{6,6},{7,7},{8,8},{9,9},{10,10... | collective-permute-start | bytes 393224 | tf_op jit(solution)/shard_map/ppermute | solution.py:22
  27.1 0.0 collective-permute-done.8.packet_ref
  27.1 1.6 %lower_physics.3 = (bf16[256,256]{1,0:T(8,128)(2,1)S(1)}, bf16[1024,512]{1,0:T(8,128)(2,1)}, f32[2,256,256]{2,1,0:T(8,128)S(1)}) custom-call(s32[8,512]{1,0:T(8,128)S(1)} %column_targets.1.targets_ref, bf16[272,256]{1,0:T(8,128)(2,1)S(1)} %collective-permute-done.8.packet_ref, bf16[1024,512]{1,0:T(8,128)(2,1)S(1)} %copy-done, ...), custom_call_target="tpu_custom_call", output_to_operand_aliasing={{1}: (9, {})} | custom-call | flops 3449999872 | tf_op jit(solution)/shard_map/lower_physics/pallas_call | solution.py:287
  28.7 0.0 collective-permute-done.7.lent_ref
  28.7 0.6 %upper_physics.3 = (bf16[256,256]{1,0:T(8,128)(2,1)S(1)}, bf16[256,256]{1,0:T(8,128)(2,1)S(1)}, bf16[256,512]{1,0:T(8,128)(2,1)S(1)}) custom-call(bf16[272,256]{1,0:T(8,128)(2,1)S(1)} %collective-permute-done.7.lent_ref, bf16[256,256]{1,0:T(8,128)(2,1)S(1)} %get-tuple-element.28.lower_answer_ref, f32[2,256,256]{2,1,0:T(8,128)S(1)} %get-tuple-element.29.first_ref, ...), custom_call_target="tpu_custom_call" | custom-call | flops 3449999872 | tf_op jit(solution)/shard_map/upper_physics/pallas_call | solution.py:303
  29.3 0.1 collective-permute-start.10
  29.4 0.6 %collective-permute-start.11 = (bf16[256,256]{1,0:T(8,128)(2,1)S(1)}, bf16[256,256]{1,0:T(8,128)(2,1)S(1)}, u32[]{:S(2)}, u32[]{:S(2)}) collective-permute-start(bf16[256,256]{1,0:T(8,128)(2,1)S(1)} %get-tuple-element.35), channel_id=1, source_target_pairs={{0,8},{1,9},{2,10},{3,11},{4,12},{5,13},{6,14},{7,15},{8,0},{9,1},... | collective-permute-start | bytes 393224 | tf_op jit(solution)/shard_map/ppermute | solution.py:22
  30.0 0.8 %store_cloud.1 = bf16[1024,512]{1,0:T(8,128)(2,1)} custom-call(bf16[256,512]{1,0:T(8,128)(2,1)S(1)} %get-tuple-element.24.refs_0_, bf16[256,512]{1,0:T(8,128)(2,1)S(1)} %get-tuple-element.30.refs_1_, bf16[1024,512]{1,0:T(8,128)(2,1)} %get-tuple-element.31.refs_2_), custom_call_target="tpu_custom_call", output_to_operand_aliasing={{}: (2, {})} | custom-call | flops 1150000000 | tf_op jit(solution)/shard_map/store_cloud/pallas_call | solution.py:324
  30.8 0.0 collective-permute-done.5.refs_0_
  30.9 4.4 %collective-permute-start.12 = (bf16[256,256]{1,0:T(8,128)(2,1)S(1)}, bf16[256,256]{1,0:T(8,128)(2,1)S(1)}, u32[]{:S(2)}, u32[]{:S(2)}) collective-permute-start(bf16[256,256]{1,0:T(8,128)(2,1)S(1)} %collective-permute-done.5.refs_0_), channel_id=1, source_target_pairs={{0,4},{1,5},{2,6},{3,7},{4,0},{5,1},{6,2},{7,3},{8,12},{9,13},{10,... | collective-permute-start | bytes 393224 | tf_op jit(solution)/shard_map/ppermute | solution.py:22
  35.2 0.0 collective-permute-done.9.refs_1_
  35.2 0.1 collective-permute-start.13
  35.3 0.7 %collective-permute-done.10.refs_2_ = bf16[256,256]{1,0:T(8,128)(2,1)S(1)} collective-permute-done((bf16[256,256]{1,0:T(8,128)(2,1)S(1)}, bf16[256,256]{1,0:T(8,128)(2,1)S(1)}, u32[]{:S(2)}, u32[]{:S(2)}) %collective-permute-start.10) | collective-permute-done | bytes 131104 | tf_op jit(solution)/shard_map/ppermute | solution.py:22
  36.0 3.2 %collective-permute-start.14 = (bf16[256,256]{1,0:T(8,128)(2,1)S(1)}, bf16[256,256]{1,0:T(8,128)(2,1)S(1)}, u32[]{:S(2)}, u32[]{:S(2)}) collective-permute-start(bf16[256,256]{1,0:T(8,128)(2,1)S(1)} %collective-permute-done.10.refs_2_), channel_id=1, source_target_pairs={{0,4},{1,5},{2,6},{3,7},{4,0},{5,1},{6,2},{7,3},{8,12},{9,13},{10,... | collective-permute-start | bytes 393224 | tf_op jit(solution)/shard_map/ppermute | solution.py:22
  39.2 0.0 collective-permute-done.11.refs_3_
  39.2 0.0 collective-permute-start.15
  39.2 0.0 collective-permute-done.12.refs_4_
  39.2 0.0 collective-permute-done.13.refs_5_
  39.2 1.0 %collective-permute-done.14.refs_6_ = bf16[256,256]{1,0:T(8,128)(2,1)S(1)} collective-permute-done((bf16[256,256]{1,0:T(8,128)(2,1)S(1)}, bf16[256,256]{1,0:T(8,128)(2,1)S(1)}, u32[]{:S(2)}, u32[]{:S(2)}) %collective-permute-start.14) | collective-permute-done | bytes 131104 | tf_op jit(solution)/shard_map/ppermute | solution.py:22
  40.2 0.4 %gather_most.1.gathered_ref = bf16[512,256]{1,0:T(8,128)(2,1)S(1)} custom-call(bf16[256,256]{1,0:T(8,128)(2,1)S(1)} %collective-permute-done.5.refs_0_, bf16[256,256]{1,0:T(8,128)(2,1)S(1)} %collective-permute-done.9.refs_1_, bf16[256,256]{1,0:T(8,128)(2,1)S(1)} %collective-permute-done.10.refs_2_, bf16[256,256]{1,0:T(8,128)(2,1)S(1)} %collective-permute-done.11.refs_3_, ...), custom_call_target="tpu_custom_call" | custom-call | flops 2300000000 | tf_op jit(solution)/shard_map/gather_most/pallas_call | solution.py:337
  40.6 0.0 collective-permute-done.15.far_ref
  40.6 1.0 %gather_last.1 = bf16[512,256]{1,0:T(8,128)(2,1)} custom-call(bf16[512,256]{1,0:T(8,128)(2,1)S(1)} %gather_most.1.gathered_ref, bf16[256,256]{1,0:T(8,128)(2,1)S(1)} %collective-permute-done.15.far_ref, bf16[512,1024]{1,0:T(8,128)(2,1)S(1)} %get-tuple-element.36.refs_7_.hot_ref), custom_call_target="tpu_custom_call" | custom-call | flops 1150000000 | tf_op jit(solution)/shard_map/gather_last/pallas_call | solution.py:346
  (2 shorter events, 0.0 us)
Async XLA Ops:
  0.6 0.8 %copy-start.9 = (s32[512,1]{0,1:T(1,128)S(1)}, s32[512,1]{0,1:T(1,128)}, u32[]{:S(2)}) copy-start(s32[512,1]{0,1:T(1,128)} %param.12) | copy-start | bytes 6148
  0.6 1.8 %collective-permute-start.1 = (s32[4,128]{1,0:T(4,128)}, s32[4,128]{1,0:T(4,128)S(1)}, u32[]{:S(2)}, u32[]{:S(2)}) collective-permute-start(s32[4,128]{1,0:T(4,128)} %bitcast.2), channel_id=1, source_target_pairs={{0,4},{1,5},{2,6},{3,7},{4,0},{5,1},{6,2},{7,3},{8,12},{9,13},{10,... | collective-permute-start | bytes 6152 | tf_op jit(solution)/shard_map/ppermute | solution.py:22
  1.4 1.7 %collective-permute-start = (bf16[512,256]{1,0:T(8,128)(2,1)}, bf16[512,256]{1,0:T(8,128)(2,1)S(1)}, u32[]{:S(2)}, u32[]{:S(2)}) collective-permute-start(bf16[512,256]{1,0:T(8,128)(2,1)} %state_ref.3), channel_id=1, source_target_pairs={{0,4},{1,5},{2,6},{3,7},{4,0},{5,1},{6,2},{7,3},{8,12},{9,13},{10,... | collective-permute-start | bytes 786440 | tf_op jit(solution)/shard_map/ppermute | solution.py:22
  1.5 1.5 %collective-permute-start.2 = (s32[4,128]{1,0:T(4,128)S(1)}, s32[4,128]{1,0:T(4,128)S(1)}, u32[]{:S(2)}, u32[]{:S(2)}) collective-permute-start(s32[4,128]{1,0:T(4,128)S(1)} %bitcast.4), channel_id=1, source_target_pairs={{0,4},{1,5},{2,6},{3,7},{4,0},{5,1},{6,2},{7,3},{8,12},{9,13},{10,... | collective-permute-start | bytes 6152 | tf_op jit(solution)/shard_map/ppermute | solution.py:22
  2.0 0.7 %copy-start.8 = (s32[512,1]{0,1:T(1,128)S(1)}, s32[512,1]{0,1:T(1,128)}, u32[]{:S(2)}) copy-start(s32[512,1]{0,1:T(1,128)} %param.11) | copy-start | bytes 6148
  2.0 1.1 %copy-start.4 = (bf16[512,256]{1,0:T(8,128)(2,1)S(1)}, bf16[512,256]{1,0:T(8,128)(2,1)}, u32[]{:S(2)}) copy-start(bf16[512,256]{1,0:T(8,128)(2,1)} %state_ref.3) | copy-start | bytes 786436
  3.4 5.2 %collective-permute-start.3 = (bf16[272,256]{1,0:T(8,128)(2,1)S(1)}, bf16[272,256]{1,0:T(8,128)(2,1)S(1)}, u32[]{:S(2)}, u32[]{:S(2)}) collective-permute-start(bf16[272,256]{1,0:T(8,128)(2,1)S(1)} %place_columns.2.refs_0_), channel_id=1, source_target_pairs={{0,16},{1,17},{2,18},{3,19},{4,20},{5,21},{6,22},{7,23},{8,24},{9,... | collective-permute-start | bytes 417800 | tf_op jit(solution)/shard_map/ppermute | solution.py:22
  3.7 11.5 %copy-start.1 = (bf16[768,256]{1,0:T(8,128)(2,1)S(1)}, bf16[768,256]{1,0:T(8,128)(2,1)}, u32[]{:S(2)}) copy-start(bf16[768,256]{1,0:T(8,128)(2,1)} %refs_0_.7) | copy-start | bytes 1179652
  3.7 11.5 %copy-start.2 = (bf16[256,768]{1,0:T(8,128)(2,1)S(1)}, bf16[256,768]{1,0:T(8,128)(2,1)}, u32[]{:S(2)}) copy-start(bf16[256,768]{1,0:T(8,128)(2,1)} %refs_2_.7) | copy-start | bytes 1179652
  3.7 11.5 %copy-start.3 = (bf16[768,256]{1,0:T(8,128)(2,1)S(1)}, bf16[768,256]{1,0:T(8,128)(2,1)}, u32[]{:S(2)}) copy-start(bf16[768,256]{1,0:T(8,128)(2,1)} %refs_3_.7) | copy-start | bytes 1179652
  3.7 11.5 %copy-start.5 = (bf16[256,256]{1,0:T(8,128)(2,1)S(1)}, bf16[256,256]{1,0:T(8,128)(2,1)}, u32[]{:S(2)}) copy-start(bf16[256,256]{1,0:T(8,128)(2,1)} %refs_1_.7) | copy-start | bytes 393220
  3.7 11.5 %copy-start.6 = (bf16[256,256]{1,0:T(8,128)(2,1)S(1)}, bf16[256,256]{1,0:T(8,128)(2,1)}, u32[]{:S(2)}) copy-start(bf16[256,256]{1,0:T(8,128)(2,1)} %refs_4_.7) | copy-start | bytes 393220
  4.3 10.9 %copy-start = (bf16[1024,512]{1,0:T(8,128)(2,1)S(1)}, bf16[1024,512]{1,0:T(8,128)(2,1)}, u32[]{:S(2)}) copy-start(bf16[1024,512]{1,0:T(8,128)(2,1)} %cloud_ref.7) | copy-start | bytes 3145732
  4.3 7.3 %collective-permute-start.6 = (bf16[272,256]{1,0:T(8,128)(2,1)S(1)}, bf16[272,256]{1,0:T(8,128)(2,1)S(1)}, u32[]{:S(2)}, u32[]{:S(2)}) collective-permute-start(bf16[272,256]{1,0:T(8,128)(2,1)S(1)} %get-tuple-element.25), channel_id=1, source_target_pairs={{0,16},{1,17},{2,18},{3,19},{4,20},{5,21},{6,22},{7,23},{8,24},{9,... | collective-permute-start | bytes 417800 | tf_op jit(solution)/shard_map/ppermute | solution.py:22
  8.6 11.2 %collective-permute-start.4 = (bf16[272,256]{1,0:T(8,128)(2,1)S(1)}, bf16[272,256]{1,0:T(8,128)(2,1)S(1)}, u32[]{:S(2)}, u32[]{:S(2)}) collective-permute-start(bf16[272,256]{1,0:T(8,128)(2,1)S(1)} %get-tuple-element.41), channel_id=1, source_target_pairs={{0,2},{1,3},{2,0},{3,1},{4,6},{5,7},{6,4},{7,5},{8,10},{9,11},{10,... | collective-permute-start | bytes 417800 | tf_op jit(solution)/shard_map/ppermute | solution.py:22
  11.6 3.6 %copy-start.7 = (bf16[256,128]{1,0:T(8,128)(2,1)S(1)}, bf16[256,128]{1,0:T(8,128)(2,1)}, u32[]{:S(2)}) copy-start(bf16[256,128]{1,0:T(8,128)(2,1)} %refs_5_.7) | copy-start | bytes 196612
  11.6 17.1 %collective-permute-start.7 = (bf16[272,256]{1,0:T(8,128)(2,1)S(1)}, bf16[272,256]{1,0:T(8,128)(2,1)S(1)}, u32[]{:S(2)}, u32[]{:S(2)}) collective-permute-start(bf16[272,256]{1,0:T(8,128)(2,1)S(1)} %get-tuple-element.39), channel_id=1, source_target_pairs={{0,10},{1,11},{2,8},{3,9},{4,14},{5,15},{6,12},{7,13},{8,2},{9,3},... | collective-permute-start | bytes 417800 | tf_op jit(solution)/shard_map/ppermute | solution.py:22
  14.9 12.2 %collective-permute-start.8 = (bf16[272,256]{1,0:T(8,128)(2,1)S(1)}, bf16[272,256]{1,0:T(8,128)(2,1)S(1)}, u32[]{:S(2)}, u32[]{:S(2)}) collective-permute-start(bf16[272,256]{1,0:T(8,128)(2,1)S(1)} %get-tuple-element.38), channel_id=1, source_target_pairs={{0,8},{1,9},{2,10},{3,11},{4,12},{5,13},{6,14},{7,15},{8,0},{9,1},... | collective-permute-start | bytes 417800 | tf_op jit(solution)/shard_map/ppermute | solution.py:22
  20.4 10.4 %collective-permute-start.5 = (bf16[256,256]{1,0:T(8,128)(2,1)S(1)}, bf16[256,256]{1,0:T(8,128)(2,1)S(1)}, u32[]{:S(2)}, u32[]{:S(2)}) collective-permute-start(bf16[256,256]{1,0:T(8,128)(2,1)S(1)} %get-tuple-element.23), channel_id=1, source_target_pairs={{0,18},{1,19},{2,16},{3,17},{4,22},{5,23},{6,20},{7,21},{8,26},{9,... | collective-permute-start | bytes 393224 | tf_op jit(solution)/shard_map/ppermute | solution.py:22
  22.0 13.3 %collective-permute-start.9 = (bf16[256,256]{1,0:T(8,128)(2,1)S(1)}, bf16[256,256]{1,0:T(8,128)(2,1)S(1)}, u32[]{:S(2)}, u32[]{:S(2)}) collective-permute-start(bf16[256,256]{1,0:T(8,128)(2,1)S(1)} %get-tuple-element.33), channel_id=1, source_target_pairs={{0,0},{1,1},{2,2},{3,3},{4,4},{5,5},{6,6},{7,7},{8,8},{9,9},{10,10... | collective-permute-start | bytes 393224 | tf_op jit(solution)/shard_map/ppermute | solution.py:22
  29.3 6.7 %collective-permute-start.10 = (bf16[256,256]{1,0:T(8,128)(2,1)S(1)}, bf16[256,256]{1,0:T(8,128)(2,1)S(1)}, u32[]{:S(2)}, u32[]{:S(2)}) collective-permute-start(bf16[256,256]{1,0:T(8,128)(2,1)S(1)} %get-tuple-element.34), channel_id=1, source_target_pairs={{0,26},{1,27},{2,24},{3,25},{4,30},{5,31},{6,28},{7,29},{8,18},{9,... | collective-permute-start | bytes 393224 | tf_op jit(solution)/shard_map/ppermute | solution.py:22
  29.4 9.8 %collective-permute-start.11 = (bf16[256,256]{1,0:T(8,128)(2,1)S(1)}, bf16[256,256]{1,0:T(8,128)(2,1)S(1)}, u32[]{:S(2)}, u32[]{:S(2)}) collective-permute-start(bf16[256,256]{1,0:T(8,128)(2,1)S(1)} %get-tuple-element.35), channel_id=1, source_target_pairs={{0,8},{1,9},{2,10},{3,11},{4,12},{5,13},{6,14},{7,15},{8,0},{9,1},... | collective-permute-start | bytes 393224 | tf_op jit(solution)/shard_map/ppermute | solution.py:22
  30.9 8.4 %collective-permute-start.12 = (bf16[256,256]{1,0:T(8,128)(2,1)S(1)}, bf16[256,256]{1,0:T(8,128)(2,1)S(1)}, u32[]{:S(2)}, u32[]{:S(2)}) collective-permute-start(bf16[256,256]{1,0:T(8,128)(2,1)S(1)} %collective-permute-done.5.refs_0_), channel_id=1, source_target_pairs={{0,4},{1,5},{2,6},{3,7},{4,0},{5,1},{6,2},{7,3},{8,12},{9,13},{10,... | collective-permute-start | bytes 393224 | tf_op jit(solution)/shard_map/ppermute | solution.py:22
  35.2 4.0 %collective-permute-start.13 = (bf16[256,256]{1,0:T(8,128)(2,1)S(1)}, bf16[256,256]{1,0:T(8,128)(2,1)S(1)}, u32[]{:S(2)}, u32[]{:S(2)}) collective-permute-start(bf16[256,256]{1,0:T(8,128)(2,1)S(1)} %collective-permute-done.9.refs_1_), channel_id=1, source_target_pairs={{0,4},{1,5},{2,6},{3,7},{4,0},{5,1},{6,2},{7,3},{8,12},{9,13},{10,... | collective-permute-start | bytes 393224 | tf_op jit(solution)/shard_map/ppermute | solution.py:22
  36.0 4.2 %collective-permute-start.14 = (bf16[256,256]{1,0:T(8,128)(2,1)S(1)}, bf16[256,256]{1,0:T(8,128)(2,1)S(1)}, u32[]{:S(2)}, u32[]{:S(2)}) collective-permute-start(bf16[256,256]{1,0:T(8,128)(2,1)S(1)} %collective-permute-done.10.refs_2_), channel_id=1, source_target_pairs={{0,4},{1,5},{2,6},{3,7},{4,0},{5,1},{6,2},{7,3},{8,12},{9,13},{10,... | collective-permute-start | bytes 393224 | tf_op jit(solution)/shard_map/ppermute | solution.py:22
  39.2 1.4 %collective-permute-start.15 = (bf16[256,256]{1,0:T(8,128)(2,1)S(1)}, bf16[256,256]{1,0:T(8,128)(2,1)S(1)}, u32[]{:S(2)}, u32[]{:S(2)}) collective-permute-start(bf16[256,256]{1,0:T(8,128)(2,1)S(1)} %collective-permute-done.11.refs_3_), channel_id=1, source_target_pairs={{0,4},{1,5},{2,6},{3,7},{4,0},{5,1},{6,2},{7,3},{8,12},{9,13},{10,... | collective-permute-start | bytes 393224 | tf_op jit(solution)/shard_map/ppermute | solution.py:22

commit v7 on v6

--- a/solution.py
+++ b/solution.py
@@ -68,32 +68,44 @@
     out_ref[...] = jnp.concatenate(rows, axis=0)
 
 
-def place_kernel(cap, units, first_du, far_state_ref, state_ref, targets_ref, far_day_ref, day_ref, *refs):
+def place_kernel(cap, units, chosen, far_state_ref, state_ref, targets_ref, far_day_ref, day_ref, *refs):
     core, _, _, _ = position()
-    out_refs = refs if len(refs) == 1 else refs[1:]
-    count = len(out_refs) * cap
+    half = units // 2
+    split = [du % half == 0 for du in chosen]
+    out_refs = refs[-(len(chosen) + sum(split)) :]
     columns, features = state_ref.shape
-    flags = []
-    for far, (rows, day_table) in enumerate(((state_ref, day_ref), (far_state_ref, far_day_ref))):
-        source_core = core if far == 0 else 1 - core
-        row, day = targets_ref[4 * far : 4 * far + 1, :], as_row(day_table[...])
-        row = jnp.where(row < first_du * cap, jnp.where(row < 0, row, row + units * cap), row) - first_du * cap
-        hot = (lax.broadcasted_iota(jnp.int32, (count, columns), 0) == row).astype(jnp.bfloat16)
+    middle = features // 2
+    placed, flags = [], []
+    for rows, dest_row, day_table in ((state_ref, 0, day_ref), (far_state_ref, 4, far_day_ref)):
+        row, day = targets_ref[dest_row : dest_row + 1, :], as_row(day_table[...])
+        row = jnp.where(row < chosen[0] * cap, jnp.where(row < 0, row, row + units * cap), row) - chosen[0] * cap
+        hot = (lax.broadcasted_iota(jnp.int32, (len(chosen) * cap, columns), 0) == row).astype(jnp.bfloat16)
         sun = jnp.broadcast_to(day.astype(jnp.float32), (FLAG_ROWS, columns)).astype(jnp.bfloat16)
-        flags.append(
-            lax.dot_general(sun, hot, (((1,), (1,)), ((), ())), preferred_element_type=jnp.float32)
-        )
-        placed = dot(hot, rows[...]).astype(jnp.bfloat16)
-        for i, out_ref in enumerate(out_refs):
-            out_ref[pl.ds(pl.multiple_of(source_core * cap, cap), cap), :] = placed[i * cap : (i + 1) * cap, :]
-    first = jnp.where(core == 0, flags[0], flags[1]).astype(jnp.bfloat16)
-    second = jnp.where(core == 0, flags[1], flags[0]).astype(jnp.bfloat16)
-    middle = features // 2
-    for i, out_ref in enumerate(out_refs):
-        if cap < middle:
-            out_ref[2 * cap :, :] = jnp.zeros((FLAG_ROWS, features), jnp.bfloat16)
-        out_ref[2 * cap :, 0:cap] = first[:, i * cap : (i + 1) * cap]
-        out_ref[2 * cap :, middle : middle + cap] = second[:, i * cap : (i + 1) * cap]
+        marks = lax.dot_general(sun, hot, (((1,), (1,)), ((), ())), preferred_element_type=jnp.float32)
+        flags.append(marks.astype(jnp.bfloat16))
+        placed.append(dot(hot, rows[...]).astype(jnp.bfloat16))
+    for first in range(2):
+
+        @pl.when(core == first)
+        def _():
+            rest = list(out_refs)
+            for i, parts in enumerate(split):
+                span = slice(i * cap, (i + 1) * cap)
+                last = rest[1] if parts else rest[0]
+                below = last.shape[0] - FLAG_ROWS
+                if cap < middle:
+                    last[below:, :] = jnp.zeros((FLAG_ROWS, features), jnp.bfloat16)
+                for source in range(2):
+                    out_ref = rest[source] if parts else last
+                    place = 0 if parts else source * cap
+                    out_ref[place : place + cap, :] = placed[source ^ first][span, :]
+                    last[below:, source * middle : source * middle + cap] = flags[source ^ first][:, span]
+                rest = rest[2:] if parts else rest[1:]
+
+
+def join(cap, packet_ref, parts):
+    packet_ref[0:cap, :] = parts[0][...]
+    packet_ref[cap:, :] = parts[1][...]
 
 
 def silu(v):
@@ -133,35 +145,38 @@
     return pl.ds(pl.multiple_of(unit * 2 * cap, 2 * cap), 2 * cap)
 
 
-def lower_kernel(cap, base, pick, low, targets_ref, packet_ref, cloud_ref, *refs):
-    weights, refs = refs[:6], refs[6 + base :]
-    (answer_ref, new_ref, first_ref), (updated_ref, sem) = refs[:3], refs[-2:]
+def lower_kernel(cap, targets_ref, first_part, second_part, cloud_ref, *refs):
+    weights, (answer_ref, new_ref, hot_ref), refs = refs[:6], refs[6:9], refs[9:]
+    refs, (packet_ref, updated_ref, sem) = refs[:-3], refs[-3:]
+    low_firsts, up_firsts = refs[: len(refs) // 2], refs[len(refs) // 2 :]
+    join(cap, packet_ref, (first_part, second_part))
     core, unit, _, inner = position()
     half, features = lax.axis_size("elem") // 4, packet_ref.shape[1]
-    place = lax.bitwise_xor(inner, low)
-    served = rows_of(place, cap)
+    served = rows_of(inner, cap)
     cloud = cloud_ref[served, :]
     answer_ref[...], updated_ref[...] = serve(cap, packet_ref, cloud, cloud_part(cloud, weights, features), weights)
     copy = pltpu.make_async_copy(updated_ref, new_ref.at[served, :], sem)
     copy.start()
-    for j, part in enumerate(cloud_part(cloud_ref[rows_of(half + place, cap), :], weights, features)):
-        first_ref[j] = part
-    if pick:
-        hot_ref = refs[3]
-        table = jnp.transpose(targets_ref[...].astype(jnp.float32)).astype(jnp.int32)
-        dest, order = table[:, 1:2], table[:, 2:3]
-        step = lax.bitwise_xor(lax.shift_right_logical(dest, 1), jnp.full_like(dest, unit))
-        side = jnp.where(lax.bitwise_and(dest, 1) == core, 0, 1)
-        row = (step * 2 + side) * cap + order
-        hot_ref[...] = (lax.broadcasted_iota(jnp.int32, hot_ref.shape, 1) == row).astype(jnp.bfloat16)
+    for base, lows, firsts in ((0, range(1, half), low_firsts), (half, range(half), up_firsts)):
+        for low, first_ref in zip(lows, firsts):
+            cloud = cloud_ref[rows_of(base + lax.bitwise_xor(inner, low), cap), :]
+            for j, part in enumerate(cloud_part(cloud, weights, features)):
+                first_ref[j] = part
+    table = jnp.transpose(targets_ref[...].astype(jnp.float32)).astype(jnp.int32)
+    dest, order = table[:, 1:2], table[:, 2:3]
+    step = lax.bitwise_xor(lax.shift_right_logical(dest, 1), jnp.full_like(dest, unit))
+    side = jnp.where(lax.bitwise_and(dest, 1) == core, 0, 1)
+    row = (step * 2 + side) * cap + order
+    hot_ref[...] = (lax.broadcasted_iota(jnp.int32, hot_ref.shape, 1) == row).astype(jnp.bfloat16)
     copy.wait()
 
 
-def upper_kernel(cap, low, lent_ref, lower_answer_ref, first_ref, cloud_ref, *refs):
-    weights, (straight_ref, crossed_ref, new_ref) = refs[:6], refs[6:]
+def upper_kernel(cap, first_part, second_part, lower_answer_ref, first_ref, cloud_ref, *refs):
+    weights, (straight_ref, crossed_ref, new_ref, packet_ref) = refs[:6], refs[6:]
     _, _, upper, inner = position()
-    upper_unit = lax.axis_size("elem") // 4 + lax.bitwise_xor(inner, low)
-    answer, new_ref[...] = serve(cap, lent_ref, cloud_ref[rows_of(upper_unit, cap), :], first_ref, weights)
+    join(cap, packet_ref, (first_part, second_part))
+    served = rows_of(lax.axis_size("elem") // 4 + inner, cap)
+    answer, new_ref[...] = serve(cap, packet_ref, cloud_ref[served, :], first_ref, weights)
 
     @pl.when(upper == 0)
     def _():
@@ -174,13 +189,31 @@
         crossed_ref[...] = lower_answer_ref[...]
 
 
-def store_kernel(cap, *refs):
+def both_kernel(cap, low, lower_ref, lent_ref, first_ref, lower_first_ref, cloud_ref, *refs):
+    weights, (straight_ref, crossed_ref, new_ref, lower_new_ref) = refs[:6], refs[6:]
+    _, _, upper, inner = position()
+    place, half = lax.bitwise_xor(inner, low), lax.axis_size("elem") // 4
+    answer, new_ref[...] = serve(cap, lent_ref, cloud_ref[rows_of(half + place, cap), :], first_ref, weights)
+    lower, lower_new_ref[...] = serve(cap, lower_ref, cloud_ref[rows_of(place, cap), :], lower_first_ref, weights)
+
+    @pl.when(upper == 0)
+    def _():
+        crossed_ref[...] = answer
+        straight_ref[...] = lower
+
+    @pl.when(upper == 1)
+    def _():
+        straight_ref[...] = answer
+        crossed_ref[...] = lower
+
+
+def store_kernel(cap, places, *refs):
     news, (new_ref, sems) = refs[:-3], refs[-2:]
     _, _, _, inner = position()
     copies = []
-    for low, piece in enumerate(news):
-        served = lax.axis_size("elem") // 4 + lax.bitwise_xor(inner, low)
-        copies.append(pltpu.make_async_copy(piece, new_ref.at[rows_of(served, cap), :], sems.at[low]))
+    for i, (piece, (base, low)) in enumerate(zip(news, places)):
+        served = base + lax.bitwise_xor(inner, low)
+        copies.append(pltpu.make_async_copy(piece, new_ref.at[rows_of(served, cap), :], sems.at[i]))
         copies[-1].start()
     for copy in copies:
         copy.wait()
@@ -253,63 +286,77 @@
         cost_estimate=work(4),
         name="column_targets",
     )(dest_table, far_dest)
+    parts = [jax.ShapeDtypeStruct((cap + rows, features), jnp.bfloat16) for rows in (0, FLAG_ROWS)]
     packets = [None] * units
     for chosen in ([half], [*range(half + 1, units), *range(half)]):
-        earlier = [packets[half]] if packets[half] is not None else []
+        earlier = packets[half][:1] if packets[half] else []
+        shapes = [parts if du % half == 0 else [packet] for du in chosen]
         outs = pl.pallas_call(
-            functools.partial(place_kernel, cap, units, chosen[0]),
-            out_shape=[packet] * len(chosen),
+            functools.partial(place_kernel, cap, units, chosen),
+            out_shape=sum(shapes, []),
             in_specs=[vmem] * (5 + len(earlier)),
-            out_specs=[vmem] * len(chosen),
+            out_specs=[vmem] * sum(map(len, shapes)),
             compiler_params=params,
             cost_estimate=work(3),
             name="place_columns",
         )(far_state, state, targets, far_day, day_table, *earlier)
-        for du, out in zip(chosen, outs):
-            packets[du] = out
+        for du, pieces in zip(chosen, shapes):
+            packets[du], outs = outs[: len(pieces)], outs[len(pieces) :]
 
     def onward(low, far):
         return lambda e, b: (e ^ (2 * low), (b + away * far) % bands)
 
-    hopped = [moved(packets[half + low], onward(half, 0)) for low in range(half)]
-    lent = [moved(jnp.where(upper == 0, hopped[low], packets[low]), onward(low, 1)) for low in range(half)]
-    kept = [jnp.where(upper == 0, packets[low], hopped[low]) for low in range(half)]
-    lower = [kept[low] if low == 0 else moved(kept[low], onward(low, 0)) for low in range(half)]
-
+    def each(route, blocks):
+        return [moved(block, route) for block in blocks]
+
+    def chosen_of(side, yes, no):
+        return [jnp.where(upper == side, a, b) for a, b in zip(yes, no)]
+
+    hopped = [each(onward(half, 0), packets[half + low]) for low in range(half)]
+    lent = [each(onward(low, 1), chosen_of(0, hopped[low], packets[low])) for low in range(half)]
+    kept = [chosen_of(0, packets[low], hopped[low]) for low in range(half)]
+    lower = [kept[low] if low == 0 else each(onward(low, 0), kept[low]) for low in range(half)]
+
+    packet_buffer = pltpu.VMEM(packet.shape, jnp.bfloat16)
     tile = jax.ShapeDtypeStruct((2 * cap, features), jnp.bfloat16)
     new_tile = jax.ShapeDtypeStruct((2 * cap, cloud.shape[1]), jnp.bfloat16)
     first_shape = jax.ShapeDtypeStruct((2, 2 * cap, conv_in.shape[1]), jnp.float32)
-    firsts = []
     hot_shape = jax.ShapeDtypeStruct((columns, groups * cap), jnp.bfloat16)
-    answers, lower_answers, news, new_cloud = [None] * units, [], [], None
-    for low in range(half):
-        pick, base = low == 0, () if low == 0 else (new_cloud,)
-        answer, new_cloud, first, *picked = pl.pallas_call(
-            functools.partial(lower_kernel, cap, len(base), pick, low),
-            out_shape=[tile, like(cloud), first_shape] + [hot_shape] * pick,
-            in_specs=[vmem] * 9 + [hbm] * len(base),
-            out_specs=[vmem, hbm, vmem] + [vmem] * pick,
-            scratch_shapes=[pltpu.VMEM(new_tile.shape, jnp.bfloat16), pltpu.SemaphoreType.DMA],
-            input_output_aliases={9: 1} if base else {},
+    answers = [None] * units
+    lower_answer, new_cloud, hot, *firsts = pl.pallas_call(
+        functools.partial(lower_kernel, cap),
+        out_shape=[tile, like(cloud), hot_shape] + [first_shape] * (units - 1),
+        in_specs=[vmem] * 10,
+        out_specs=[vmem, hbm] + [vmem] * units,
+        scratch_shapes=[packet_buffer, pltpu.VMEM(new_tile.shape, jnp.bfloat16), pltpu.SemaphoreType.DMA],
+        compiler_params=params,
+        cost_estimate=work(3),
+        name="lower_physics",
+    )(targets, *lower[0], cloud, *weights)
+    low_firsts, up_firsts = [None] + firsts[: half - 1], firsts[half - 1 :]
+    answers[0], answers[half], new = pl.pallas_call(
+        functools.partial(upper_kernel, cap),
+        out_shape=[tile, tile, new_tile],
+        in_specs=[vmem] * 11,
+        out_specs=[vmem] * 3,
+        scratch_shapes=[packet_buffer],
+        compiler_params=params,
+        cost_estimate=work(3),
+        name="upper_physics",
+    )(*lent[0], lower_answer, up_firsts[0], cloud, *weights)
+    news, places = [new], [(half, 0)]
+    for low in range(1, half):
+        answers[low], answers[half + low], *both = pl.pallas_call(
+            functools.partial(both_kernel, cap, low),
+            out_shape=[tile, tile, new_tile, new_tile],
+            in_specs=[vmem] * 11,
+            out_specs=[vmem] * 4,
             compiler_params=params,
             cost_estimate=work(3),
-            name="lower_physics",
-        )(targets, lower[low], cloud, *weights, *base)
-        lower_answers.append(answer)
-        firsts.append(first)
-        if pick:
-            hot = picked[0]
-    for low in range(half):
-        answers[low], answers[half + low], new = pl.pallas_call(
-            functools.partial(upper_kernel, cap, low),
-            out_shape=[tile, tile, new_tile],
-            in_specs=[vmem] * 10,
-            out_specs=[vmem] * 3,
-            compiler_params=params,
-            cost_estimate=work(3),
-            name="upper_physics",
-        )(lent[low], lower_answers[low], firsts[low], cloud, *weights)
-        news.append(new)
+            name="both_physics",
+        )(*lower[low], *lent[low], up_firsts[low], low_firsts[low], cloud, *weights)
+        news += both
+        places += [(half, low), (0, low)]
 
     def home(du):
         def target(e, b):
@@ -322,14 +369,14 @@
     sequence = [du for low in range(half) for du in (half + low, low)]
     back = [moved(answers[du], home(du)) for du in sequence]
     new_cloud = pl.pallas_call(
-        functools.partial(store_kernel, cap),
+        functools.partial(store_kernel, cap, places),
         out_shape=like(cloud),
-        in_specs=[vmem] * half + [hbm],
+        in_specs=[vmem] * len(news) + [hbm],
         out_specs=hbm,
-        scratch_shapes=[pltpu.SemaphoreType.DMA((half,))],
-        input_output_aliases={half: 0},
-        compiler_params=params,
-        cost_estimate=work(1),
+        scratch_shapes=[pltpu.SemaphoreType.DMA((len(news),))],
+        input_output_aliases={len(news): 0},
+        compiler_params=params,
+        cost_estimate=work(0.01),
         name="store_cloud",
     )(*news, new_cloud)
     back[0], new_cloud = lax.optimization_barrier((back[0], new_cloud))
@@ -340,7 +387,7 @@
         in_specs=[vmem] * (2 * units),
         out_specs=vmem,
         compiler_params=params,
-        cost_estimate=work(2),
+        cost_estimate=work(0.01),
         name="gather_most",
     )(*back, *far_back[:-1], hot)
     tendency = pl.pallas_call(
@@ -350,7 +397,7 @@
         out_specs=hbm,
         scratch_shapes=[pltpu.VMEM(state.shape, jnp.bfloat16), pltpu.SemaphoreType.DMA((2,))],
         compiler_params=params,
-        cost_estimate=work(1),
+        cost_estimate=work(0.01),
         name="gather_last",
     )(most, far_back[-1], hot)
     return (tendency, new_cloud)

time: 41.8 us -> 40.8 us (0.976)
  the two profiles are of different devices: /device:TPU:13 before, /device:TPU:11 now
where the time goes in v7:
time: 40.8 us; the launch traced here: 40.6 us
  starting transfers between devices  27.7 us (68%)
  Pallas kernels  6.58 us (16%)
  waiting for transfers between devices  5.15 us (13%)
  between operations  0.81 us (2%)
    ppermute x18, starting transfers between devices, moved(): return lax.ppermute(block, ('elem', 'band'), route)  27.7 us
    ppermute x18, waiting for transfers between devices, moved(): return lax.ppermute(block, ('elem', 'band'), route)  5.15 us
    pallas_call x1, Pallas kernels, per_device(): pl.pallas_call(functools.partial(lower_kernel, cap), out_shape=[tile, lik...  1.54 us
    pallas_call x1, Pallas kernels, per_device(): pl.pallas_call(functools.partial(both_kernel, cap, low), out_shape=[tile,...  1.06 us
    pallas_call x1, Pallas kernels, per_device(): pl.pallas_call(functools.partial(finish_kernel, cap, sequence[-1]), out_s...  0.94 us
    pallas_call x1, Pallas kernels, per_device(): pl.pallas_call(functools.partial(store_kernel, cap, places), out_shape=li...  0.9 us
    pallas_call x2, Pallas kernels, per_device(): pl.pallas_call(functools.partial(place_kernel, cap, units, chosen), out_s...  0.87 us
  transfers between devices with their start and end apart: 18, of which 6 were waited for; matrix products, arithmetic and copies ran while one was open for 0% of the time, Pallas kernels for 13%

profile of v7, /device:TPU:11, one launch (start us, length us, event | category | flops | bytes accessed | tf_op | source)
XLA Modules:
  0.0 40.6 jit_solution(2816319179564259406)
XLA Ops:
  0.6 0.0 copy-start.9
  0.6 0.7 %collective-permute-start.1 = (s32[4,128]{1,0:T(4,128)}, s32[4,128]{1,0:T(4,128)S(1)}, u32[]{:S(2)}, u32[]{:S(2)}) collective-permute-start(s32[4,128]{1,0:T(4,128)} %bitcast.2), channel_id=1, source_target_pairs={{0,4},{1,5},{2,6},{3,7},{4,0},{5,1},{6,2},{7,3},{8,12},{9,13},{10,... | collective-permute-start | bytes 6152 | tf_op jit(solution)/shard_map/ppermute | solution.py:22
  1.4 0.0 copy-done.9
  1.4 0.6 %collective-permute-start.2 = (s32[4,128]{1,0:T(4,128)S(1)}, s32[4,128]{1,0:T(4,128)S(1)}, u32[]{:S(2)}, u32[]{:S(2)}) collective-permute-start(s32[4,128]{1,0:T(4,128)S(1)} %bitcast.4), channel_id=1, source_target_pairs={{0,4},{1,5},{2,6},{3,7},{4,0},{5,1},{6,2},{7,3},{8,12},{9,13},{10,... | collective-permute-start | bytes 6152 | tf_op jit(solution)/shard_map/ppermute | solution.py:22
  2.0 0.0 collective-permute-start
  2.0 0.0 copy-start.8
  2.0 0.0 copy-start.4
  2.0 0.4 %collective-permute-done.1.far_dest_ref = s32[4,128]{1,0:T(4,128)S(1)} collective-permute-done((s32[4,128]{1,0:T(4,128)}, s32[4,128]{1,0:T(4,128)S(1)}, u32[]{:S(2)}, u32[]{:S(2)}) %collective-permute-start.1) | collective-permute-done | bytes 2080 | tf_op jit(solution)/shard_map/ppermute | solution.py:22
  2.4 0.3 copy-done.8
  2.7 0.2 column_targets.1.targets_ref
  2.9 0.0 collective-permute-done.2.far_day_ref
  2.9 0.9 %collective-permute-done.far_state_ref = bf16[512,256]{1,0:T(8,128)(2,1)S(1)} collective-permute-done((bf16[512,256]{1,0:T(8,128)(2,1)}, bf16[512,256]{1,0:T(8,128)(2,1)S(1)}, u32[]{:S(2)}, u32[]{:S(2)}) %collective-permute-start) | collective-permute-done | bytes 262176 | tf_op jit(solution)/shard_map/ppermute | solution.py:22
  3.7 0.0 copy-done.4
  3.7 0.3 place_columns.2
  4.0 1.3 %collective-permute-start.3 = (bf16[128,256]{1,0:T(8,128)(2,1)S(1)}, bf16[128,256]{1,0:T(8,128)(2,1)S(1)}, u32[]{:S(2)}, u32[]{:S(2)}) collective-permute-start(bf16[128,256]{1,0:T(8,128)(2,1)S(1)} %get-tuple-element.23.refs_0_), channel_id=1, source_target_pairs={{0,16},{1,17},{2,18},{3,19},{4,20},{5,21},{6,22},{7,23},{8,24},{9,... | collective-permute-start | bytes 196616 | tf_op jit(solution)/shard_map/ppermute | solution.py:22
  5.3 0.0 copy-start
  5.4 0.2 collective-permute-start.5
  5.6 0.0 copy-start.2
  5.6 0.0 copy-start.3
  5.6 0.0 copy-start.6
  5.6 0.0 copy-start.7
  5.6 0.6 %place_columns.3 = (bf16[272,256]{1,0:T(8,128)(2,1)S(1)}, bf16[128,256]{1,0:T(8,128)(2,1)S(1)}, bf16[144,256]{1,0:T(8,128)(2,1)S(1)}, bf16[272,256]{1,0:T(8,128)(2,1)S(1)}) custom-call(bf16[512,256]{1,0:T(8,128)(2,1)S(1)} %collective-permute-done.far_state_ref, bf16[512,256]{1,0:T(8,128)(2,1)S(1)} %copy-done.4, s32[8,512]{1,0:T(8,128)S(1)} %column_targets.1.targets_ref, ...), custom_call_target="tpu_custom_call" | custom-call | flops 3449999872 | tf_op jit(solution)/shard_map/place_columns/pallas_call | solution.py:294
  6.2 0.0 copy-start.1
  6.2 1.3 %collective-permute-start.8 = (bf16[272,256]{1,0:T(8,128)(2,1)S(1)}, bf16[272,256]{1,0:T(8,128)(2,1)S(1)}, u32[]{:S(2)}, u32[]{:S(2)}) collective-permute-start(bf16[272,256]{1,0:T(8,128)(2,1)S(1)} %get-tuple-element.32), channel_id=1, source_target_pairs={{0,16},{1,17},{2,18},{3,19},{4,20},{5,21},{6,22},{7,23},{8,24},{9,... | collective-permute-start | bytes 417800 | tf_op jit(solution)/shard_map/ppermute | solution.py:22
  7.5 0.2 collective-permute-done.3
  7.7 2.4 %collective-permute-start.4 = (bf16[128,256]{1,0:T(8,128)(2,1)S(1)}, bf16[128,256]{1,0:T(8,128)(2,1)S(1)}, u32[]{:S(2)}, u32[]{:S(2)}) collective-permute-start(bf16[128,256]{1,0:T(8,128)(2,1)S(1)} %get-tuple-element.49), channel_id=1, source_target_pairs={{0,2},{1,3},{2,0},{3,1},{4,6},{5,7},{6,4},{7,5},{8,10},{9,11},{10,... | collective-permute-start | bytes 196616 | tf_op jit(solution)/shard_map/ppermute | solution.py:22
  10.1 0.0 collective-permute-done.5
  10.1 1.4 %collective-permute-start.6 = (bf16[144,256]{1,0:T(8,128)(2,1)S(1)}, bf16[144,256]{1,0:T(8,128)(2,1)S(1)}, u32[]{:S(2)}, u32[]{:S(2)}) collective-permute-start(bf16[144,256]{1,0:T(8,128)(2,1)S(1)} %get-tuple-element.47), channel_id=1, source_target_pairs={{0,2},{1,3},{2,0},{3,1},{4,6},{5,7},{6,4},{7,5},{8,10},{9,11},{10,... | collective-permute-start | bytes 221192 | tf_op jit(solution)/shard_map/ppermute | solution.py:22
  11.5 0.0 copy-done
  11.5 0.0 copy-done.2
  11.5 0.0 copy-done.3
  11.5 0.0 copy-done.6
  11.5 0.0 copy-done.7
  11.5 0.0 copy-done.1
  11.5 0.0 copy-done.5
  11.5 1.5 %lower_physics.1 = (bf16[256,256]{1,0:T(8,128)(2,1)S(1)}, bf16[1024,512]{1,0:T(8,128)(2,1)}, bf16[512,1024]{1,0:T(8,128)(2,1)S(1)}, f32[2,256,256]{2,1,0:T(8,128...) custom-call(s32[8,512]{1,0:T(8,128)S(1)} %column_targets.1.targets_ref, ...), custom_call_target="tpu_custom_call" | custom-call | flops 3449999872 | tf_op jit(solution)/shard_map/lower_physics/pallas_call | solution.py:326
  13.1 0.0 collective-permute-done.8
  13.1 1.3 %collective-permute-start.10 = (bf16[272,256]{1,0:T(8,128)(2,1)S(1)}, bf16[272,256]{1,0:T(8,128)(2,1)S(1)}, u32[]{:S(2)}, u32[]{:S(2)}) collective-permute-start(bf16[272,256]{1,0:T(8,128)(2,1)S(1)} %get-tuple-element.44), channel_id=1, source_target_pairs={{0,10},{1,11},{2,8},{3,9},{4,14},{5,15},{6,12},{7,13},{8,2},{9,3},... | collective-permute-start | bytes 417800 | tf_op jit(solution)/shard_map/ppermute | solution.py:22
  14.4 1.2 %collective-permute-start.9 = (bf16[272,256]{1,0:T(8,128)(2,1)S(1)}, bf16[272,256]{1,0:T(8,128)(2,1)S(1)}, u32[]{:S(2)}, u32[]{:S(2)}) collective-permute-start(bf16[272,256]{1,0:T(8,128)(2,1)S(1)} %get-tuple-element.45), channel_id=1, source_target_pairs={{0,8},{1,9},{2,10},{3,11},{4,12},{5,13},{6,14},{7,15},{8,0},{9,1},... | collective-permute-start | bytes 417800 | tf_op jit(solution)/shard_map/ppermute | solution.py:22
  15.7 0.0 collective-permute-done.4.first_part
  15.7 2.9 %collective-permute-done.6.second_part = bf16[144,256]{1,0:T(8,128)(2,1)S(1)} collective-permute-done((bf16[144,256]{1,0:T(8,128)(2,1)S(1)}, bf16[144,256]{1,0:T(8,128)(2,1)S(1)}, u32[]{:S(2)}, u32[]{:S(2)}) %collective-permute-start.6) | collective-permute-done | bytes 73760 | tf_op jit(solution)/shard_map/ppermute | solution.py:22
  18.6 0.6 %upper_physics.1 = (bf16[256,256]{1,0:T(8,128)(2,1)S(1)}, bf16[256,256]{1,0:T(8,128)(2,1)S(1)}, bf16[256,512]{1,0:T(8,128)(2,1)S(1)}) custom-call(bf16[128,256]{1,0:T(8,128)(2,1)S(1)} %collective-permute-done.4.first_part, bf16[144,256]{1,0:T(8,128)(2,1)S(1)} %collective-permute-done.6.second_part, bf16[256,256]{1,0:T(8,128)(2,1)S(1)} %get-tuple-element.27.lower_answer_ref, ...), custom_call_target="tpu_custom_call" | custom-call | flops 3449999872 | tf_op jit(solution)/shard_map/upper_physics/pallas_call | solution.py:337
  19.2 4.4 %collective-permute-start.7 = (bf16[256,256]{1,0:T(8,128)(2,1)S(1)}, bf16[256,256]{1,0:T(8,128)(2,1)S(1)}, u32[]{:S(2)}, u32[]{:S(2)}) collective-permute-start(bf16[256,256]{1,0:T(8,128)(2,1)S(1)} %get-tuple-element.29), channel_id=1, source_target_pairs={{0,18},{1,19},{2,16},{3,17},{4,22},{5,23},{6,20},{7,21},{8,26},{9,... | collective-permute-start | bytes 393224 | tf_op jit(solution)/shard_map/ppermute | solution.py:22
  23.6 0.7 %collective-permute-start.11 = (bf16[256,256]{1,0:T(8,128)(2,1)S(1)}, bf16[256,256]{1,0:T(8,128)(2,1)S(1)}, u32[]{:S(2)}, u32[]{:S(2)}) collective-permute-start(bf16[256,256]{1,0:T(8,128)(2,1)S(1)} %get-tuple-element.39), channel_id=1, source_target_pairs={{0,0},{1,1},{2,2},{3,3},{4,4},{5,5},{6,6},{7,7},{8,8},{9,9},{10,10... | collective-permute-start | bytes 393224 | tf_op jit(solution)/shard_map/ppermute | solution.py:22
  24.2 0.3 collective-permute-done.10.lent_ref
  24.5 0.0 collective-permute-done.9.lower_ref
  24.5 1.1 %both_physics.1 = (bf16[256,256]{1,0:T(8,128)(2,1)S(1)}, bf16[256,256]{1,0:T(8,128)(2,1)S(1)}, bf16[256,512]{1,0:T(8,128)(2,1)S(1)}, bf16[256,512]{1,0:T(8,128)(2,1)S(1)}) custom-call(bf16[272,256]{1,0:T(8,128)(2,1)S(1)} %collective-permute-done.9.lower_ref, bf16[272,256]{1,0:T(8,128)(2,1)S(1)} %collective-permute-done.10.lent_ref, ...), custom_call_target="tpu_custom_call" | custom-call | flops 3449999872 | tf_op jit(solution)/shard_map/both_physics/pallas_call | solution.py:349
  25.6 3.7 %collective-permute-start.12 = (bf16[256,256]{1,0:T(8,128)(2,1)S(1)}, bf16[256,256]{1,0:T(8,128)(2,1)S(1)}, u32[]{:S(2)}, u32[]{:S(2)}) collective-permute-start(bf16[256,256]{1,0:T(8,128)(2,1)S(1)} %get-tuple-element.40), channel_id=1, source_target_pairs={{0,26},{1,27},{2,24},{3,25},{4,30},{5,31},{6,28},{7,29},{8,18},{9,... | collective-permute-start | bytes 393224 | tf_op jit(solution)/shard_map/ppermute | solution.py:22
  29.3 1.9 %collective-permute-start.13 = (bf16[256,256]{1,0:T(8,128)(2,1)S(1)}, bf16[256,256]{1,0:T(8,128)(2,1)S(1)}, u32[]{:S(2)}, u32[]{:S(2)}) collective-permute-start(bf16[256,256]{1,0:T(8,128)(2,1)S(1)} %get-tuple-element.41), channel_id=1, source_target_pairs={{0,8},{1,9},{2,10},{3,11},{4,12},{5,13},{6,14},{7,15},{8,0},{9,1},... | collective-permute-start | bytes 393224 | tf_op jit(solution)/shard_map/ppermute | solution.py:22
  31.2 0.9 %store_cloud.1 = bf16[1024,512]{1,0:T(8,128)(2,1)} custom-call(bf16[256,512]{1,0:T(8,128)(2,1)S(1)} %get-tuple-element.30.refs_0_, bf16[256,512]{1,0:T(8,128)(2,1)S(1)} %get-tuple-element.35.refs_1_, bf16[256,512]{1,0:T(8,128)(2,1)S(1)} %get-tuple-element.36.refs_2_, bf16[1024,512]{1,0:T(8,128)(2,1)} %get-tuple-element.37.refs_3_), custom_call_target="tpu_custom_call", output_to_operand_aliasing={{}: (3, {})} | custom-call | flops 11500000 | tf_op jit(solution)/shard_map/store_cloud/pallas_call | solution.py:371
  32.1 0.0 collective-permute-done.7.refs_0_
  32.1 2.0 %collective-permute-start.14 = (bf16[256,256]{1,0:T(8,128)(2,1)S(1)}, bf16[256,256]{1,0:T(8,128)(2,1)S(1)}, u32[]{:S(2)}, u32[]{:S(2)}) collective-permute-start(bf16[256,256]{1,0:T(8,128)(2,1)S(1)} %collective-permute-done.7.refs_0_), channel_id=1, source_target_pairs={{0,4},{1,5},{2,6},{3,7},{4,0},{5,1},{6,2},{7,3},{8,12},{9,13},{10,... | collective-permute-start | bytes 393224 | tf_op jit(solution)/shard_map/ppermute | solution.py:22
  34.1 0.0 collective-permute-done.11.refs_1_
  34.1 0.1 collective-permute-start.15
  34.2 0.0 collective-permute-done.12.refs_2_
  34.2 1.4 %collective-permute-start.16 = (bf16[256,256]{1,0:T(8,128)(2,1)S(1)}, bf16[256,256]{1,0:T(8,128)(2,1)S(1)}, u32[]{:S(2)}, u32[]{:S(2)}) collective-permute-start(bf16[256,256]{1,0:T(8,128)(2,1)S(1)} %collective-permute-done.12.refs_2_), channel_id=1, source_target_pairs={{0,4},{1,5},{2,6},{3,7},{4,0},{5,1},{6,2},{7,3},{8,12},{9,13},{10,... | collective-permute-start | bytes 393224 | tf_op jit(solution)/shard_map/ppermute | solution.py:22
  35.6 0.0 collective-permute-done.13.refs_3_
  35.6 3.1 %collective-permute-start.17 = (bf16[256,256]{1,0:T(8,128)(2,1)S(1)}, bf16[256,256]{1,0:T(8,128)(2,1)S(1)}, u32[]{:S(2)}, u32[]{:S(2)}) collective-permute-start(bf16[256,256]{1,0:T(8,128)(2,1)S(1)} %collective-permute-done.13.refs_3_), channel_id=1, source_target_pairs={{0,4},{1,5},{2,6},{3,7},{4,0},{5,1},{6,2},{7,3},{8,12},{9,13},{10,... | collective-permute-start | bytes 393224 | tf_op jit(solution)/shard_map/ppermute | solution.py:22
  38.7 0.0 collective-permute-done.14.refs_4_
  38.7 0.0 collective-permute-done.15.refs_5_
  38.7 0.0 collective-permute-done.16.refs_6_
  38.7 0.5 %gather_most.1.gathered_ref = bf16[512,256]{1,0:T(8,128)(2,1)S(1)} custom-call(bf16[256,256]{1,0:T(8,128)(2,1)S(1)} %collective-permute-done.7.refs_0_, bf16[256,256]{1,0:T(8,128)(2,1)S(1)} %collective-permute-done.11.refs_1_, bf16[256,256]{1,0:T(8,128)(2,1)S(1)} %collective-permute-done.12.refs_2_, bf16[256,256]{1,0:T(8,128)(2,1)S(1)} %collective-permute-done.13.refs_3_, ...), custom_call_target="tpu_custom_call" | custom-call | flops 11500000 | tf_op jit(solution)/shard_map/gather_most/pallas_call | solution.py:384
  39.1 0.5 %collective-permute-done.17.far_ref = bf16[256,256]{1,0:T(8,128)(2,1)S(1)} collective-permute-done((bf16[256,256]{1,0:T(8,128)(2,1)S(1)}, bf16[256,256]{1,0:T(8,128)(2,1)S(1)}, u32[]{:S(2)}, u32[]{:S(2)}) %collective-permute-start.17) | collective-permute-done | bytes 131104 | tf_op jit(solution)/shard_map/ppermute | solution.py:22
  39.7 0.9 %gather_last.1 = bf16[512,256]{1,0:T(8,128)(2,1)} custom-call(bf16[512,256]{1,0:T(8,128)(2,1)S(1)} %gather_most.1.gathered_ref, bf16[256,256]{1,0:T(8,128)(2,1)S(1)} %collective-permute-done.17.far_ref, bf16[512,1024]{1,0:T(8,128)(2,1)S(1)} %get-tuple-element.42.refs_7_.hot_ref), custom_call_target="tpu_custom_call" | custom-call | flops 11500000 | tf_op jit(solution)/shard_map/gather_last/pallas_call | solution.py:393
  (4 shorter events, 0.1 us)
Async XLA Ops:
  0.6 0.8 %copy-start.9 = (s32[512,1]{0,1:T(1,128)S(1)}, s32[512,1]{0,1:T(1,128)}, u32[]{:S(2)}) copy-start(s32[512,1]{0,1:T(1,128)} %param.12) | copy-start | bytes 6148
  0.6 1.8 %collective-permute-start.1 = (s32[4,128]{1,0:T(4,128)}, s32[4,128]{1,0:T(4,128)S(1)}, u32[]{:S(2)}, u32[]{:S(2)}) collective-permute-start(s32[4,128]{1,0:T(4,128)} %bitcast.2), channel_id=1, source_target_pairs={{0,4},{1,5},{2,6},{3,7},{4,0},{5,1},{6,2},{7,3},{8,12},{9,13},{10,... | collective-permute-start | bytes 6152 | tf_op jit(solution)/shard_map/ppermute | solution.py:22
  1.4 1.5 %collective-permute-start.2 = (s32[4,128]{1,0:T(4,128)S(1)}, s32[4,128]{1,0:T(4,128)S(1)}, u32[]{:S(2)}, u32[]{:S(2)}) collective-permute-start(s32[4,128]{1,0:T(4,128)S(1)} %bitcast.4), channel_id=1, source_target_pairs={{0,4},{1,5},{2,6},{3,7},{4,0},{5,1},{6,2},{7,3},{8,12},{9,13},{10,... | collective-permute-start | bytes 6152 | tf_op jit(solution)/shard_map/ppermute | solution.py:22
  2.0 1.7 %collective-permute-start = (bf16[512,256]{1,0:T(8,128)(2,1)}, bf16[512,256]{1,0:T(8,128)(2,1)S(1)}, u32[]{:S(2)}, u32[]{:S(2)}) collective-permute-start(bf16[512,256]{1,0:T(8,128)(2,1)} %state_ref.3), channel_id=1, source_target_pairs={{0,4},{1,5},{2,6},{3,7},{4,0},{5,1},{6,2},{7,3},{8,12},{9,13},{10,... | collective-permute-start | bytes 786440 | tf_op jit(solution)/shard_map/ppermute | solution.py:22
  2.0 0.7 %copy-start.8 = (s32[512,1]{0,1:T(1,128)S(1)}, s32[512,1]{0,1:T(1,128)}, u32[]{:S(2)}) copy-start(s32[512,1]{0,1:T(1,128)} %param.11) | copy-start | bytes 6148
  2.0 1.7 %copy-start.4 = (bf16[512,256]{1,0:T(8,128)(2,1)S(1)}, bf16[512,256]{1,0:T(8,128)(2,1)}, u32[]{:S(2)}) copy-start(bf16[512,256]{1,0:T(8,128)(2,1)} %state_ref.3) | copy-start | bytes 786436
  4.0 3.6 %collective-permute-start.3 = (bf16[128,256]{1,0:T(8,128)(2,1)S(1)}, bf16[128,256]{1,0:T(8,128)(2,1)S(1)}, u32[]{:S(2)}, u32[]{:S(2)}) collective-permute-start(bf16[128,256]{1,0:T(8,128)(2,1)S(1)} %get-tuple-element.23.refs_0_), channel_id=1, source_target_pairs={{0,16},{1,17},{2,18},{3,19},{4,20},{5,21},{6,22},{7,23},{8,24},{9,... | collective-permute-start | bytes 196616 | tf_op jit(solution)/shard_map/ppermute | solution.py:22
  5.3 6.1 %copy-start = (bf16[1024,512]{1,0:T(8,128)(2,1)S(1)}, bf16[1024,512]{1,0:T(8,128)(2,1)}, u32[]{:S(2)}) copy-start(bf16[1024,512]{1,0:T(8,128)(2,1)} %cloud_ref.5) | copy-start | bytes 3145732
  5.4 4.7 %collective-permute-start.5 = (bf16[144,256]{1,0:T(8,128)(2,1)S(1)}, bf16[144,256]{1,0:T(8,128)(2,1)S(1)}, u32[]{:S(2)}, u32[]{:S(2)}) collective-permute-start(bf16[144,256]{1,0:T(8,128)(2,1)S(1)} %get-tuple-element.25), channel_id=1, source_target_pairs={{0,16},{1,17},{2,18},{3,19},{4,20},{5,21},{6,22},{7,23},{8,24},{9,... | collective-permute-start | bytes 221192 | tf_op jit(solution)/shard_map/ppermute | solution.py:22
  5.6 5.9 %copy-start.2 = (bf16[256,768]{1,0:T(8,128)(2,1)S(1)}, bf16[256,768]{1,0:T(8,128)(2,1)}, u32[]{:S(2)}) copy-start(bf16[256,768]{1,0:T(8,128)(2,1)} %refs_2_.5) | copy-start | bytes 1179652
  5.6 5.9 %copy-start.3 = (bf16[768,256]{1,0:T(8,128)(2,1)S(1)}, bf16[768,256]{1,0:T(8,128)(2,1)}, u32[]{:S(2)}) copy-start(bf16[768,256]{1,0:T(8,128)(2,1)} %refs_3_.5) | copy-start | bytes 1179652
  5.6 5.9 %copy-start.6 = (bf16[256,256]{1,0:T(8,128)(2,1)S(1)}, bf16[256,256]{1,0:T(8,128)(2,1)}, u32[]{:S(2)}) copy-start(bf16[256,256]{1,0:T(8,128)(2,1)} %refs_4_.5) | copy-start | bytes 393220
  5.6 5.9 %copy-start.7 = (bf16[256,128]{1,0:T(8,128)(2,1)S(1)}, bf16[256,128]{1,0:T(8,128)(2,1)}, u32[]{:S(2)}) copy-start(bf16[256,128]{1,0:T(8,128)(2,1)} %refs_5_.5) | copy-start | bytes 196612
  6.2 5.3 %copy-start.1 = (bf16[768,256]{1,0:T(8,128)(2,1)S(1)}, bf16[768,256]{1,0:T(8,128)(2,1)}, u32[]{:S(2)}) copy-start(bf16[768,256]{1,0:T(8,128)(2,1)} %refs_0_.5) | copy-start | bytes 1179652
  6.2 6.9 %collective-permute-start.8 = (bf16[272,256]{1,0:T(8,128)(2,1)S(1)}, bf16[272,256]{1,0:T(8,128)(2,1)S(1)}, u32[]{:S(2)}, u32[]{:S(2)}) collective-permute-start(bf16[272,256]{1,0:T(8,128)(2,1)S(1)} %get-tuple-element.32), channel_id=1, source_target_pairs={{0,16},{1,17},{2,18},{3,19},{4,20},{5,21},{6,22},{7,23},{8,24},{9,... | collective-permute-start | bytes 417800 | tf_op jit(solution)/shard_map/ppermute | solution.py:22
  7.7 8.0 %collective-permute-start.4 = (bf16[128,256]{1,0:T(8,128)(2,1)S(1)}, bf16[128,256]{1,0:T(8,128)(2,1)S(1)}, u32[]{:S(2)}, u32[]{:S(2)}) collective-permute-start(bf16[128,256]{1,0:T(8,128)(2,1)S(1)} %get-tuple-element.49), channel_id=1, source_target_pairs={{0,2},{1,3},{2,0},{3,1},{4,6},{5,7},{6,4},{7,5},{8,10},{9,11},{10,... | collective-permute-start | bytes 196616 | tf_op jit(solution)/shard_map/ppermute | solution.py:22
  10.1 1.5 %copy-start.5 = (bf16[256,256]{1,0:T(8,128)(2,1)S(1)}, bf16[256,256]{1,0:T(8,128)(2,1)}, u32[]{:S(2)}) copy-start(bf16[256,256]{1,0:T(8,128)(2,1)} %refs_1_.5) | copy-start | bytes 393220
  10.1 8.5 %collective-permute-start.6 = (bf16[144,256]{1,0:T(8,128)(2,1)S(1)}, bf16[144,256]{1,0:T(8,128)(2,1)S(1)}, u32[]{:S(2)}, u32[]{:S(2)}) collective-permute-start(bf16[144,256]{1,0:T(8,128)(2,1)S(1)} %get-tuple-element.47), channel_id=1, source_target_pairs={{0,2},{1,3},{2,0},{3,1},{4,6},{5,7},{6,4},{7,5},{8,10},{9,11},{10,... | collective-permute-start | bytes 221192 | tf_op jit(solution)/shard_map/ppermute | solution.py:22
  13.1 11.4 %collective-permute-start.10 = (bf16[272,256]{1,0:T(8,128)(2,1)S(1)}, bf16[272,256]{1,0:T(8,128)(2,1)S(1)}, u32[]{:S(2)}, u32[]{:S(2)}) collective-permute-start(bf16[272,256]{1,0:T(8,128)(2,1)S(1)} %get-tuple-element.44), channel_id=1, source_target_pairs={{0,10},{1,11},{2,8},{3,9},{4,14},{5,15},{6,12},{7,13},{8,2},{9,3},... | collective-permute-start | bytes 417800 | tf_op jit(solution)/shard_map/ppermute | solution.py:22
  14.4 10.1 %collective-permute-start.9 = (bf16[272,256]{1,0:T(8,128)(2,1)S(1)}, bf16[272,256]{1,0:T(8,128)(2,1)S(1)}, u32[]{:S(2)}, u32[]{:S(2)}) collective-permute-start(bf16[272,256]{1,0:T(8,128)(2,1)S(1)} %get-tuple-element.45), channel_id=1, source_target_pairs={{0,8},{1,9},{2,10},{3,11},{4,12},{5,13},{6,14},{7,15},{8,0},{9,1},... | collective-permute-start | bytes 417800 | tf_op jit(solution)/shard_map/ppermute | solution.py:22
  19.2 12.9 %collective-permute-start.7 = (bf16[256,256]{1,0:T(8,128)(2,1)S(1)}, bf16[256,256]{1,0:T(8,128)(2,1)S(1)}, u32[]{:S(2)}, u32[]{:S(2)}) collective-permute-start(bf16[256,256]{1,0:T(8,128)(2,1)S(1)} %get-tuple-element.29), channel_id=1, source_target_pairs={{0,18},{1,19},{2,16},{3,17},{4,22},{5,23},{6,20},{7,21},{8,26},{9,... | collective-permute-start | bytes 393224 | tf_op jit(solution)/shard_map/ppermute | solution.py:22
  23.6 10.5 %collective-permute-start.11 = (bf16[256,256]{1,0:T(8,128)(2,1)S(1)}, bf16[256,256]{1,0:T(8,128)(2,1)S(1)}, u32[]{:S(2)}, u32[]{:S(2)}) collective-permute-start(bf16[256,256]{1,0:T(8,128)(2,1)S(1)} %get-tuple-element.39), channel_id=1, source_target_pairs={{0,0},{1,1},{2,2},{3,3},{4,4},{5,5},{6,6},{7,7},{8,8},{9,9},{10,10... | collective-permute-start | bytes 393224 | tf_op jit(solution)/shard_map/ppermute | solution.py:22
  25.6 8.6 %collective-permute-start.12 = (bf16[256,256]{1,0:T(8,128)(2,1)S(1)}, bf16[256,256]{1,0:T(8,128)(2,1)S(1)}, u32[]{:S(2)}, u32[]{:S(2)}) collective-permute-start(bf16[256,256]{1,0:T(8,128)(2,1)S(1)} %get-tuple-element.40), channel_id=1, source_target_pairs={{0,26},{1,27},{2,24},{3,25},{4,30},{5,31},{6,28},{7,29},{8,18},{9,... | collective-permute-start | bytes 393224 | tf_op jit(solution)/shard_map/ppermute | solution.py:22
  29.3 6.3 %collective-permute-start.13 = (bf16[256,256]{1,0:T(8,128)(2,1)S(1)}, bf16[256,256]{1,0:T(8,128)(2,1)S(1)}, u32[]{:S(2)}, u32[]{:S(2)}) collective-permute-start(bf16[256,256]{1,0:T(8,128)(2,1)S(1)} %get-tuple-element.41), channel_id=1, source_target_pairs={{0,8},{1,9},{2,10},{3,11},{4,12},{5,13},{6,14},{7,15},{8,0},{9,1},... | collective-permute-start | bytes 393224 | tf_op jit(solution)/shard_map/ppermute | solution.py:22
  32.1 6.5 %collective-permute-start.14 = (bf16[256,256]{1,0:T(8,128)(2,1)S(1)}, bf16[256,256]{1,0:T(8,128)(2,1)S(1)}, u32[]{:S(2)}, u32[]{:S(2)}) collective-permute-start(bf16[256,256]{1,0:T(8,128)(2,1)S(1)} %collective-permute-done.7.refs_0_), channel_id=1, source_target_pairs={{0,4},{1,5},{2,6},{3,7},{4,0},{5,1},{6,2},{7,3},{8,12},{9,13},{10,... | collective-permute-start | bytes 393224 | tf_op jit(solution)/shard_map/ppermute | solution.py:22
  34.1 4.6 %collective-permute-start.15 = (bf16[256,256]{1,0:T(8,128)(2,1)S(1)}, bf16[256,256]{1,0:T(8,128)(2,1)S(1)}, u32[]{:S(2)}, u32[]{:S(2)}) collective-permute-start(bf16[256,256]{1,0:T(8,128)(2,1)S(1)} %collective-permute-done.11.refs_1_), channel_id=1, source_target_pairs={{0,4},{1,5},{2,6},{3,7},{4,0},{5,1},{6,2},{7,3},{8,12},{9,13},{10,... | collective-permute-start | bytes 393224 | tf_op jit(solution)/shard_map/ppermute | solution.py:22
  34.2 4.5 %collective-permute-start.16 = (bf16[256,256]{1,0:T(8,128)(2,1)S(1)}, bf16[256,256]{1,0:T(8,128)(2,1)S(1)}, u32[]{:S(2)}, u32[]{:S(2)}) collective-permute-start(bf16[256,256]{1,0:T(8,128)(2,1)S(1)} %collective-permute-done.12.refs_2_), channel_id=1, source_target_pairs={{0,4},{1,5},{2,6},{3,7},{4,0},{5,1},{6,2},{7,3},{8,12},{9,13},{10,... | collective-permute-start | bytes 393224 | tf_op jit(solution)/shard_map/ppermute | solution.py:22
  35.6 4.1 %collective-permute-start.17 = (bf16[256,256]{1,0:T(8,128)(2,1)S(1)}, bf16[256,256]{1,0:T(8,128)(2,1)S(1)}, u32[]{:S(2)}, u32[]{:S(2)}) collective-permute-start(bf16[256,256]{1,0:T(8,128)(2,1)S(1)} %collective-permute-done.13.refs_3_), channel_id=1, source_target_pairs={{0,4},{1,5},{2,6},{3,7},{4,0},{5,1},{6,2},{7,3},{8,12},{9,13},{10,... | collective-permute-start | bytes 393224 | tf_op jit(solution)/shard_map/ppermute | solution.py:22

commit v8 on v7

--- a/solution.py
+++ b/solution.py
@@ -240,7 +240,7 @@
 
 
 def finish_kernel(cap, last, gathered_ref, far_ref, hot_ref, out_ref, buffer_ref, sems):
-    block = far_ref[pl.ds(pl.multiple_of(position()[0] * cap, cap), cap), :]
+    block = far_ref[...]
     parts = sems.shape[0]
     step = out_ref.shape[0] // parts
     copies = []
@@ -380,7 +380,8 @@
         name="store_cloud",
     )(*news, new_cloud)
     back[0], new_cloud = lax.optimization_barrier((back[0], new_cloud))
-    far_back = [swapped(block) for block in back]
+    last_rows = lax.dynamic_slice_in_dim(back[-1], (1 - elem % 2) * cap, cap, axis=0)
+    far_back = [swapped(block) for block in back[:-1] + [last_rows]]
     most = pl.pallas_call(
         functools.partial(gather_kernel, cap, sequence),
         out_shape=like(state),

time: 40.8 us -> 40.7 us (level)
  no operation moved by 1% of the time
where the time goes in v8:
time: 40.7 us; the launch traced here: 40.5 us
  starting transfers between devices  27.7 us (68%)
  Pallas kernels  6.56 us (16%)
  waiting for transfers between devices  5.08 us (12%)
  between operations  0.81 us (2%)
    ppermute x18, starting transfers between devices, moved(): return lax.ppermute(block, ('elem', 'band'), route)  27.7 us
    ppermute x18, waiting for transfers between devices, moved(): return lax.ppermute(block, ('elem', 'band'), route)  5.08 us
    pallas_call x1, Pallas kernels, per_device(): pl.pallas_call(functools.partial(lower_kernel, cap), out_shape=[tile, lik...  1.54 us
    pallas_call x1, Pallas kernels, per_device(): pl.pallas_call(functools.partial(both_kernel, cap, low), out_shape=[tile,...  1.06 us
    pallas_call x1, Pallas kernels, per_device(): pl.pallas_call(functools.partial(finish_kernel, cap, sequence[-1]), out_s...  0.93 us
    pallas_call x1, Pallas kernels, per_device(): pl.pallas_call(functools.partial(store_kernel, cap, places), out_shape=li...  0.9 us
    pallas_call x2, Pallas kernels, per_device(): pl.pallas_call(functools.partial(place_kernel, cap, units, chosen), out_s...  0.87 us
  transfers between devices with their start and end apart: 18, of which 6 were waited for; matrix products, arithmetic and copies ran while one was open for 0% of the time, Pallas kernels for 13%

profile of v8, /device:TPU:11, one launch (start us, length us, event | category | flops | bytes accessed | tf_op | source)
XLA Modules:
  0.0 40.5 jit_solution(5530457073882424444)
XLA Ops:
  0.6 0.0 copy-start.9
  0.6 0.7 %collective-permute-start.1 = (s32[4,128]{1,0:T(4,128)}, s32[4,128]{1,0:T(4,128)S(1)}, u32[]{:S(2)}, u32[]{:S(2)}) collective-permute-start(s32[4,128]{1,0:T(4,128)} %bitcast.2), channel_id=1, source_target_pairs={{0,4},{1,5},{2,6},{3,7},{4,0},{5,1},{6,2},{7,3},{8,12},{9,13},{10,... | collective-permute-start | bytes 6152 | tf_op jit(solution)/shard_map/ppermute | solution.py:22
  1.4 0.0 copy-done.9
  1.4 0.6 %collective-permute-start.2 = (s32[4,128]{1,0:T(4,128)S(1)}, s32[4,128]{1,0:T(4,128)S(1)}, u32[]{:S(2)}, u32[]{:S(2)}) collective-permute-start(s32[4,128]{1,0:T(4,128)S(1)} %bitcast.4), channel_id=1, source_target_pairs={{0,4},{1,5},{2,6},{3,7},{4,0},{5,1},{6,2},{7,3},{8,12},{9,13},{10,... | collective-permute-start | bytes 6152 | tf_op jit(solution)/shard_map/ppermute | solution.py:22
  2.0 0.0 collective-permute-start
  2.0 0.0 copy-start.8
  2.0 0.0 copy-start.4
  2.0 0.4 %collective-permute-done.1.far_dest_ref = s32[4,128]{1,0:T(4,128)S(1)} collective-permute-done((s32[4,128]{1,0:T(4,128)}, s32[4,128]{1,0:T(4,128)S(1)}, u32[]{:S(2)}, u32[]{:S(2)}) %collective-permute-start.1) | collective-permute-done | bytes 2080 | tf_op jit(solution)/shard_map/ppermute | solution.py:22
  2.4 0.3 copy-done.8
  2.7 0.2 column_targets.1.targets_ref
  2.9 0.0 collective-permute-done.2.far_day_ref
  2.9 0.9 %collective-permute-done.far_state_ref = bf16[512,256]{1,0:T(8,128)(2,1)S(1)} collective-permute-done((bf16[512,256]{1,0:T(8,128)(2,1)}, bf16[512,256]{1,0:T(8,128)(2,1)S(1)}, u32[]{:S(2)}, u32[]{:S(2)}) %collective-permute-start) | collective-permute-done | bytes 262176 | tf_op jit(solution)/shard_map/ppermute | solution.py:22
  3.7 0.0 copy-done.4
  3.7 0.3 place_columns.2
  4.0 1.3 %collective-permute-start.3 = (bf16[128,256]{1,0:T(8,128)(2,1)S(1)}, bf16[128,256]{1,0:T(8,128)(2,1)S(1)}, u32[]{:S(2)}, u32[]{:S(2)}) collective-permute-start(bf16[128,256]{1,0:T(8,128)(2,1)S(1)} %get-tuple-element.23.refs_0_), channel_id=1, source_target_pairs={{0,16},{1,17},{2,18},{3,19},{4,20},{5,21},{6,22},{7,23},{8,24},{9,... | collective-permute-start | bytes 196616 | tf_op jit(solution)/shard_map/ppermute | solution.py:22
  5.3 0.0 copy-start
  5.4 0.2 collective-permute-start.5
  5.6 0.0 copy-start.2
  5.6 0.0 copy-start.3
  5.6 0.0 copy-start.6
  5.6 0.0 copy-start.7
  5.6 0.6 %place_columns.3 = (bf16[272,256]{1,0:T(8,128)(2,1)S(1)}, bf16[128,256]{1,0:T(8,128)(2,1)S(1)}, bf16[144,256]{1,0:T(8,128)(2,1)S(1)}, bf16[272,256]{1,0:T(8,128)(2,1)S(1)}) custom-call(bf16[512,256]{1,0:T(8,128)(2,1)S(1)} %collective-permute-done.far_state_ref, bf16[512,256]{1,0:T(8,128)(2,1)S(1)} %copy-done.4, s32[8,512]{1,0:T(8,128)S(1)} %column_targets.1.targets_ref, ...), custom_call_target="tpu_custom_call" | custom-call | flops 3449999872 | tf_op jit(solution)/shard_map/place_columns/pallas_call | solution.py:294
  6.2 0.0 copy-start.1
  6.2 1.3 %collective-permute-start.8 = (bf16[272,256]{1,0:T(8,128)(2,1)S(1)}, bf16[272,256]{1,0:T(8,128)(2,1)S(1)}, u32[]{:S(2)}, u32[]{:S(2)}) collective-permute-start(bf16[272,256]{1,0:T(8,128)(2,1)S(1)} %get-tuple-element.32), channel_id=1, source_target_pairs={{0,16},{1,17},{2,18},{3,19},{4,20},{5,21},{6,22},{7,23},{8,24},{9,... | collective-permute-start | bytes 417800 | tf_op jit(solution)/shard_map/ppermute | solution.py:22
  7.5 0.2 collective-permute-done.3
  7.7 2.4 %collective-permute-start.4 = (bf16[128,256]{1,0:T(8,128)(2,1)S(1)}, bf16[128,256]{1,0:T(8,128)(2,1)S(1)}, u32[]{:S(2)}, u32[]{:S(2)}) collective-permute-start(bf16[128,256]{1,0:T(8,128)(2,1)S(1)} %get-tuple-element.49), channel_id=1, source_target_pairs={{0,2},{1,3},{2,0},{3,1},{4,6},{5,7},{6,4},{7,5},{8,10},{9,11},{10,... | collective-permute-start | bytes 196616 | tf_op jit(solution)/shard_map/ppermute | solution.py:22
  10.1 0.0 collective-permute-done.5
  10.1 1.4 %collective-permute-start.6 = (bf16[144,256]{1,0:T(8,128)(2,1)S(1)}, bf16[144,256]{1,0:T(8,128)(2,1)S(1)}, u32[]{:S(2)}, u32[]{:S(2)}) collective-permute-start(bf16[144,256]{1,0:T(8,128)(2,1)S(1)} %get-tuple-element.47), channel_id=1, source_target_pairs={{0,2},{1,3},{2,0},{3,1},{4,6},{5,7},{6,4},{7,5},{8,10},{9,11},{10,... | collective-permute-start | bytes 221192 | tf_op jit(solution)/shard_map/ppermute | solution.py:22
  11.5 0.0 copy-done
  11.5 0.0 copy-done.2
  11.5 0.0 copy-done.3
  11.5 0.0 copy-done.6
  11.5 0.0 copy-done.7
  11.5 0.0 copy-done.1
  11.5 0.0 copy-done.5
  11.5 1.5 %lower_physics.1 = (bf16[256,256]{1,0:T(8,128)(2,1)S(1)}, bf16[1024,512]{1,0:T(8,128)(2,1)}, bf16[512,1024]{1,0:T(8,128)(2,1)S(1)}, f32[2,256,256]{2,1,0:T(8,128...) custom-call(s32[8,512]{1,0:T(8,128)S(1)} %column_targets.1.targets_ref, ...), custom_call_target="tpu_custom_call" | custom-call | flops 3449999872 | tf_op jit(solution)/shard_map/lower_physics/pallas_call | solution.py:326
  13.1 0.0 collective-permute-done.8
  13.1 1.3 %collective-permute-start.10 = (bf16[272,256]{1,0:T(8,128)(2,1)S(1)}, bf16[272,256]{1,0:T(8,128)(2,1)S(1)}, u32[]{:S(2)}, u32[]{:S(2)}) collective-permute-start(bf16[272,256]{1,0:T(8,128)(2,1)S(1)} %get-tuple-element.44), channel_id=1, source_target_pairs={{0,10},{1,11},{2,8},{3,9},{4,14},{5,15},{6,12},{7,13},{8,2},{9,3},... | collective-permute-start | bytes 417800 | tf_op jit(solution)/shard_map/ppermute | solution.py:22
  14.4 1.2 %collective-permute-start.9 = (bf16[272,256]{1,0:T(8,128)(2,1)S(1)}, bf16[272,256]{1,0:T(8,128)(2,1)S(1)}, u32[]{:S(2)}, u32[]{:S(2)}) collective-permute-start(bf16[272,256]{1,0:T(8,128)(2,1)S(1)} %get-tuple-element.45), channel_id=1, source_target_pairs={{0,8},{1,9},{2,10},{3,11},{4,12},{5,13},{6,14},{7,15},{8,0},{9,1},... | collective-permute-start | bytes 417800 | tf_op jit(solution)/shard_map/ppermute | solution.py:22
  15.7 0.0 collective-permute-done.4.first_part
  15.7 2.9 %collective-permute-done.6.second_part = bf16[144,256]{1,0:T(8,128)(2,1)S(1)} collective-permute-done((bf16[144,256]{1,0:T(8,128)(2,1)S(1)}, bf16[144,256]{1,0:T(8,128)(2,1)S(1)}, u32[]{:S(2)}, u32[]{:S(2)}) %collective-permute-start.6) | collective-permute-done | bytes 73760 | tf_op jit(solution)/shard_map/ppermute | solution.py:22
  18.6 0.6 %upper_physics.1 = (bf16[256,256]{1,0:T(8,128)(2,1)S(1)}, bf16[256,256]{1,0:T(8,128)(2,1)S(1)}, bf16[256,512]{1,0:T(8,128)(2,1)S(1)}) custom-call(bf16[128,256]{1,0:T(8,128)(2,1)S(1)} %collective-permute-done.4.first_part, bf16[144,256]{1,0:T(8,128)(2,1)S(1)} %collective-permute-done.6.second_part, bf16[256,256]{1,0:T(8,128)(2,1)S(1)} %get-tuple-element.27.lower_answer_ref, ...), custom_call_target="tpu_custom_call" | custom-call | flops 3449999872 | tf_op jit(solution)/shard_map/upper_physics/pallas_call | solution.py:337
  19.2 4.4 %collective-permute-start.7 = (bf16[256,256]{1,0:T(8,128)(2,1)S(1)}, bf16[256,256]{1,0:T(8,128)(2,1)S(1)}, u32[]{:S(2)}, u32[]{:S(2)}) collective-permute-start(bf16[256,256]{1,0:T(8,128)(2,1)S(1)} %get-tuple-element.29), channel_id=1, source_target_pairs={{0,18},{1,19},{2,16},{3,17},{4,22},{5,23},{6,20},{7,21},{8,26},{9,... | collective-permute-start | bytes 393224 | tf_op jit(solution)/shard_map/ppermute | solution.py:22
  23.6 0.7 %collective-permute-start.11 = (bf16[256,256]{1,0:T(8,128)(2,1)S(1)}, bf16[256,256]{1,0:T(8,128)(2,1)S(1)}, u32[]{:S(2)}, u32[]{:S(2)}) collective-permute-start(bf16[256,256]{1,0:T(8,128)(2,1)S(1)} %get-tuple-element.39), channel_id=1, source_target_pairs={{0,0},{1,1},{2,2},{3,3},{4,4},{5,5},{6,6},{7,7},{8,8},{9,9},{10,10... | collective-permute-start | bytes 393224 | tf_op jit(solution)/shard_map/ppermute | solution.py:22
  24.2 0.3 collective-permute-done.10.lent_ref
  24.5 0.0 collective-permute-done.9.lower_ref
  24.5 1.1 %both_physics.1 = (bf16[256,256]{1,0:T(8,128)(2,1)S(1)}, bf16[256,256]{1,0:T(8,128)(2,1)S(1)}, bf16[256,512]{1,0:T(8,128)(2,1)S(1)}, bf16[256,512]{1,0:T(8,128)(2,1)S(1)}) custom-call(bf16[272,256]{1,0:T(8,128)(2,1)S(1)} %collective-permute-done.9.lower_ref, bf16[272,256]{1,0:T(8,128)(2,1)S(1)} %collective-permute-done.10.lent_ref, ...), custom_call_target="tpu_custom_call" | custom-call | flops 3449999872 | tf_op jit(solution)/shard_map/both_physics/pallas_call | solution.py:349
  25.6 3.7 %collective-permute-start.12 = (bf16[256,256]{1,0:T(8,128)(2,1)S(1)}, bf16[256,256]{1,0:T(8,128)(2,1)S(1)}, u32[]{:S(2)}, u32[]{:S(2)}) collective-permute-start(bf16[256,256]{1,0:T(8,128)(2,1)S(1)} %get-tuple-element.40), channel_id=1, source_target_pairs={{0,26},{1,27},{2,24},{3,25},{4,30},{5,31},{6,28},{7,29},{8,18},{9,... | collective-permute-start | bytes 393224 | tf_op jit(solution)/shard_map/ppermute | solution.py:22
  29.3 1.9 %collective-permute-start.13 = (bf16[256,256]{1,0:T(8,128)(2,1)S(1)}, bf16[256,256]{1,0:T(8,128)(2,1)S(1)}, u32[]{:S(2)}, u32[]{:S(2)}) collective-permute-start(bf16[256,256]{1,0:T(8,128)(2,1)S(1)} %get-tuple-element.41), channel_id=1, source_target_pairs={{0,8},{1,9},{2,10},{3,11},{4,12},{5,13},{6,14},{7,15},{8,0},{9,1},... | collective-permute-start | bytes 393224 | tf_op jit(solution)/shard_map/ppermute | solution.py:22
  31.2 0.9 %store_cloud.1 = bf16[1024,512]{1,0:T(8,128)(2,1)} custom-call(bf16[256,512]{1,0:T(8,128)(2,1)S(1)} %get-tuple-element.30.refs_0_, bf16[256,512]{1,0:T(8,128)(2,1)S(1)} %get-tuple-element.35.refs_1_, bf16[256,512]{1,0:T(8,128)(2,1)S(1)} %get-tuple-element.36.refs_2_, bf16[1024,512]{1,0:T(8,128)(2,1)} %get-tuple-element.37.refs_3_), custom_call_target="tpu_custom_call", output_to_operand_aliasing={{}: (3, {})} | custom-call | flops 11500000 | tf_op jit(solution)/shard_map/store_cloud/pallas_call | solution.py:371
  32.1 0.0 collective-permute-done.7.refs_0_
  32.1 2.0 %collective-permute-start.14 = (bf16[256,256]{1,0:T(8,128)(2,1)S(1)}, bf16[256,256]{1,0:T(8,128)(2,1)S(1)}, u32[]{:S(2)}, u32[]{:S(2)}) collective-permute-start(bf16[256,256]{1,0:T(8,128)(2,1)S(1)} %collective-permute-done.7.refs_0_), channel_id=1, source_target_pairs={{0,4},{1,5},{2,6},{3,7},{4,0},{5,1},{6,2},{7,3},{8,12},{9,13},{10,... | collective-permute-start | bytes 393224 | tf_op jit(solution)/shard_map/ppermute | solution.py:22
  34.1 0.0 collective-permute-done.11.refs_1_
  34.1 0.1 collective-permute-start.15
  34.2 0.0 collective-permute-done.12.refs_2_
  34.2 1.4 %collective-permute-start.16 = (bf16[256,256]{1,0:T(8,128)(2,1)S(1)}, bf16[256,256]{1,0:T(8,128)(2,1)S(1)}, u32[]{:S(2)}, u32[]{:S(2)}) collective-permute-start(bf16[256,256]{1,0:T(8,128)(2,1)S(1)} %collective-permute-done.12.refs_2_), channel_id=1, source_target_pairs={{0,4},{1,5},{2,6},{3,7},{4,0},{5,1},{6,2},{7,3},{8,12},{9,13},{10,... | collective-permute-start | bytes 393224 | tf_op jit(solution)/shard_map/ppermute | solution.py:22
  35.6 0.0 collective-permute-done.13.refs_3_
  35.6 3.1 %collective-permute-start.17 = (bf16[128,256]{1,0:T(8,128)(2,1)S(1)}, bf16[128,256]{1,0:T(8,128)(2,1)S(1)}, u32[]{:S(2)}, u32[]{:S(2)}) collective-permute-start(bf16[128,256]{1,0:T(8,128)(2,1)S(1)} %constant_dynamic-slice_fusion), channel_id=1, source_target_pairs={{0,4},{1,5},{2,6},{3,7},{4,0},{5,1},{6,2},{7,3},{8,12},{9,13},{10,... | collective-permute-start | bytes 196616 | tf_op jit(solution)/shard_map/ppermute | solution.py:22
  38.7 0.0 collective-permute-done.14.refs_4_
  38.7 0.0 collective-permute-done.15.refs_5_
  38.7 0.0 collective-permute-done.16.refs_6_
  38.7 0.5 %gather_most.1.gathered_ref = bf16[512,256]{1,0:T(8,128)(2,1)S(1)} custom-call(bf16[256,256]{1,0:T(8,128)(2,1)S(1)} %collective-permute-done.7.refs_0_, bf16[256,256]{1,0:T(8,128)(2,1)S(1)} %collective-permute-done.11.refs_1_, bf16[256,256]{1,0:T(8,128)(2,1)S(1)} %collective-permute-done.12.refs_2_, bf16[256,256]{1,0:T(8,128)(2,1)S(1)} %collective-permute-done.13.refs_3_, ...), custom_call_target="tpu_custom_call" | custom-call | flops 11500000 | tf_op jit(solution)/shard_map/gather_most/pallas_call | solution.py:385
  39.2 0.4 %collective-permute-done.17.far_ref = bf16[128,256]{1,0:T(8,128)(2,1)S(1)} collective-permute-done((bf16[128,256]{1,0:T(8,128)(2,1)S(1)}, bf16[128,256]{1,0:T(8,128)(2,1)S(1)}, u32[]{:S(2)}, u32[]{:S(2)}) %collective-permute-start.17) | collective-permute-done | bytes 65568 | tf_op jit(solution)/shard_map/ppermute | solution.py:22
  39.6 0.9 %gather_last.1 = bf16[512,256]{1,0:T(8,128)(2,1)} custom-call(bf16[512,256]{1,0:T(8,128)(2,1)S(1)} %gather_most.1.gathered_ref, bf16[128,256]{1,0:T(8,128)(2,1)S(1)} %collective-permute-done.17.far_ref, bf16[512,1024]{1,0:T(8,128)(2,1)S(1)} %get-tuple-element.42.refs_7_.hot_ref), custom_call_target="tpu_custom_call" | custom-call | flops 11500000 | tf_op jit(solution)/shard_map/gather_last/pallas_call | solution.py:394
  (5 shorter events, 0.1 us)
Async XLA Ops:
  0.6 0.8 %copy-start.9 = (s32[512,1]{0,1:T(1,128)S(1)}, s32[512,1]{0,1:T(1,128)}, u32[]{:S(2)}) copy-start(s32[512,1]{0,1:T(1,128)} %param.12) | copy-start | bytes 6148
  0.6 1.8 %collective-permute-start.1 = (s32[4,128]{1,0:T(4,128)}, s32[4,128]{1,0:T(4,128)S(1)}, u32[]{:S(2)}, u32[]{:S(2)}) collective-permute-start(s32[4,128]{1,0:T(4,128)} %bitcast.2), channel_id=1, source_target_pairs={{0,4},{1,5},{2,6},{3,7},{4,0},{5,1},{6,2},{7,3},{8,12},{9,13},{10,... | collective-permute-start | bytes 6152 | tf_op jit(solution)/shard_map/ppermute | solution.py:22
  1.4 1.5 %collective-permute-start.2 = (s32[4,128]{1,0:T(4,128)S(1)}, s32[4,128]{1,0:T(4,128)S(1)}, u32[]{:S(2)}, u32[]{:S(2)}) collective-permute-start(s32[4,128]{1,0:T(4,128)S(1)} %bitcast.4), channel_id=1, source_target_pairs={{0,4},{1,5},{2,6},{3,7},{4,0},{5,1},{6,2},{7,3},{8,12},{9,13},{10,... | collective-permute-start | bytes 6152 | tf_op jit(solution)/shard_map/ppermute | solution.py:22
  2.0 1.7 %collective-permute-start = (bf16[512,256]{1,0:T(8,128)(2,1)}, bf16[512,256]{1,0:T(8,128)(2,1)S(1)}, u32[]{:S(2)}, u32[]{:S(2)}) collective-permute-start(bf16[512,256]{1,0:T(8,128)(2,1)} %state_ref.3), channel_id=1, source_target_pairs={{0,4},{1,5},{2,6},{3,7},{4,0},{5,1},{6,2},{7,3},{8,12},{9,13},{10,... | collective-permute-start | bytes 786440 | tf_op jit(solution)/shard_map/ppermute | solution.py:22
  2.0 0.7 %copy-start.8 = (s32[512,1]{0,1:T(1,128)S(1)}, s32[512,1]{0,1:T(1,128)}, u32[]{:S(2)}) copy-start(s32[512,1]{0,1:T(1,128)} %param.11) | copy-start | bytes 6148
  2.0 1.7 %copy-start.4 = (bf16[512,256]{1,0:T(8,128)(2,1)S(1)}, bf16[512,256]{1,0:T(8,128)(2,1)}, u32[]{:S(2)}) copy-start(bf16[512,256]{1,0:T(8,128)(2,1)} %state_ref.3) | copy-start | bytes 786436
  4.0 3.6 %collective-permute-start.3 = (bf16[128,256]{1,0:T(8,128)(2,1)S(1)}, bf16[128,256]{1,0:T(8,128)(2,1)S(1)}, u32[]{:S(2)}, u32[]{:S(2)}) collective-permute-start(bf16[128,256]{1,0:T(8,128)(2,1)S(1)} %get-tuple-element.23.refs_0_), channel_id=1, source_target_pairs={{0,16},{1,17},{2,18},{3,19},{4,20},{5,21},{6,22},{7,23},{8,24},{9,... | collective-permute-start | bytes 196616 | tf_op jit(solution)/shard_map/ppermute | solution.py:22
  5.3 6.1 %copy-start = (bf16[1024,512]{1,0:T(8,128)(2,1)S(1)}, bf16[1024,512]{1,0:T(8,128)(2,1)}, u32[]{:S(2)}) copy-start(bf16[1024,512]{1,0:T(8,128)(2,1)} %cloud_ref.5) | copy-start | bytes 3145732
  5.4 4.7 %collective-permute-start.5 = (bf16[144,256]{1,0:T(8,128)(2,1)S(1)}, bf16[144,256]{1,0:T(8,128)(2,1)S(1)}, u32[]{:S(2)}, u32[]{:S(2)}) collective-permute-start(bf16[144,256]{1,0:T(8,128)(2,1)S(1)} %get-tuple-element.25), channel_id=1, source_target_pairs={{0,16},{1,17},{2,18},{3,19},{4,20},{5,21},{6,22},{7,23},{8,24},{9,... | collective-permute-start | bytes 221192 | tf_op jit(solution)/shard_map/ppermute | solution.py:22
  5.6 5.9 %copy-start.2 = (bf16[256,768]{1,0:T(8,128)(2,1)S(1)}, bf16[256,768]{1,0:T(8,128)(2,1)}, u32[]{:S(2)}) copy-start(bf16[256,768]{1,0:T(8,128)(2,1)} %refs_2_.5) | copy-start | bytes 1179652
  5.6 5.9 %copy-start.3 = (bf16[768,256]{1,0:T(8,128)(2,1)S(1)}, bf16[768,256]{1,0:T(8,128)(2,1)}, u32[]{:S(2)}) copy-start(bf16[768,256]{1,0:T(8,128)(2,1)} %refs_3_.5) | copy-start | bytes 1179652
  5.6 5.9 %copy-start.6 = (bf16[256,256]{1,0:T(8,128)(2,1)S(1)}, bf16[256,256]{1,0:T(8,128)(2,1)}, u32[]{:S(2)}) copy-start(bf16[256,256]{1,0:T(8,128)(2,1)} %refs_4_.5) | copy-start | bytes 393220
  5.6 5.9 %copy-start.7 = (bf16[256,128]{1,0:T(8,128)(2,1)S(1)}, bf16[256,128]{1,0:T(8,128)(2,1)}, u32[]{:S(2)}) copy-start(bf16[256,128]{1,0:T(8,128)(2,1)} %refs_5_.5) | copy-start | bytes 196612
  6.2 5.3 %copy-start.1 = (bf16[768,256]{1,0:T(8,128)(2,1)S(1)}, bf16[768,256]{1,0:T(8,128)(2,1)}, u32[]{:S(2)}) copy-start(bf16[768,256]{1,0:T(8,128)(2,1)} %refs_0_.5) | copy-start | bytes 1179652
  6.2 6.9 %collective-permute-start.8 = (bf16[272,256]{1,0:T(8,128)(2,1)S(1)}, bf16[272,256]{1,0:T(8,128)(2,1)S(1)}, u32[]{:S(2)}, u32[]{:S(2)}) collective-permute-start(bf16[272,256]{1,0:T(8,128)(2,1)S(1)} %get-tuple-element.32), channel_id=1, source_target_pairs={{0,16},{1,17},{2,18},{3,19},{4,20},{5,21},{6,22},{7,23},{8,24},{9,... | collective-permute-start | bytes 417800 | tf_op jit(solution)/shard_map/ppermute | solution.py:22
  7.7 8.0 %collective-permute-start.4 = (bf16[128,256]{1,0:T(8,128)(2,1)S(1)}, bf16[128,256]{1,0:T(8,128)(2,1)S(1)}, u32[]{:S(2)}, u32[]{:S(2)}) collective-permute-start(bf16[128,256]{1,0:T(8,128)(2,1)S(1)} %get-tuple-element.49), channel_id=1, source_target_pairs={{0,2},{1,3},{2,0},{3,1},{4,6},{5,7},{6,4},{7,5},{8,10},{9,11},{10,... | collective-permute-start | bytes 196616 | tf_op jit(solution)/shard_map/ppermute | solution.py:22
  10.1 1.5 %copy-start.5 = (bf16[256,256]{1,0:T(8,128)(2,1)S(1)}, bf16[256,256]{1,0:T(8,128)(2,1)}, u32[]{:S(2)}) copy-start(bf16[256,256]{1,0:T(8,128)(2,1)} %refs_1_.5) | copy-start | bytes 393220
  10.1 8.5 %collective-permute-start.6 = (bf16[144,256]{1,0:T(8,128)(2,1)S(1)}, bf16[144,256]{1,0:T(8,128)(2,1)S(1)}, u32[]{:S(2)}, u32[]{:S(2)}) collective-permute-start(bf16[144,256]{1,0:T(8,128)(2,1)S(1)} %get-tuple-element.47), channel_id=1, source_target_pairs={{0,2},{1,3},{2,0},{3,1},{4,6},{5,7},{6,4},{7,5},{8,10},{9,11},{10,... | collective-permute-start | bytes 221192 | tf_op jit(solution)/shard_map/ppermute | solution.py:22
  13.1 11.4 %collective-permute-start.10 = (bf16[272,256]{1,0:T(8,128)(2,1)S(1)}, bf16[272,256]{1,0:T(8,128)(2,1)S(1)}, u32[]{:S(2)}, u32[]{:S(2)}) collective-permute-start(bf16[272,256]{1,0:T(8,128)(2,1)S(1)} %get-tuple-element.44), channel_id=1, source_target_pairs={{0,10},{1,11},{2,8},{3,9},{4,14},{5,15},{6,12},{7,13},{8,2},{9,3},... | collective-permute-start | bytes 417800 | tf_op jit(solution)/shard_map/ppermute | solution.py:22
  14.4 10.1 %collective-permute-start.9 = (bf16[272,256]{1,0:T(8,128)(2,1)S(1)}, bf16[272,256]{1,0:T(8,128)(2,1)S(1)}, u32[]{:S(2)}, u32[]{:S(2)}) collective-permute-start(bf16[272,256]{1,0:T(8,128)(2,1)S(1)} %get-tuple-element.45), channel_id=1, source_target_pairs={{0,8},{1,9},{2,10},{3,11},{4,12},{5,13},{6,14},{7,15},{8,0},{9,1},... | collective-permute-start | bytes 417800 | tf_op jit(solution)/shard_map/ppermute | solution.py:22
  19.2 13.0 %collective-permute-start.7 = (bf16[256,256]{1,0:T(8,128)(2,1)S(1)}, bf16[256,256]{1,0:T(8,128)(2,1)S(1)}, u32[]{:S(2)}, u32[]{:S(2)}) collective-permute-start(bf16[256,256]{1,0:T(8,128)(2,1)S(1)} %get-tuple-element.29), channel_id=1, source_target_pairs={{0,18},{1,19},{2,16},{3,17},{4,22},{5,23},{6,20},{7,21},{8,26},{9,... | collective-permute-start | bytes 393224 | tf_op jit(solution)/shard_map/ppermute | solution.py:22
  23.6 10.6 %collective-permute-start.11 = (bf16[256,256]{1,0:T(8,128)(2,1)S(1)}, bf16[256,256]{1,0:T(8,128)(2,1)S(1)}, u32[]{:S(2)}, u32[]{:S(2)}) collective-permute-start(bf16[256,256]{1,0:T(8,128)(2,1)S(1)} %get-tuple-element.39), channel_id=1, source_target_pairs={{0,0},{1,1},{2,2},{3,3},{4,4},{5,5},{6,6},{7,7},{8,8},{9,9},{10,10... | collective-permute-start | bytes 393224 | tf_op jit(solution)/shard_map/ppermute | solution.py:22
  25.6 8.6 %collective-permute-start.12 = (bf16[256,256]{1,0:T(8,128)(2,1)S(1)}, bf16[256,256]{1,0:T(8,128)(2,1)S(1)}, u32[]{:S(2)}, u32[]{:S(2)}) collective-permute-start(bf16[256,256]{1,0:T(8,128)(2,1)S(1)} %get-tuple-element.40), channel_id=1, source_target_pairs={{0,26},{1,27},{2,24},{3,25},{4,30},{5,31},{6,28},{7,29},{8,18},{9,... | collective-permute-start | bytes 393224 | tf_op jit(solution)/shard_map/ppermute | solution.py:22
  29.3 6.3 %collective-permute-start.13 = (bf16[256,256]{1,0:T(8,128)(2,1)S(1)}, bf16[256,256]{1,0:T(8,128)(2,1)S(1)}, u32[]{:S(2)}, u32[]{:S(2)}) collective-permute-start(bf16[256,256]{1,0:T(8,128)(2,1)S(1)} %get-tuple-element.41), channel_id=1, source_target_pairs={{0,8},{1,9},{2,10},{3,11},{4,12},{5,13},{6,14},{7,15},{8,0},{9,1},... | collective-permute-start | bytes 393224 | tf_op jit(solution)/shard_map/ppermute | solution.py:22
  32.1 6.5 %collective-permute-start.14 = (bf16[256,256]{1,0:T(8,128)(2,1)S(1)}, bf16[256,256]{1,0:T(8,128)(2,1)S(1)}, u32[]{:S(2)}, u32[]{:S(2)}) collective-permute-start(bf16[256,256]{1,0:T(8,128)(2,1)S(1)} %collective-permute-done.7.refs_0_), channel_id=1, source_target_pairs={{0,4},{1,5},{2,6},{3,7},{4,0},{5,1},{6,2},{7,3},{8,12},{9,13},{10,... | collective-permute-start | bytes 393224 | tf_op jit(solution)/shard_map/ppermute | solution.py:22
  34.1 4.6 %collective-permute-start.15 = (bf16[256,256]{1,0:T(8,128)(2,1)S(1)}, bf16[256,256]{1,0:T(8,128)(2,1)S(1)}, u32[]{:S(2)}, u32[]{:S(2)}) collective-permute-start(bf16[256,256]{1,0:T(8,128)(2,1)S(1)} %collective-permute-done.11.refs_1_), channel_id=1, source_target_pairs={{0,4},{1,5},{2,6},{3,7},{4,0},{5,1},{6,2},{7,3},{8,12},{9,13},{10,... | collective-permute-start | bytes 393224 | tf_op jit(solution)/shard_map/ppermute | solution.py:22
  34.2 4.5 %collective-permute-start.16 = (bf16[256,256]{1,0:T(8,128)(2,1)S(1)}, bf16[256,256]{1,0:T(8,128)(2,1)S(1)}, u32[]{:S(2)}, u32[]{:S(2)}) collective-permute-start(bf16[256,256]{1,0:T(8,128)(2,1)S(1)} %collective-permute-done.12.refs_2_), channel_id=1, source_target_pairs={{0,4},{1,5},{2,6},{3,7},{4,0},{5,1},{6,2},{7,3},{8,12},{9,13},{10,... | collective-permute-start | bytes 393224 | tf_op jit(solution)/shard_map/ppermute | solution.py:22
  35.6 4.0 %collective-permute-start.17 = (bf16[128,256]{1,0:T(8,128)(2,1)S(1)}, bf16[128,256]{1,0:T(8,128)(2,1)S(1)}, u32[]{:S(2)}, u32[]{:S(2)}) collective-permute-start(bf16[128,256]{1,0:T(8,128)(2,1)S(1)} %constant_dynamic-slice_fusion), channel_id=1, source_target_pairs={{0,4},{1,5},{2,6},{3,7},{4,0},{5,1},{6,2},{7,3},{8,12},{9,13},{10,... | collective-permute-start | bytes 196616 | tf_op jit(solution)/shard_map/ppermute | solution.py:22
